TPU v7x, 32 devices: a whole 2x2x4 slice. The times are simulated.
32 devices in a mesh: tm: 32 (over z, y, x, core).
Axes of the slice: x: 2, y: 2, z: 4, core: 2. Of those that a mesh axis runs over, the one named last changes fastest.
Arguments:
- inv_diag: float32 [32, 384, 384], P('tm'), may hold values from -0.4 to 4.4, as said below
- low_coupling: float32 [32, 384, 384], P('tm'), may hold values from -0.09375 to 0.09375
- up_coupling: float32 [32, 384, 384], P('tm'), may hold values from -0.09375 to 0.09375
Outputs:
- diag_inverse: float32 [32, 384, 384], P('tm')
- cross_inverse: float32 [32, 384, 384], P('tm')
Inputs may be any that keep to these rules, and one draw needn't show every extreme that they name: `inv_diag`: each block is symmetric.
All inputs are finite; a program needn't handle non-finite values.
Results may differ from a plain program's by a relative error of at most 0.00012.
Values sent between devices are 32-bit elements; how exact they have to be, the bound alone decides.
No kernel may reach another device: no remote copies, remote signals or barrier semaphores. Data moves between devices by JAX's collectives and lax.ppermute only.
A program may use at most 64 MiB of HBM per device.

v0:
```python
import jax
import jax.numpy as jnp
from jax import lax
from jax.sharding import PartitionSpec as P

row_offset = 3


def passed_along(array, axis, by):
    peers = lax.axis_size(axis)
    return lax.ppermute(array, axis, [(i, (i + by) % peers) for i in range(peers)])


def product(left, right):
    return jnp.dot(left, right, precision=lax.Precision.HIGHEST, preferred_element_type=jnp.float32)


def body(inv_diag, low_coupling, up_coupling):
    inverse = inv_diag[0]
    lowers = low_coupling[0]
    uppers = up_coupling[0]
    width = inverse.shape[0]
    length = lax.axis_size("tm")
    levels = length.bit_length() - 1
    place = lax.axis_index("tm")
    position = (place + row_offset) % length
    zeros = jnp.zeros((width, width), jnp.float32)
    sigma = jnp.where(position == 0, inverse, zeros)
    high_own = zeros
    low_own = zeros
    lower_cross = zeros
    g_mat = product(inverse, lowers)
    h_mat = product(inverse, uppers)

    def eliminate(operands):
        current, sigma_low, sigma_high, sigma_ba = operands
        sigma_ab = sigma_ba.T
        part_low = -(product(g_mat, sigma_low) + product(h_mat, sigma_ba))
        part_high = -(product(g_mat, sigma_ab) + product(h_mat, sigma_high))
        sigma_tt = inverse - product(g_mat, part_low.T) - product(h_mat, part_high.T)
        return (sigma_tt, part_low, part_high)

    def keep(operands):
        return (operands[0], zeros, zeros)

    for step_num in range(levels):
        stride = length // 2 ** (step_num + 1)
        active = position % (2 * stride) == stride
        has_upper = position + stride < length
        from_low, owned_high = passed_along((sigma, high_own), "tm", stride)
        from_high, owned_low = passed_along((sigma, low_own), "tm", -stride)
        sigma_ba = owned_high.T + owned_low
        sigma_high = jnp.where(has_upper, from_high, zeros)
        sigma_ba = jnp.where(has_upper, sigma_ba, zeros)
        sigma, part_low, part_high = lax.cond(
            active, eliminate, keep, (sigma, from_low, sigma_high, sigma_ba)
        )
        high_own = part_high
        low_own = part_low
        lower_cross = jnp.where(active, part_low, lower_cross)
    return (sigma[None], lower_cross[None])


def solution(mesh):
    placed = (P("tm", None, None), P("tm", None, None), P("tm", None, None))
    return jax.shard_map(
        body,
        mesh=mesh,
        in_specs=placed,
        out_specs=(P("tm", None, None), P("tm", None, None)),
        check_vma=False,
    )
```

profile of v0, /device:TPU:4, one launch (start us, length us, event | category | flops | bytes accessed | tf_op | source)
XLA Modules:
  0.0 288.7 jit_solution(8937752699105270516)
XLA Ops:
  0.7 2.7 collective-permute-start.1
  7.8 35.4 %collective-permute-done.1 = f32[384,384]{1,0:T(8,128)S(1)} collective-permute-done((f32[384,384]{1,0:T(8,128)S(1)}, f32[384,384]{1,0:T(8,128)S(1)}, u32[]{:S(2)}, u32[]{:S(2)}) %collective-permute-start.1) | collective-permute-done | bytes 589856 | tf_op jit(solution)/shard_map/ppermute | solution.py:11
  43.1 11.6 %collective-permute-done = f32[384,384]{1,0:T(8,128)} collective-permute-done((f32[384,384]{1,0:T(8,128)}, f32[384,384]{1,0:T(8,128)}, u32[]{:S(2)}, u32[]{:S(2)}) %collective-permute-start) | collective-permute-done | bytes 589856 | tf_op jit(solution)/shard_map/ppermute | solution.py:11
  54.8 3.3 %conditional.5 = (f32[384,384]{0,1:T(8,128)S(1)}, f32[384,384]{1,0:T(8,128)}, f32[384,384]{0,1:T(8,128)}) conditional(s32[]{:T(128)} %convert_element_type.19, (f32[384,384]{1,0:T(8,128)}) %tuple.78, (f32[384,384]{1,0:T(8,128)S(1)}, f32[384,384]{1,0:T(8,128)}, s32[]{:T(128)}, f32[384,384]{0,1:T(8,128)S(1)}, f32[384,384]{1,0:T(8,128)S(1)}, ...), branch_computations={%region_0.1_spmd, %region_1.2_spmd} | conditional | flops 4078190592 | bytes 20643916 | solution.py:55
  59.1 3.5 %collective-permute-start.5 = (f32[384,384]{1,0:T(8,128)}, f32[384,384]{1,0:T(8,128)}, u32[]{:S(2)}, u32[]{:S(2)}) collective-permute-start(f32[384,384]{1,0:T(8,128)} %copy.17), channel_id=1, source_target_pairs={{0,24},{1,25},{2,26},{3,27},{4,28},{5,29},{6,30},{7,31},{8,0},{9,1... | collective-permute-start | bytes 1769480 | tf_op jit(solution)/shard_map/ppermute | solution.py:11
  62.6 3.9 %collective-permute-start.4 = (f32[384,384]{1,0:T(8,128)}, f32[384,384]{1,0:T(8,128)}, u32[]{:S(2)}, u32[]{:S(2)}) collective-permute-start(f32[384,384]{1,0:T(8,128)} %get-tuple-element.300), channel_id=1, source_target_pairs={{0,24},{1,25},{2,26},{3,27},{4,28},{5,29},{6,30},{7,31},{8,0},{9,1... | collective-permute-start | bytes 1769480 | tf_op jit(solution)/shard_map/ppermute | solution.py:11
  66.4 10.2 %collective-permute-done.5 = f32[384,384]{1,0:T(8,128)} collective-permute-done((f32[384,384]{1,0:T(8,128)}, f32[384,384]{1,0:T(8,128)}, u32[]{:S(2)}, u32[]{:S(2)}) %collective-permute-start.5) | collective-permute-done | bytes 589856 | tf_op jit(solution)/shard_map/ppermute | solution.py:11
  76.7 13.2 %collective-permute-done.2 = f32[384,384]{1,0:T(8,128)} collective-permute-done((f32[384,384]{1,0:T(8,128)}, f32[384,384]{1,0:T(8,128)}, u32[]{:S(2)}, u32[]{:S(2)}) %collective-permute-start.2) | collective-permute-done | bytes 589856 | tf_op jit(solution)/shard_map/ppermute | solution.py:11
  89.8 12.5 %collective-permute-done.3 = f32[384,384]{0,1:T(8,128)} collective-permute-done((f32[384,384]{0,1:T(8,128)}, f32[384,384]{0,1:T(8,128)}, u32[]{:S(2)}, u32[]{:S(2)}) %collective-permute-start.3) | collective-permute-done | bytes 589856 | tf_op jit(solution)/shard_map/ppermute | solution.py:11
  102.4 11.3 %collective-permute-done.4 = f32[384,384]{1,0:T(8,128)} collective-permute-done((f32[384,384]{1,0:T(8,128)}, f32[384,384]{1,0:T(8,128)}, u32[]{:S(2)}, u32[]{:S(2)}) %collective-permute-start.4) | collective-permute-done | bytes 589856 | tf_op jit(solution)/shard_map/ppermute | solution.py:11
  113.6 2.2 conditional.6
  117.4 2.4 collective-permute-start.6
  119.9 2.8 collective-permute-start.8
  122.7 27.9 %collective-permute-done.9 = f32[384,384]{1,0:T(8,128)} collective-permute-done((f32[384,384]{1,0:T(8,128)}, f32[384,384]{1,0:T(8,128)}, u32[]{:S(2)}, u32[]{:S(2)}) %collective-permute-start.9) | collective-permute-done | bytes 589856 | tf_op jit(solution)/shard_map/ppermute | solution.py:11
  150.6 8.9 %collective-permute-done.6 = f32[384,384]{1,0:T(8,128)} collective-permute-done((f32[384,384]{1,0:T(8,128)}, f32[384,384]{1,0:T(8,128)}, u32[]{:S(2)}, u32[]{:S(2)}) %collective-permute-start.6) | collective-permute-done | bytes 589856 | tf_op jit(solution)/shard_map/ppermute | solution.py:11
  159.4 12.6 %collective-permute-done.7 = f32[384,384]{0,1:T(8,128)} collective-permute-done((f32[384,384]{0,1:T(8,128)}, f32[384,384]{0,1:T(8,128)}, u32[]{:S(2)}, u32[]{:S(2)}) %collective-permute-start.7) | collective-permute-done | bytes 589856 | tf_op jit(solution)/shard_map/ppermute | solution.py:11
  172.1 1.9 conditional.7
  175.0 2.0 collective-permute-start.10
  177.0 1.6 collective-permute-start.11
  180.0 36.8 %collective-permute-done.13 = f32[384,384]{1,0:T(8,128)} collective-permute-done((f32[384,384]{1,0:T(8,128)}, f32[384,384]{1,0:T(8,128)}, u32[]{:S(2)}, u32[]{:S(2)}) %collective-permute-start.13) | collective-permute-done | bytes 589856 | tf_op jit(solution)/shard_map/ppermute | solution.py:11
  216.8 11.8 %collective-permute-done.12 = f32[384,384]{1,0:T(8,128)} collective-permute-done((f32[384,384]{1,0:T(8,128)}, f32[384,384]{1,0:T(8,128)}, u32[]{:S(2)}, u32[]{:S(2)}) %collective-permute-start.12) | collective-permute-done | bytes 589856 | tf_op jit(solution)/shard_map/ppermute | solution.py:11
  228.6 1.9 conditional.8
  231.6 17.1 %collective-permute-start.17 = (f32[384,384]{1,0:T(8,128)}, f32[384,384]{1,0:T(8,128)}, u32[]{:S(2)}, u32[]{:S(2)}) collective-permute-start(f32[384,384]{1,0:T(8,128)} %copy.26), channel_id=1, source_target_pairs={{0,31},{1,0},{2,1},{3,2},{4,3},{5,4},{6,5},{7,6},{8,7},{9,8},{10,9... | collective-permute-start | bytes 1769480 | tf_op jit(solution)/shard_map/ppermute | solution.py:11
  248.6 2.7 collective-permute-start.16
  251.3 7.5 %collective-permute-done.17 = f32[384,384]{1,0:T(8,128)} collective-permute-done((f32[384,384]{1,0:T(8,128)}, f32[384,384]{1,0:T(8,128)}, u32[]{:S(2)}, u32[]{:S(2)}) %collective-permute-start.17) | collective-permute-done | bytes 589856 | tf_op jit(solution)/shard_map/ppermute | solution.py:11
  258.8 6.0 %collective-permute-done.14 = f32[384,384]{1,0:T(8,128)} collective-permute-done((f32[384,384]{1,0:T(8,128)}, f32[384,384]{1,0:T(8,128)}, u32[]{:S(2)}, u32[]{:S(2)}) %collective-permute-start.14) | collective-permute-done | bytes 589856 | tf_op jit(solution)/shard_map/ppermute | solution.py:11
  264.8 7.0 %collective-permute-done.15 = f32[384,384]{0,1:T(8,128)} collective-permute-done((f32[384,384]{0,1:T(8,128)}, f32[384,384]{0,1:T(8,128)}, u32[]{:S(2)}, u32[]{:S(2)}) %collective-permute-start.15) | collective-permute-done | bytes 589856 | tf_op jit(solution)/shard_map/ppermute | solution.py:11
  271.8 14.6 %conditional.9 = (f32[384,384]{0,1:T(8,128)S(1)}, f32[384,384]{1,0:T(8,128)S(1)}) conditional(s32[]{:T(128)} %convert_element_type.15, f32[384,384]{0,1:T(8,128)S(1)} %get-tuple-element.307, (f32[384,384]{1,0:T(8,128)S(1)}, f32[384,384]{1,0:T(8,128)}, s32[]{:T(128)}, f32[384,384]{1,0:T(8,128)}, f32[384,384]{1,0:T(8,128)}, ...), branch_computations={%region_8.9_spmd, %region_9.10_spmd} | conditional | flops 4078190592 | bytes 24182908 | solution.py:55
  272.0 1.3 add_select_fusion.4
  274.6 3.9 %fusion.25 = f32[384,384]{1,0:T(8,128)} fusion(f32[384,384]{1,0:T(8,128)S(1)} %fusion.40, f32[384,384]{1,0:T(8,128)S(1)} %get-tuple-element.280, f32[384,384]{1,0:T(8,128)} %get-tuple-element.281, f32[384,384]{1,0:T(8,128)S(1)} %get-tuple-element.279, pred[]{:T(512)S(6)} %lt.39), kind=kOutput, calls=%fused_computation.51 | convolution fusion | flops 679919616 | bytes 2949121 | tf_op jit(solution)/shard_map/cond/branch_1_fun/dot_general | solution.py:15
  279.9 2.3 fusion.24
  284.3 2.0 fusion.26
  (48 shorter events, 25.3 us)
Async XLA Ops:
  0.6 4.6 %copy-start = (f32[1,384,384]{2,1,0:T(8,128)S(1)}, f32[1,384,384]{2,1,0:T(8,128)}, u32[]{:S(2)}) copy-start(f32[1,384,384]{2,1,0:T(8,128)} %param.14) | copy-start | bytes 1769476
  0.6 2.7 copy-start.1
  0.7 42.4 %collective-permute-start.1 = (f32[384,384]{1,0:T(8,128)S(1)}, f32[384,384]{1,0:T(8,128)S(1)}, u32[]{:S(2)}, u32[]{:S(2)}) collective-permute-start(f32[384,384]{1,0:T(8,128)S(1)} %broadcast_in_dim.24), channel_id=1, source_target_pairs={{0,16},{1,17},{2,18},{3,19},{4,20},{5,21},{6,22},{7,23},{8,24},{9,... | collective-permute-start | bytes 1769480 | tf_op jit(solution)/shard_map/ppermute | solution.py:11
  4.2 50.5 %collective-permute-start = (f32[384,384]{1,0:T(8,128)}, f32[384,384]{1,0:T(8,128)}, u32[]{:S(2)}, u32[]{:S(2)}) collective-permute-start(f32[384,384]{1,0:T(8,128)} %broadcast_select_fusion), channel_id=1, source_target_pairs={{0,16},{1,17},{2,18},{3,19},{4,20},{5,21},{6,22},{7,23},{8,24},{9,... | collective-permute-start | bytes 1769480 | tf_op jit(solution)/shard_map/ppermute | solution.py:11
  5.2 1.3 copy-start.6
  59.1 17.6 %collective-permute-start.5 = (f32[384,384]{1,0:T(8,128)}, f32[384,384]{1,0:T(8,128)}, u32[]{:S(2)}, u32[]{:S(2)}) collective-permute-start(f32[384,384]{1,0:T(8,128)} %copy.17), channel_id=1, source_target_pairs={{0,24},{1,25},{2,26},{3,27},{4,28},{5,29},{6,30},{7,31},{8,0},{9,1... | collective-permute-start | bytes 1769480 | tf_op jit(solution)/shard_map/ppermute | solution.py:11
  62.6 27.2 %collective-permute-start.2 = (f32[384,384]{1,0:T(8,128)}, f32[384,384]{1,0:T(8,128)}, u32[]{:S(2)}, u32[]{:S(2)}) collective-permute-start(f32[384,384]{1,0:T(8,128)} %copy.17), channel_id=1, source_target_pairs={{0,8},{1,9},{2,10},{3,11},{4,12},{5,13},{6,14},{7,15},{8,16},{9,17... | collective-permute-start | bytes 1769480 | tf_op jit(solution)/shard_map/ppermute | solution.py:11
  62.6 39.8 %collective-permute-start.3 = (f32[384,384]{0,1:T(8,128)}, f32[384,384]{0,1:T(8,128)}, u32[]{:S(2)}, u32[]{:S(2)}) collective-permute-start(f32[384,384]{0,1:T(8,128)} %get-tuple-element.299), channel_id=1, source_target_pairs={{0,8},{1,9},{2,10},{3,11},{4,12},{5,13},{6,14},{7,15},{8,16},{9,17... | collective-permute-start | bytes 1769480 | tf_op jit(solution)/shard_map/ppermute | solution.py:11
  62.6 51.0 %collective-permute-start.4 = (f32[384,384]{1,0:T(8,128)}, f32[384,384]{1,0:T(8,128)}, u32[]{:S(2)}, u32[]{:S(2)}) collective-permute-start(f32[384,384]{1,0:T(8,128)} %get-tuple-element.300), channel_id=1, source_target_pairs={{0,24},{1,25},{2,26},{3,27},{4,28},{5,29},{6,30},{7,31},{8,0},{9,1... | collective-permute-start | bytes 1769480 | tf_op jit(solution)/shard_map/ppermute | solution.py:11
  116.9 33.7 %collective-permute-start.9 = (f32[384,384]{1,0:T(8,128)}, f32[384,384]{1,0:T(8,128)}, u32[]{:S(2)}, u32[]{:S(2)}) collective-permute-start(f32[384,384]{1,0:T(8,128)} %copy.20), channel_id=1, source_target_pairs={{0,28},{1,29},{2,30},{3,31},{4,0},{5,1},{6,2},{7,3},{8,4},{9,5},{1... | collective-permute-start | bytes 1769480 | tf_op jit(solution)/shard_map/ppermute | solution.py:11
  117.4 42.0 %collective-permute-start.6 = (f32[384,384]{1,0:T(8,128)}, f32[384,384]{1,0:T(8,128)}, u32[]{:S(2)}, u32[]{:S(2)}) collective-permute-start(f32[384,384]{1,0:T(8,128)} %copy.20), channel_id=1, source_target_pairs={{0,4},{1,5},{2,6},{3,7},{4,8},{5,9},{6,10},{7,11},{8,12},{9,13},{1... | collective-permute-start | bytes 1769480 | tf_op jit(solution)/shard_map/ppermute | solution.py:11
  119.8 52.3 %collective-permute-start.7 = (f32[384,384]{0,1:T(8,128)}, f32[384,384]{0,1:T(8,128)}, u32[]{:S(2)}, u32[]{:S(2)}) collective-permute-start(f32[384,384]{0,1:T(8,128)} %get-tuple-element.302), channel_id=1, source_target_pairs={{0,4},{1,5},{2,6},{3,7},{4,8},{5,9},{6,10},{7,11},{8,12},{9,13},{1... | collective-permute-start | bytes 1769480 | tf_op jit(solution)/shard_map/ppermute | solution.py:11
  119.9 52.2 %collective-permute-start.8 = (f32[384,384]{1,0:T(8,128)}, f32[384,384]{1,0:T(8,128)}, u32[]{:S(2)}, u32[]{:S(2)}) collective-permute-start(f32[384,384]{1,0:T(8,128)} %get-tuple-element.303), channel_id=1, source_target_pairs={{0,28},{1,29},{2,30},{3,31},{4,0},{5,1},{6,2},{7,3},{8,4},{9,5},{1... | collective-permute-start | bytes 1769480 | tf_op jit(solution)/shard_map/ppermute | solution.py:11
  175.0 41.8 %collective-permute-start.13 = (f32[384,384]{1,0:T(8,128)}, f32[384,384]{1,0:T(8,128)}, u32[]{:S(2)}, u32[]{:S(2)}) collective-permute-start(f32[384,384]{1,0:T(8,128)} %copy.23), channel_id=1, source_target_pairs={{0,30},{1,31},{2,0},{3,1},{4,2},{5,3},{6,4},{7,5},{8,6},{9,7},{10,... | collective-permute-start | bytes 1769480 | tf_op jit(solution)/shard_map/ppermute | solution.py:11
  175.0 41.8 %collective-permute-start.10 = (f32[384,384]{1,0:T(8,128)}, f32[384,384]{1,0:T(8,128)}, u32[]{:S(2)}, u32[]{:S(2)}) collective-permute-start(f32[384,384]{1,0:T(8,128)} %copy.23), channel_id=1, source_target_pairs={{0,2},{1,3},{2,4},{3,5},{4,6},{5,7},{6,8},{7,9},{8,10},{9,11},{10,... | collective-permute-start | bytes 1769480 | tf_op jit(solution)/shard_map/ppermute | solution.py:11
  177.0 39.8 %collective-permute-start.11 = (f32[384,384]{0,1:T(8,128)}, f32[384,384]{0,1:T(8,128)}, u32[]{:S(2)}, u32[]{:S(2)}) collective-permute-start(f32[384,384]{0,1:T(8,128)} %get-tuple-element.305), channel_id=1, source_target_pairs={{0,2},{1,3},{2,4},{3,5},{4,6},{5,7},{6,8},{7,9},{8,10},{9,11},{10,... | collective-permute-start | bytes 1769480 | tf_op jit(solution)/shard_map/ppermute | solution.py:11
  178.7 49.9 %collective-permute-start.12 = (f32[384,384]{1,0:T(8,128)}, f32[384,384]{1,0:T(8,128)}, u32[]{:S(2)}, u32[]{:S(2)}) collective-permute-start(f32[384,384]{1,0:T(8,128)} %get-tuple-element.306), channel_id=1, source_target_pairs={{0,30},{1,31},{2,0},{3,1},{4,2},{5,3},{6,4},{7,5},{8,6},{9,7},{10,... | collective-permute-start | bytes 1769480 | tf_op jit(solution)/shard_map/ppermute | solution.py:11
  231.6 27.2 %collective-permute-start.17 = (f32[384,384]{1,0:T(8,128)}, f32[384,384]{1,0:T(8,128)}, u32[]{:S(2)}, u32[]{:S(2)}) collective-permute-start(f32[384,384]{1,0:T(8,128)} %copy.26), channel_id=1, source_target_pairs={{0,31},{1,0},{2,1},{3,2},{4,3},{5,4},{6,5},{7,6},{8,7},{9,8},{10,9... | collective-permute-start | bytes 1769480 | tf_op jit(solution)/shard_map/ppermute | solution.py:11
  248.6 16.2 %collective-permute-start.14 = (f32[384,384]{1,0:T(8,128)}, f32[384,384]{1,0:T(8,128)}, u32[]{:S(2)}, u32[]{:S(2)}) collective-permute-start(f32[384,384]{1,0:T(8,128)} %copy.26), channel_id=1, source_target_pairs={{0,1},{1,2},{2,3},{3,4},{4,5},{5,6},{6,7},{7,8},{8,9},{9,10},{10,1... | collective-permute-start | bytes 1769480 | tf_op jit(solution)/shard_map/ppermute | solution.py:11
  248.6 23.2 %collective-permute-start.15 = (f32[384,384]{0,1:T(8,128)}, f32[384,384]{0,1:T(8,128)}, u32[]{:S(2)}, u32[]{:S(2)}) collective-permute-start(f32[384,384]{0,1:T(8,128)} %get-tuple-element.308), channel_id=1, source_target_pairs={{0,1},{1,2},{2,3},{3,4},{4,5},{5,6},{6,7},{7,8},{8,9},{9,10},{10,1... | collective-permute-start | bytes 1769480 | tf_op jit(solution)/shard_map/ppermute | solution.py:11
  248.6 23.2 %collective-permute-start.16 = (f32[384,384]{1,0:T(8,128)}, f32[384,384]{1,0:T(8,128)}, u32[]{:S(2)}, u32[]{:S(2)}) collective-permute-start(f32[384,384]{1,0:T(8,128)} %get-tuple-element.309), channel_id=1, source_target_pairs={{0,31},{1,0},{2,1},{3,2},{4,3},{5,4},{6,5},{7,6},{8,7},{9,8},{10,9... | collective-permute-start | bytes 1769480 | tf_op jit(solution)/shard_map/ppermute | solution.py:11
  282.2 0.8 copy-start.2
  283.0 1.3 copy-start.5
  284.3 2.1 copy-start.3
where the time goes:
time: 292 us; the launch traced here: 289 us
  waiting for transfers between devices  213 us (73%)
  starting transfers between devices  41.4 us (14%)
  matrix products  14.6 us (5%)
  local copies, waits for them, and re-layouts  14.3 us (5%)
  other arithmetic  3.16 us (1%)
    ppermute x18, waiting for transfers between devices, passed_along(): lax.ppermute(array, axis, [(i, (i + by) % peers) for i in range(peers)])  213 us
    ppermute x18, starting transfers between devices, passed_along(): lax.ppermute(array, axis, [(i, (i + by) % peers) for i in range(peers)])  41.4 us
    dot_general x8, matrix products, product(): jnp.dot(left, right, precision=lax.Precision.HIGHEST, preferred_element_t...  14.6 us
    broadcast_in_dim x9, local copies, waits for them, and re-layouts, body(): zeros = jnp.zeros((width, width), jnp.float32)  6.89 us
  transfers between devices with their start and end apart: 18, of which 14 were waited for; matrix products, arithmetic and copies ran while one was open for 1% of the time, Pallas kernels for 0%

commit v1 on v0

v1 whole, which is shorter than its diff:
```python
import functools

import jax
import jax.numpy as jnp
from jax import lax
from jax.experimental import pallas as pl
from jax.experimental.pallas import tpu as pltpu
from jax.sharding import PartitionSpec as P

row_offset = 3
lanes = 128
group = 8
axis = "tm"
bf16 = jnp.bfloat16
f32 = jnp.float32


def sym_rows(width):
    blocks = width // lanes
    pairs = blocks // 2
    return (blocks * (blocks - 1) // 2 + blocks - pairs) * lanes + 8 * pairs


def full_rows(width):
    return width * (width // lanes)


def tri():
    r = lax.broadcasted_iota(jnp.int32, (lanes, lanes), 0)
    c = lax.broadcasted_iota(jnp.int32, (lanes, lanes), 1)
    return r, c


def put_sym(ref, at, mat):
    blocks = mat.shape[0] // lanes
    block = lambda i, j: mat[i * lanes : (i + 1) * lanes, j * lanes : (j + 1) * lanes]
    for i in range(blocks):
        for j in range(i):
            ref[pl.ds(at, lanes), :] = block(i, j)
            at += lanes
    r, c = tri()
    for i in range(0, blocks - 1, 2):
        one, two = block(i, i), block(i + 1, i + 1)
        ref[pl.ds(at, lanes), :] = jnp.where(r >= c, one, two)
        at += lanes
        line = jnp.sum(jnp.where(r == c, two, 0.0), axis=0, keepdims=True)
        ref[pl.ds(at, 8), :] = jnp.broadcast_to(line, (8, lanes))
        at += 8
    if blocks % 2:
        ref[pl.ds(at, lanes), :] = block(blocks - 1, blocks - 1)


def get_sym(ref, at, width):
    blocks = width // lanes
    got = {}
    for i in range(blocks):
        for j in range(i):
            got[i, j] = ref[pl.ds(at, lanes), :]
            got[j, i] = got[i, j].T
            at += lanes
    r, c = tri()
    for i in range(0, blocks - 1, 2):
        both = ref[pl.ds(at, lanes), :]
        turned = both.T
        at += lanes
        line = ref[pl.ds(at, 8), :][0:1, :]
        at += 8
        got[i, i] = jnp.where(r >= c, both, turned)
        got[i + 1, i + 1] = jnp.where(r == c, line, jnp.where(r < c, both, turned))
    if blocks % 2:
        got[blocks - 1, blocks - 1] = ref[pl.ds(at, lanes), :]
    return jnp.concatenate(
        [jnp.concatenate([got[i, j] for j in range(blocks)], axis=1) for i in range(blocks)], axis=0
    )


def put_full(ref, at, mat):
    width = mat.shape[0]
    for j in range(width // lanes):
        ref[pl.ds(at + j * width, width), :] = mat[:, j * lanes : (j + 1) * lanes]


def get_full(ref, at, width):
    return jnp.concatenate(
        [ref[pl.ds(at + j * width, width), :] for j in range(width // lanes)], axis=1
    )


def parts_of(mat):
    high = mat.astype(bf16)
    return high, (mat - high.astype(f32)).astype(bf16)


def times(left, right, turned=False):
    dims = (((1,), (1 if turned else 0,)), ((), ()))
    dot = lambda a, b: lax.dot_general(a, b, dims, preferred_element_type=f32)
    return dot(left[0], right[0]) + (dot(left[0], right[1]) + dot(left[1], right[0]))


def eliminate(node, state):
    diag, g_mat, h_mat = node
    aa, ba, bb = state
    low = times(g_mat, aa)
    if ba is not None:
        low = low + times(h_mat, ba)
        high = -(times(g_mat, ba, True) + times(h_mat, bb))
    low = -low
    low_parts = parts_of(low)
    own = diag - times(g_mat, low_parts, True)
    if ba is None:
        return own, low, low_parts, None, None
    high_parts = parts_of(high)
    own = own - times(h_mat, high_parts, True)
    return own, low, low_parts, high, high_parts


def place_now(length):
    return lax.rem(lax.axis_index(axis) + row_offset, length)


def fetch(source, target, sem):
    copy = pltpu.make_async_copy(source, target, sem)
    copy.start()
    copy.wait()


def prepare_kernel(inv_ref, low_ref, up_ref, node_ref, part_ref, sym_ref):
    width = inv_ref.shape[1]
    inverse = inv_ref[0]
    inv_parts = parts_of(inverse)
    put_sym(sym_ref, 0, inverse)
    ps, pf = sym_rows(width), full_rows(width)
    node_ref[pl.ds(0, ps), :] = sym_ref[...]
    part_ref[pl.ds(0, ps), :] = sym_ref[...]
    g_mat = times(inv_parts, parts_of(low_ref[0]))
    put_full(node_ref, ps, g_mat)
    put_full(part_ref, ps, g_mat)
    put_full(node_ref, ps + pf, times(inv_parts, parts_of(up_ref[0])))


def get_node(ref, width, whole=True):
    ps, pf = sym_rows(width), full_rows(width)
    return (
        get_sym(ref, 0, width),
        parts_of(get_full(ref, ps, width)),
        parts_of(get_full(ref, ps + pf, width)) if whole else None,
    )


def get_state(ref, width):
    ps, pf = sym_rows(width), full_rows(width)
    return (get_sym(ref, 0, width), get_full(ref, ps, width), get_sym(ref, ps + pf, width))


def put_state(ref, aa, ba, bb):
    width = aa.shape[0]
    ps, pf = sym_rows(width), full_rows(width)
    put_sym(ref, 0, aa)
    put_full(ref, ps, ba)
    put_sym(ref, ps + pf, bb)


def top_kernel(
    length,
    is_open,
    mid_node,
    mid_from_low,
    mid_from_high,
    own_node,
    low_node,
    root_mid,
    root_low,
    root_high,
    inv_ref,
    *refs,
):
    base_cross = None if is_open else refs[0]
    diag_ref, cross_ref, below_ref, above_ref, sym_ref = refs[-12:-7]
    first, second, root, aa_ref, ba_ref, bb_ref, sem = refs[-7:]
    width = inv_ref.shape[1]
    turn = lax.rem(place_now(length), 4 * group)
    at_low, at_mid, at_high = turn == group, turn == 2 * group, turn == 3 * group
    active = jnp.logical_or(at_low, jnp.logical_or(at_mid, at_high))

    @pl.when(jnp.logical_not(active))
    def _():
        diag_ref[0] = inv_ref[0]
        cross_ref[0] = jnp.zeros((width, width), f32) if is_open else base_cross[0]

    @pl.when(at_mid)
    def _():
        fetch(mid_node, first, sem)
        fetch(low_node, second, sem)
        fetch(root_mid, root, sem)

    @pl.when(at_low)
    def _():
        fetch(mid_from_high, first, sem)
        fetch(own_node, second, sem)
        fetch(root_low, root, sem)

    @pl.when(at_high)
    def _():
        fetch(mid_from_low, first, sem)
        fetch(own_node, second, sem)
        fetch(root_high, root, sem)

    @pl.when(active)
    def _():
        node = get_node(first, width, not is_open)
        if is_open:
            aa, ba, bb = get_sym(root, 0, width), None, None
            state = (parts_of(aa), None, None)
        else:
            aa, ba, bb = get_state(root, width)
            state = (parts_of(aa), parts_of(ba), parts_of(bb))
        own, low, _, high, _ = eliminate(node, state)

        @pl.when(at_mid)
        def _():
            diag_ref[0] = own
            cross_ref[0] = low

        @pl.when(jnp.logical_not(at_high))
        def _():
            aa_ref[...] = aa
            ba_ref[...] = low
            bb_ref[...] = own

        @pl.when(at_high)
        def _():
            aa_ref[...] = own
            if is_open:
                ba_ref[...] = jnp.zeros((width, width), f32)
                bb_ref[...] = jnp.zeros((width, width), f32)
            else:
                ba_ref[...] = high.T
                bb_ref[...] = bb

        aa2, ba2, bb2 = aa_ref[...], ba_ref[...], bb_ref[...]
        own2, low2, _, high2, _ = eliminate(
            get_node(second, width), (parts_of(aa2), parts_of(ba2), parts_of(bb2))
        )

        @pl.when(jnp.logical_not(at_mid))
        def _():
            diag_ref[0] = own2
            cross_ref[0] = low2
            put_state(below_ref, aa2, low2, own2)
            put_state(above_ref, own2, high2.T, bb2)
            put_sym(sym_ref, 0, own2)

        @pl.when(at_mid)
        def _():
            put_state(below_ref, own2, high2.T, bb2)


def offset_of(length):
    place = place_now(length)
    turn = lax.rem(place, 4 * group)
    offset = lax.rem(turn, group)
    return turn, offset, turn - offset == 3 * group


def choose_kernel(length, is_open, *refs):
    (from_low, from_high, to_three, to_five, to_seven, end_three, end_five, end_seven) = refs[:8]
    out_ref, zeros_ref, sem = refs[8:]
    rows, end_rows = out_ref.shape[0], end_three.shape[0]
    turn, offset, last = offset_of(length)
    lower = lax.rem(turn, 2 * group) < group

    def pick(condition, source):
        @pl.when(condition)
        def _():
            fetch(source, out_ref, sem)

    def pick_end(condition, source):
        if not is_open:
            return pick(condition, source)

        @pl.when(condition)
        def _():
            zeros_ref[...] = jnp.zeros(zeros_ref.shape, f32)
            fetch(source, out_ref.at[pl.ds(0, end_rows), :], sem)
            fetch(zeros_ref, out_ref.at[pl.ds(end_rows, rows - end_rows), :], sem)

    others = jnp.logical_not(last)
    pick(jnp.logical_and(offset == 1, lower), from_high)
    pick(jnp.logical_and(offset == 1, jnp.logical_not(lower)), from_low)
    for at, usual, end in ((3, to_three, end_three), (5, to_five, end_five), (7, to_seven, end_seven)):
        pick(jnp.logical_and(offset == at, others), usual)
        pick_end(jnp.logical_and(offset == at, last), end)


def go_down(node, refs, to_low):
    aa_ref, ba_ref, bb_ref = refs
    state = tuple(parts_of(ref[...]) for ref in refs)
    own, low, _, high, _ = eliminate(node, state)

    @pl.when(to_low)
    def _():
        ba_ref[...] = low
        bb_ref[...] = own

    @pl.when(jnp.logical_not(to_low))
    def _():
        aa_ref[...] = own
        ba_ref[...] = high.T


def odd_kernel(
    length, state, own_node, four_seven, four_five, four_one, near, nearer, _diag, _cross, diag_ref, cross_ref,
    state_ref, first, second, third, aa_ref, ba_ref, bb_ref, diag_out, cross_out, sem
):
    width = aa_ref.shape[0]
    _, offset, _ = offset_of(length)

    @pl.when(lax.rem(offset, 2) == 1)
    def _():
        fetch(state, state_ref, sem)
        fetch(own_node, third, sem)
        for at, four, two in ((1, four_one, near), (3, near, nearer), (5, four_five, near), (7, four_seven, nearer)):

            @pl.when(offset == at)
            def _(four=four, two=two):
                fetch(four, first, sem)
                fetch(two, second, sem)

        refs = (aa_ref, ba_ref, bb_ref)
        aa_ref[...], ba_ref[...], bb_ref[...] = get_state(state_ref, width)
        go_down(get_node(first, width), refs, offset < group // 2)
        go_down(get_node(second, width), refs, lax.rem(offset, group // 2) < group // 4)
        own, low, _, _, _ = eliminate(get_node(third, width), tuple(parts_of(ref[...]) for ref in refs))
        diag_out[...] = own
        cross_out[...] = low
        fetch(diag_out, diag_ref.at[0], sem)
        fetch(cross_out, cross_ref.at[0], sem)


def even_kernel(
    length, state, own_node, four_six, four_two, _diag, _cross, diag_ref, cross_ref,
    state_ref, first, third, aa_ref, ba_ref, bb_ref, diag_out, cross_out, sem,
):
    width = aa_ref.shape[0]
    _, offset, _ = offset_of(length)

    @pl.when(jnp.logical_and(lax.rem(offset, 2) == 0, offset > 0))
    def _():
        fetch(state, state_ref, sem)
        fetch(own_node, third, sem)
        refs = (aa_ref, ba_ref, bb_ref)
        aa_ref[...], ba_ref[...], bb_ref[...] = get_state(state_ref, width)

        @pl.when(offset != group // 2)
        def _():
            @pl.when(offset < group // 2)
            def _():
                fetch(four_two, first, sem)

            @pl.when(offset > group // 2)
            def _():
                fetch(four_six, first, sem)

            go_down(get_node(first, width), refs, offset < group // 2)

        own, low, _, _, _ = eliminate(get_node(third, width), tuple(parts_of(ref[...]) for ref in refs))
        diag_out[...] = own
        cross_out[...] = low
        fetch(diag_out, diag_ref.at[0], sem)
        fetch(cross_out, cross_ref.at[0], sem)


def pack_kernel(aa_ref, ba_ref, bb_ref, out_ref):
    put_state(out_ref, aa_ref[...], ba_ref[...], bb_ref[...])


def sent(array, length, by, wanted):
    device = lambda position: (position - row_offset) % length
    pairs = [(device(p), device(p + by)) for p in range(length) if wanted(p)]
    return lax.ppermute(array, axis, pairs)


def upper_levels(inverse, node_g, node_h, length):
    width = inverse.shape[0]
    place = (lax.axis_index(axis) + row_offset) % length
    product = functools.partial(jnp.dot, precision=lax.Precision.HIGHEST, preferred_element_type=f32)
    zeros = jnp.zeros((width, width), f32)
    sigma = jnp.where(place == 0, inverse, zeros)
    low_own, high_own, cross = zeros, zeros, zeros
    stride = length // 2
    while True:
        everywhere = lambda p: True
        from_low, owned_high = (sent(x, length, stride, everywhere) for x in (sigma, high_own))
        from_high, owned_low = (sent(x, length, -stride, everywhere) for x in (sigma, low_own))
        has_upper = place + stride < length
        sigma_high = jnp.where(has_upper, from_high, zeros)
        sigma_ba = jnp.where(has_upper, owned_high.T + owned_low, zeros)
        if stride == 2 * group:
            return sigma, cross, (from_low, sigma_ba, sigma_high)
        active = place % (2 * stride) == stride
        low = -(product(node_g, from_low) + product(node_h, sigma_ba))
        high = -(product(node_g, sigma_ba.T) + product(node_h, sigma_high))
        own = inverse - product(node_g, low.T) - product(node_h, high.T)
        sigma = jnp.where(active, own, sigma)
        low_own = jnp.where(active, low, zeros)
        high_own = jnp.where(active, high, zeros)
        cross = jnp.where(active, low, cross)
        stride //= 2


def body(inv_diag, low_coupling, up_coupling):
    width = inv_diag.shape[1]
    length = lax.axis_size(axis)
    is_open = length == 4 * group
    ps, pf = sym_rows(width), full_rows(width)
    node_rows, part_rows, state_rows = ps + 2 * pf, ps + pf, 2 * ps + pf
    rows_of = lambda rows: jax.ShapeDtypeStruct((rows, lanes), f32)
    square = (width, width)
    whole = jax.ShapeDtypeStruct((1,) + square, f32)
    vmem, anywhere = pl.BlockSpec(memory_space=pltpu.VMEM), pl.BlockSpec(memory_space=pl.ANY)
    room = lambda rows: pltpu.VMEM((rows, lanes), f32)
    params = pltpu.CompilerParams(vmem_limit_bytes=48 * 2**20)
    span = 4 * group

    def at(*turns):
        return lambda p: p % span in turns

    node, part, sym = pl.pallas_call(
        prepare_kernel,
        out_shape=(rows_of(node_rows), rows_of(part_rows), rows_of(ps)),
        in_specs=[vmem] * 3,
        out_specs=[vmem] * 3,
        compiler_params=params,
        name="prepare",
    )(inv_diag, low_coupling, up_coupling)

    mid = 2 * group
    if is_open:
        lead = part
        base_diag, base_cross = inv_diag, None
        root_mid, root_low, root_high = (sent(sym, length, by, at(0)) for by in (mid, group, 3 * group))
    else:
        lead = node
        g_mat, h_mat = (
            jnp.concatenate([node[ps + k * pf + j * width :][:width] for j in range(width // lanes)], axis=1)
            for k in (0, 1)
        )
        base_diag, base_cross, state = upper_levels(inv_diag[0], g_mat, h_mat, length)
        base_diag, base_cross = base_diag[None], base_cross[None]
        root_mid = pl.pallas_call(
            pack_kernel, out_shape=rows_of(state_rows), in_specs=[vmem] * 3, out_specs=vmem,
            compiler_params=params, name="pack",
        )(*state)
        root_low, root_high = (sent(root_mid, length, by, at(mid)) for by in (-group, group))
    mid_from_high = sent(lead, length, -group, at(mid))
    low_node = sent(node, length, group, at(group))
    mid_from_low = sent(lead, length, group, at(mid))

    half = group // 2
    inner = lambda *offsets: (lambda p: p % group in offsets)
    four_two = sent(node, length, -2, inner(half))
    four_six = sent(node, length, 2, inner(half))
    four_seven = sent(node, length, 3, inner(half))
    near = sent(node, length, -1, inner(2, 4, 6))
    nearer = sent(node, length, 1, inner(2, 6))
    four_one = sent(four_two, length, -1, inner(2))
    four_five = sent(four_six, length, -1, inner(6))

    top = functools.partial(top_kernel, length, is_open)
    root_rows = ps if is_open else state_rows
    diag, cross, below, above, end = pl.pallas_call(
        top,
        out_shape=(whole, whole, rows_of(state_rows), rows_of(state_rows), rows_of(ps)),
        in_specs=[anywhere] * 8 + [vmem] * (1 if is_open else 2),
        out_specs=[vmem] * 5,
        scratch_shapes=[room(lead.shape[0]), room(node_rows), room(root_rows)]
        + [pltpu.VMEM(square, f32)] * 3
        + [pltpu.SemaphoreType.DMA],
        compiler_params=params,
        name="upper",
    )(lead, mid_from_low, mid_from_high, node, low_node, root_mid, root_low, root_high, base_diag,
      *(() if is_open else (base_cross,)))

    to_three = sent(below, length, -5, at(group, mid, 3 * group))
    from_low = sent(above, length, 1, at(group, 3 * group))
    from_high = sent(below, length, -7, at(group, 3 * group))
    to_five = sent(below, length, -3, at(group, mid, 3 * group))
    to_seven = sent(below, length, -1, at(group, mid, 3 * group))
    end = end if is_open else above
    end_three, end_five, end_seven = (sent(end, length, by, at(3 * group)) for by in (3, 5, 7))
    state = pl.pallas_call(
        functools.partial(choose_kernel, length, is_open),
        out_shape=rows_of(state_rows),
        in_specs=[anywhere] * 8,
        out_specs=anywhere,
        scratch_shapes=[room(state_rows - ps), pltpu.SemaphoreType.DMA],
        compiler_params=params,
        name="choose",
    )(from_low, from_high, to_three, to_five, to_seven, end_three, end_five, end_seven)
    state_next = sent(state, length, 1, inner(1, 3, 5))

    def lower(kernel, name, inputs, nodes):
        count = len(inputs)
        return pl.pallas_call(
            functools.partial(kernel, length),
            out_shape=(whole, whole),
            in_specs=[anywhere] * (count + 2),
            out_specs=[anywhere] * 2,
            scratch_shapes=[room(state_rows)]
            + [room(node_rows)] * nodes
            + [pltpu.VMEM(square, f32)] * 5
            + [pltpu.SemaphoreType.DMA],
            input_output_aliases={count: 0, count + 1: 1},
            compiler_params=params,
            name=name,
        )(*inputs, diag, cross)

    diag, cross = lower(odd_kernel, "odd", (state, node, four_seven, four_five, four_one, near, nearer), 3)
    diag, cross = lower(even_kernel, "even", (state_next, node, four_six, four_two), 2)
    return diag, cross


def solution(mesh):
    placed = (P(axis, None, None),) * 3
    return jax.shard_map(
        body, mesh=mesh, in_specs=placed, out_specs=placed[:2], check_vma=False
    )
```

time: 292 us -> 117 us (0.40)
  the two profiles are of different devices: /device:TPU:4 before, /device:TPU:24 now
where the time goes in v1:
time: 117 us
  starting transfers between devices  68.2 us (58%)
  waiting for transfers between devices  22.5 us (19%)
  Pallas kernels  19.2 us (16%)
  local copies, waits for them, and re-layouts  5.71 us (5%)
  between operations  1.25 us (1%)
    ppermute x22, starting transfers between devices, sent(): return lax.ppermute(array, axis, pairs)  68.2 us
    ppermute x22, waiting for transfers between devices, sent(): return lax.ppermute(array, axis, pairs)  22.5 us
    pallas_call x2, Pallas kernels, lower(): pl.pallas_call(functools.partial(kernel, length), out_shape=(whole, whole...  15.9 us
    unnamed x18, local copies, waits for them, and re-layouts  5.71 us
  transfers between devices with their start and end apart: 22, of which 1 were waited for; matrix products, arithmetic and copies ran while one was open for 0% of the time, Pallas kernels for 15%

profile of v1, /device:TPU:24, one launch (start us, length us, event | category | flops | bytes accessed | tf_op | source)
XLA Modules:
  0.0 116.9 jit_solution(14739780382629366899)
XLA Ops:
  0.6 1.1 copy-done.2
  1.7 1.1 copy-done.3
  2.8 1.1 copy-done.4
  3.8 1.3 %prepare.1 = (f32[2952,128]{1,0:T(8,128)S(1)}, f32[1800,128]{1,0:T(8,128)S(1)}, f32[648,128]{1,0:T(8,128)S(1)}) custom-call(f32[1,384,384]{2,1,0:T(8,128)S(1)} %copy-done.2, f32[1,384,384]{2,1,0:T(8,128)S(1)} %copy-done.3, f32[1,384,384]{2,1,0:T(8,128)S(1)} %copy-done.4), custom_call_target="tpu_custom_call" | custom-call | tf_op jit(solution)/shard_map/prepare/pallas_call | solution.py:428
  5.2 0.8 collective-permute-start.2
  5.9 0.7 collective-permute-start.3
  6.6 0.7 collective-permute-start.4
  7.3 0.7 collective-permute-start
  8.0 0.7 collective-permute-start.1
  8.8 0.7 collective-permute-start.5
  9.5 0.8 collective-permute-start.15
  10.2 0.8 collective-permute-start.16
  11.1 1.1 copy-done.6
  12.2 1.6 %upper.1 = (f32[1,384,384]{2,1,0:T(8,128)}, f32[1,384,384]{2,1,0:T(8,128)}, f32[2448,128]{1,0:T(8,128)S(1)}, f32[2448,128]{1,0:T(8,128)}, f32[648,128]{1,0:T(8,128)S(1)}) custom-call(f32[1800,128]{1,0:T(8,128)S(1)} %get-tuple-element.12.mid_node, f32[1800,128]{1,0:T(8,128)S(1)} %collective-permute-done.mid_from_low, ...), custom_call_target="tpu_custom_call" | custom-call | tf_op jit(solution)/shard_map/upper/pallas_call | solution.py:471
  13.7 0.7 collective-permute-start.10
  14.5 1.3 %collective-permute-start.11 = (f32[648,128]{1,0:T(8,128)S(1)}, f32[648,128]{1,0:T(8,128)S(1)}, u32[]{:S(2)}, u32[]{:S(2)}) collective-permute-start(f32[648,128]{1,0:T(8,128)S(1)} %get-tuple-element.17), channel_id=1, source_target_pairs={{21,24}} | collective-permute-start | bytes 995336 | tf_op jit(solution)/shard_map/ppermute | solution.py:380
  15.8 0.7 collective-permute-start.12
  16.5 0.7 collective-permute-start.13
  17.2 0.7 collective-permute-start.7
  17.9 22.4 %collective-permute-done.11.refs_5_ = f32[648,128]{1,0:T(8,128)S(1)} collective-permute-done((f32[648,128]{1,0:T(8,128)S(1)}, f32[648,128]{1,0:T(8,128)S(1)}, u32[]{:S(2)}, u32[]{:S(2)}) %collective-permute-start.11) | collective-permute-done | bytes 331808 | tf_op jit(solution)/shard_map/ppermute | solution.py:380
  40.4 0.7 collective-permute-start.8
  41.1 0.7 collective-permute-start.9
  41.9 0.9 collective-permute-start.6
  42.8 0.8 collective-permute-start.17
  43.6 1.3 %collective-permute-start.20 = (f32[2952,128]{1,0:T(8,128)}, f32[2952,128]{1,0:T(8,128)S(1)}, u32[]{:S(2)}, u32[]{:S(2)}) collective-permute-start(f32[2952,128]{1,0:T(8,128)} %copy-done), channel_id=1, source_target_pairs={{31,30},{1,0},{3,2},{7,6},{9,8},{11,10},{15,14},{17,16},{19,18},{2... | collective-permute-start | bytes 4534280 | tf_op jit(solution)/shard_map/ppermute | solution.py:380
  44.9 1.3 %collective-permute-start.21 = (f32[2952,128]{1,0:T(8,128)}, f32[2952,128]{1,0:T(8,128)}, u32[]{:S(2)}, u32[]{:S(2)}) collective-permute-start(f32[2952,128]{1,0:T(8,128)} %copy-done), channel_id=1, source_target_pairs={{31,0},{3,4},{7,8},{11,12},{15,16},{19,20},{23,24},{27,28}} | collective-permute-start | bytes 4534280 | tf_op jit(solution)/shard_map/ppermute | solution.py:380
  46.2 0.8 collective-permute-start.18
  47.2 1.8 %collective-permute-start.19 = (f32[2952,128]{1,0:T(8,128)S(1)}, f32[2952,128]{1,0:T(8,128)}, u32[]{:S(2)}, u32[]{:S(2)}) collective-permute-start(f32[2952,128]{1,0:T(8,128)S(1)} %collective-permute-done.16.four_two), channel_id=1, source_target_pairs={{31,30},{7,6},{15,14},{23,22}} | collective-permute-start | bytes 4534280 | tf_op jit(solution)/shard_map/ppermute | solution.py:380
  49.0 0.4 choose.1.state
  49.5 50.1 %collective-permute-start.14 = (f32[2448,128]{1,0:T(8,128)S(1)}, f32[2448,128]{1,0:T(8,128)S(1)}, u32[]{:S(2)}, u32[]{:S(2)}) collective-permute-start(f32[2448,128]{1,0:T(8,128)S(1)} %choose.1.state), channel_id=1, source_target_pairs={{30,31},{0,1},{2,3},{6,7},{8,9},{10,11},{14,15},{16,17},{18,19},{2... | collective-permute-start | bytes 3760136 | tf_op jit(solution)/shard_map/ppermute | solution.py:380
  99.6 1.1 copy-done.5
  100.8 15.9 %odd.1 = (f32[1,384,384]{2,1,0:T(8,128)}, f32[1,384,384]{2,1,0:T(8,128)}) custom-call(f32[2448,128]{1,0:T(8,128)S(1)} %choose.1.state, f32[2952,128]{1,0:T(8,128)S(1)} %copy-done.1, f32[2952,128]{1,0:T(8,128)S(1)} %collective-permute-done.17.four_seven, ...), custom_call_target="tpu_custom_call", output_to_operand_aliasing={{0}: (7, {}), {1}: (8, {})} | custom-call | tf_op jit(solution)/shard_map/odd/pallas_call | solution.py:504
  (35 shorter events, 0.4 us)
Async XLA Ops:
  0.6 1.1 copy-start.2
  1.7 1.1 copy-start.3
  2.8 1.1 copy-start.4
  5.2 5.9 %copy-start = (f32[2952,128]{1,0:T(8,128)}, f32[2952,128]{1,0:T(8,128)S(1)}, u32[]{:S(2)}) copy-start(f32[2952,128]{1,0:T(8,128)S(1)} %get-tuple-element.13.own_node) | copy-start | bytes 4534276
  5.2 5.9 %collective-permute-start.2 = (f32[2952,128]{1,0:T(8,128)S(1)}, f32[2952,128]{1,0:T(8,128)S(1)}, u32[]{:S(2)}, u32[]{:S(2)}) collective-permute-start(f32[2952,128]{1,0:T(8,128)S(1)} %get-tuple-element.13.own_node), channel_id=1, source_target_pairs={{5,13}} | collective-permute-start | bytes 4534280 | tf_op jit(solution)/shard_map/ppermute | solution.py:380
  5.9 2.8 %collective-permute-start.3 = (f32[648,128]{1,0:T(8,128)S(1)}, f32[648,128]{1,0:T(8,128)S(1)}, u32[]{:S(2)}, u32[]{:S(2)}) collective-permute-start(f32[648,128]{1,0:T(8,128)S(1)} %get-tuple-element.14), channel_id=1, source_target_pairs={{29,13}} | collective-permute-start | bytes 995336 | tf_op jit(solution)/shard_map/ppermute | solution.py:380
  6.6 2.8 %collective-permute-start.4 = (f32[648,128]{1,0:T(8,128)S(1)}, f32[648,128]{1,0:T(8,128)S(1)}, u32[]{:S(2)}, u32[]{:S(2)}) collective-permute-start(f32[648,128]{1,0:T(8,128)S(1)} %get-tuple-element.14), channel_id=1, source_target_pairs={{29,5}} | collective-permute-start | bytes 995336 | tf_op jit(solution)/shard_map/ppermute | solution.py:380
  7.3 3.7 %collective-permute-start = (f32[1800,128]{1,0:T(8,128)S(1)}, f32[1800,128]{1,0:T(8,128)S(1)}, u32[]{:S(2)}, u32[]{:S(2)}) collective-permute-start(f32[1800,128]{1,0:T(8,128)S(1)} %get-tuple-element.12.mid_node), channel_id=1, source_target_pairs={{13,21}} | collective-permute-start | bytes 2764808 | tf_op jit(solution)/shard_map/ppermute | solution.py:380
  8.0 3.0 %collective-permute-start.1 = (f32[1800,128]{1,0:T(8,128)S(1)}, f32[1800,128]{1,0:T(8,128)S(1)}, u32[]{:S(2)}, u32[]{:S(2)}) collective-permute-start(f32[1800,128]{1,0:T(8,128)S(1)} %get-tuple-element.12.mid_node), channel_id=1, source_target_pairs={{13,5}} | collective-permute-start | bytes 2764808 | tf_op jit(solution)/shard_map/ppermute | solution.py:380
  8.8 1.5 %collective-permute-start.5 = (f32[648,128]{1,0:T(8,128)S(1)}, f32[648,128]{1,0:T(8,128)S(1)}, u32[]{:S(2)}, u32[]{:S(2)}) collective-permute-start(f32[648,128]{1,0:T(8,128)S(1)} %get-tuple-element.14), channel_id=1, source_target_pairs={{29,21}} | collective-permute-start | bytes 995336 | tf_op jit(solution)/shard_map/ppermute | solution.py:380
  9.5 7.0 %collective-permute-start.15 = (f32[2952,128]{1,0:T(8,128)S(1)}, f32[2952,128]{1,0:T(8,128)S(1)}, u32[]{:S(2)}, u32[]{:S(2)}) collective-permute-start(f32[2952,128]{1,0:T(8,128)S(1)} %get-tuple-element.13.own_node), channel_id=1, source_target_pairs={{1,3},{9,11},{17,19},{25,27}} | collective-permute-start | bytes 4534280 | tf_op jit(solution)/shard_map/ppermute | solution.py:380
  10.2 6.9 %collective-permute-start.16 = (f32[2952,128]{1,0:T(8,128)S(1)}, f32[2952,128]{1,0:T(8,128)S(1)}, u32[]{:S(2)}, u32[]{:S(2)}) collective-permute-start(f32[2952,128]{1,0:T(8,128)S(1)} %get-tuple-element.13.own_node), channel_id=1, source_target_pairs={{1,31},{9,7},{17,15},{25,23}} | collective-permute-start | bytes 4534280 | tf_op jit(solution)/shard_map/ppermute | solution.py:380
  11.1 1.1 copy-start.6
  13.7 29.0 %collective-permute-start.10 = (f32[2448,128]{1,0:T(8,128)S(1)}, f32[2448,128]{1,0:T(8,128)S(1)}, u32[]{:S(2)}, u32[]{:S(2)}) collective-permute-start(f32[2448,128]{1,0:T(8,128)S(1)} %get-tuple-element.16), channel_id=1, source_target_pairs={{5,4},{13,12},{21,20}} | collective-permute-start | bytes 3760136 | tf_op jit(solution)/shard_map/ppermute | solution.py:380
  14.5 25.9 %collective-permute-start.11 = (f32[648,128]{1,0:T(8,128)S(1)}, f32[648,128]{1,0:T(8,128)S(1)}, u32[]{:S(2)}, u32[]{:S(2)}) collective-permute-start(f32[648,128]{1,0:T(8,128)S(1)} %get-tuple-element.17), channel_id=1, source_target_pairs={{21,24}} | collective-permute-start | bytes 995336 | tf_op jit(solution)/shard_map/ppermute | solution.py:380
  15.8 25.3 %collective-permute-start.12 = (f32[648,128]{1,0:T(8,128)S(1)}, f32[648,128]{1,0:T(8,128)S(1)}, u32[]{:S(2)}, u32[]{:S(2)}) collective-permute-start(f32[648,128]{1,0:T(8,128)S(1)} %get-tuple-element.17), channel_id=1, source_target_pairs={{21,26}} | collective-permute-start | bytes 995336 | tf_op jit(solution)/shard_map/ppermute | solution.py:380
  16.5 25.4 %collective-permute-start.13 = (f32[648,128]{1,0:T(8,128)S(1)}, f32[648,128]{1,0:T(8,128)S(1)}, u32[]{:S(2)}, u32[]{:S(2)}) collective-permute-start(f32[648,128]{1,0:T(8,128)S(1)} %get-tuple-element.17), channel_id=1, source_target_pairs={{21,28}} | collective-permute-start | bytes 995336 | tf_op jit(solution)/shard_map/ppermute | solution.py:380
  17.2 26.4 %collective-permute-start.7 = (f32[2448,128]{1,0:T(8,128)S(1)}, f32[2448,128]{1,0:T(8,128)S(1)}, u32[]{:S(2)}, u32[]{:S(2)}) collective-permute-start(f32[2448,128]{1,0:T(8,128)S(1)} %get-tuple-element.16), channel_id=1, source_target_pairs={{5,30},{21,14}} | collective-permute-start | bytes 3760136 | tf_op jit(solution)/shard_map/ppermute | solution.py:380
  40.4 4.5 %collective-permute-start.8 = (f32[2448,128]{1,0:T(8,128)S(1)}, f32[2448,128]{1,0:T(8,128)S(1)}, u32[]{:S(2)}, u32[]{:S(2)}) collective-permute-start(f32[2448,128]{1,0:T(8,128)S(1)} %get-tuple-element.16), channel_id=1, source_target_pairs={{5,0},{13,8},{21,16}} | collective-permute-start | bytes 3760136 | tf_op jit(solution)/shard_map/ppermute | solution.py:380
  41.1 5.1 %collective-permute-start.9 = (f32[2448,128]{1,0:T(8,128)S(1)}, f32[2448,128]{1,0:T(8,128)S(1)}, u32[]{:S(2)}, u32[]{:S(2)}) collective-permute-start(f32[2448,128]{1,0:T(8,128)S(1)} %get-tuple-element.16), channel_id=1, source_target_pairs={{5,2},{13,10},{21,18}} | collective-permute-start | bytes 3760136 | tf_op jit(solution)/shard_map/ppermute | solution.py:380
  41.9 58.9 %copy-start.1 = (f32[2952,128]{1,0:T(8,128)S(1)}, f32[2952,128]{1,0:T(8,128)}, u32[]{:S(2)}) copy-start(f32[2952,128]{1,0:T(8,128)} %copy-done) | copy-start | bytes 4534276
  41.9 5.1 %collective-permute-start.6 = (f32[2448,128]{1,0:T(8,128)}, f32[2448,128]{1,0:T(8,128)S(1)}, u32[]{:S(2)}, u32[]{:S(2)}) collective-permute-start(f32[2448,128]{1,0:T(8,128)} %get-tuple-element.15), channel_id=1, source_target_pairs={{5,6},{21,22}} | collective-permute-start | bytes 3760136 | tf_op jit(solution)/shard_map/ppermute | solution.py:380
  42.8 4.2 %copy-start.7 = (f32[2448,128]{1,0:T(8,128)}, f32[2448,128]{1,0:T(8,128)S(1)}, u32[]{:S(2)}) copy-start(f32[2448,128]{1,0:T(8,128)S(1)} %collective-permute-done.10.refs_4_) | copy-start | bytes 3760132
  42.8 6.7 %collective-permute-start.17 = (f32[2952,128]{1,0:T(8,128)}, f32[2952,128]{1,0:T(8,128)S(1)}, u32[]{:S(2)}, u32[]{:S(2)}) collective-permute-start(f32[2952,128]{1,0:T(8,128)} %copy-done), channel_id=1, source_target_pairs={{1,4},{9,12},{17,20},{25,28}} | collective-permute-start | bytes 4534280 | tf_op jit(solution)/shard_map/ppermute | solution.py:380
  43.6 56.0 %collective-permute-start.20 = (f32[2952,128]{1,0:T(8,128)}, f32[2952,128]{1,0:T(8,128)S(1)}, u32[]{:S(2)}, u32[]{:S(2)}) collective-permute-start(f32[2952,128]{1,0:T(8,128)} %copy-done), channel_id=1, source_target_pairs={{31,30},{1,0},{3,2},{7,6},{9,8},{11,10},{15,14},{17,16},{19,18},{2... | collective-permute-start | bytes 4534280 | tf_op jit(solution)/shard_map/ppermute | solution.py:380
  44.9 54.7 %collective-permute-start.21 = (f32[2952,128]{1,0:T(8,128)}, f32[2952,128]{1,0:T(8,128)}, u32[]{:S(2)}, u32[]{:S(2)}) collective-permute-start(f32[2952,128]{1,0:T(8,128)} %copy-done), channel_id=1, source_target_pairs={{31,0},{3,4},{7,8},{11,12},{15,16},{19,20},{23,24},{27,28}} | collective-permute-start | bytes 4534280 | tf_op jit(solution)/shard_map/ppermute | solution.py:380
  46.2 1.1 copy-start.8
  46.2 53.4 %collective-permute-start.18 = (f32[2952,128]{1,0:T(8,128)S(1)}, f32[2952,128]{1,0:T(8,128)S(1)}, u32[]{:S(2)}, u32[]{:S(2)}) collective-permute-start(f32[2952,128]{1,0:T(8,128)S(1)} %collective-permute-done.15.four_six), channel_id=1, source_target_pairs={{3,2},{11,10},{19,18},{27,26}} | collective-permute-start | bytes 4534280 | tf_op jit(solution)/shard_map/ppermute | solution.py:380
  47.2 52.4 %collective-permute-start.19 = (f32[2952,128]{1,0:T(8,128)S(1)}, f32[2952,128]{1,0:T(8,128)}, u32[]{:S(2)}, u32[]{:S(2)}) collective-permute-start(f32[2952,128]{1,0:T(8,128)S(1)} %collective-permute-done.16.four_two), channel_id=1, source_target_pairs={{31,30},{7,6},{15,14},{23,22}} | collective-permute-start | bytes 4534280 | tf_op jit(solution)/shard_map/ppermute | solution.py:380
  49.5 67.2 %collective-permute-start.14 = (f32[2448,128]{1,0:T(8,128)S(1)}, f32[2448,128]{1,0:T(8,128)S(1)}, u32[]{:S(2)}, u32[]{:S(2)}) collective-permute-start(f32[2448,128]{1,0:T(8,128)S(1)} %choose.1.state), channel_id=1, source_target_pairs={{30,31},{0,1},{2,3},{6,7},{8,9},{10,11},{14,15},{16,17},{18,19},{2... | collective-permute-start | bytes 3760136 | tf_op jit(solution)/shard_map/ppermute | solution.py:380
  99.6 1.2 %copy-start.5 = (f32[2952,128]{1,0:T(8,128)}, f32[2952,128]{1,0:T(8,128)S(1)}, u32[]{:S(2)}) copy-start(f32[2952,128]{1,0:T(8,128)S(1)} %collective-permute-done.20.near) | copy-start | bytes 4534276

commit v2 on v0

v2 whole, which is shorter than its diff:
```python
import functools

import jax
import jax.numpy as jnp
from jax import lax
from jax.experimental import pallas as pl
from jax.experimental.pallas import tpu as pltpu
from jax.sharding import PartitionSpec as P

row_offset = 3
lanes = 128
group = 8
axis = "tm"
bf16 = jnp.bfloat16
f32 = jnp.float32


def sym_rows(width):
    blocks = width // lanes
    pairs = blocks // 2
    return (blocks * (blocks - 1) // 2 + blocks - pairs) * lanes + 8 * pairs


def full_rows(width):
    return width * (width // lanes)


def tri():
    r = lax.broadcasted_iota(jnp.int32, (lanes, lanes), 0)
    c = lax.broadcasted_iota(jnp.int32, (lanes, lanes), 1)
    return r, c


def put_sym(ref, at, mat):
    blocks = mat.shape[0] // lanes
    block = lambda i, j: mat[i * lanes : (i + 1) * lanes, j * lanes : (j + 1) * lanes]
    for i in range(blocks):
        for j in range(i):
            ref[pl.ds(at, lanes), :] = block(i, j)
            at += lanes
    r, c = tri()
    for i in range(0, blocks - 1, 2):
        one, two = block(i, i), block(i + 1, i + 1)
        ref[pl.ds(at, lanes), :] = jnp.where(r >= c, one, two)
        at += lanes
        line = jnp.sum(jnp.where(r == c, two, 0.0), axis=0, keepdims=True)
        ref[pl.ds(at, 8), :] = jnp.broadcast_to(line, (8, lanes))
        at += 8
    if blocks % 2:
        ref[pl.ds(at, lanes), :] = block(blocks - 1, blocks - 1)


def get_sym(ref, at, width):
    blocks = width // lanes
    got = {}
    for i in range(blocks):
        for j in range(i):
            got[i, j] = ref[pl.ds(at, lanes), :]
            got[j, i] = got[i, j].T
            at += lanes
    r, c = tri()
    for i in range(0, blocks - 1, 2):
        both = ref[pl.ds(at, lanes), :]
        turned = both.T
        at += lanes
        line = ref[pl.ds(at, 8), :][0:1, :]
        at += 8
        got[i, i] = jnp.where(r >= c, both, turned)
        got[i + 1, i + 1] = jnp.where(r == c, line, jnp.where(r < c, both, turned))
    if blocks % 2:
        got[blocks - 1, blocks - 1] = ref[pl.ds(at, lanes), :]
    return jnp.concatenate(
        [jnp.concatenate([got[i, j] for j in range(blocks)], axis=1) for i in range(blocks)], axis=0
    )


def put_full(ref, at, mat):
    width = mat.shape[0]
    for j in range(width // lanes):
        ref[pl.ds(at + j * width, width), :] = mat[:, j * lanes : (j + 1) * lanes]


def get_full(ref, at, width):
    return jnp.concatenate(
        [ref[pl.ds(at + j * width, width), :] for j in range(width // lanes)], axis=1
    )


def parts_of(mat):
    high = mat.astype(bf16)
    return high, (mat - high.astype(f32)).astype(bf16)


def times(left, right, turned=False):
    dims = (((1,), (1 if turned else 0,)), ((), ()))
    dot = lambda a, b: lax.dot_general(a, b, dims, preferred_element_type=f32)
    return dot(left[0], right[0]) + (dot(left[0], right[1]) + dot(left[1], right[0]))


def place_now(length):
    return lax.rem(lax.axis_index(axis) + row_offset, length)


def fetch(sems, *pairs):
    copies = [pltpu.make_async_copy(source, target, sems.at[i]) for i, (source, target) in enumerate(pairs)]
    for copy in copies:
        copy.start()
    for copy in copies:
        copy.wait()


def own_kernel(inv_ref, low_ref, up_ref, sym_ref, part_ref, node_ref, rooms, sems):
    width = inv_ref.shape[1]
    fetch(sems, *((ref.at[0], rooms.at[i]) for i, ref in enumerate((inv_ref, low_ref, up_ref))))
    inverse = rooms[0]
    inv_parts = parts_of(inverse)
    ps, pf = sym_rows(width), full_rows(width)
    put_sym(sym_ref, 0, inverse)
    part_ref[pl.ds(0, ps), :] = sym_ref[...]
    put_full(part_ref, ps, times(inv_parts, parts_of(rooms[1])))
    node_ref[pl.ds(0, ps + pf), :] = part_ref[...]
    put_full(node_ref, ps + pf, times(inv_parts, parts_of(rooms[2])))


def get_node(ref, width):
    ps, pf = sym_rows(width), full_rows(width)
    return get_sym(ref, 0, width), get_full(ref, ps, width), get_full(ref, ps + pf, width)


def put_state(ref, aa, ba, bb):
    ps = sym_rows(aa.shape[0])
    put_sym(ref, 0, aa)
    put_sym(ref, ps, bb)
    put_full(ref, 2 * ps, ba)


def roles_of(length):
    place = place_now(length)
    return place == 0, place == group, place == 2 * group, place == 3 * group


def ahead_kernel(length, node, came_part, came_root, out, sym_ref):
    width = out.shape[1]
    ps = sym_rows(width)
    _, at_low, at_mid, _ = roles_of(length)

    @pl.when(at_low)
    def _():
        own_d, own_g, own_h = get_node(node, width)
        h_parts = parts_of(own_h)
        out[0] = times(h_parts, parts_of(get_full(came_part, ps, width))) - own_g
        passed = times(h_parts, parts_of(get_sym(came_part, 0, width)))
        out[1] = own_d + times(parts_of(passed), h_parts, True)

    @pl.when(at_mid)
    def _():
        own_d, own_g, _ = get_node(node, width)
        own_parts = parts_of(own_g)
        cross = -times(own_parts, parts_of(get_sym(came_root, 0, width)))
        own = own_d - times(own_parts, parts_of(cross), True)
        put_sym(sym_ref, 0, own)
        out[0] = cross
        out[1] = own


def halve(four, state, low_ref, high_ref):
    aa, ba, bb = state
    width = aa.shape[0]
    diag, g_mat, h_mat = get_node(four, width)
    g_parts, h_parts = parts_of(g_mat), parts_of(h_mat)
    ba_parts = parts_of(ba)
    low = -(times(g_parts, parts_of(aa)) + times(h_parts, ba_parts))
    put_full(low_ref, 2 * sym_rows(width), low)
    high = -(times(g_parts, ba_parts, True) + times(h_parts, parts_of(bb)))
    put_full(high_ref, 2 * sym_rows(width), high.T)
    own = diag - times(g_parts, parts_of(low), True) - times(h_parts, parts_of(high), True)
    ps = sym_rows(width)
    put_sym(low_ref, 0, aa)
    put_sym(low_ref, ps, own)
    high_ref[pl.ds(0, ps), :] = low_ref[pl.ds(ps, ps), :]
    put_sym(high_ref, ps, bb)


def upper_kernel(
    length, ahead, root_mid, root_low, mid_high, mid_zero, node, came_node, came_four,
    diag_ref, cross_ref, low_ref, high_ref, aa_ref, ba_ref, bb_ref,
):
    width = aa_ref.shape[0]
    at_zero, at_low, at_mid, at_high = roles_of(length)

    @pl.when(at_low)
    def _():
        root = get_sym(root_low, 0, width)
        passed = parts_of(ahead[0])
        cross = times(passed, parts_of(root))
        own = ahead[1] + times(parts_of(cross), passed, True)
        diag_ref[0], cross_ref[0] = own, cross
        aa_ref[...], ba_ref[...], bb_ref[...] = root, cross, own

    @pl.when(at_mid)
    def _():
        mid_cross, mid = ahead[0], ahead[1]
        diag_ref[0], cross_ref[0] = mid, mid_cross
        low_d, low_g, low_h = get_node(came_node, width)
        low_g, low_h = parts_of(low_g), parts_of(low_h)
        cross_parts = parts_of(mid_cross)
        part_low = -(times(low_g, parts_of(get_sym(root_mid, 0, width))) + times(low_h, cross_parts))
        part_high = -(times(low_g, cross_parts, True) + times(low_h, parts_of(mid)))
        own = low_d - times(low_g, parts_of(part_low), True) - times(low_h, parts_of(part_high), True)
        aa_ref[...], ba_ref[...], bb_ref[...] = own, part_high.T, mid

    def above(mid_ref, node_ref):
        own_d, own_g, _ = get_node(node_ref, width)
        mid = get_sym(mid_ref, 0, width)
        own_g = parts_of(own_g)
        cross = -times(own_g, parts_of(mid))
        return mid, cross, own_d - times(own_g, parts_of(cross), True)

    @pl.when(at_high)
    def _():
        mid, cross, own = above(mid_high, node)
        diag_ref[0], cross_ref[0] = own, cross
        aa_ref[...], ba_ref[...], bb_ref[...] = mid, cross, own

    @pl.when(at_zero)
    def _():
        _, _, own = above(mid_zero, came_node)
        zeros = jnp.zeros((width, width), f32)
        diag_ref[0], cross_ref[0] = get_sym(node, 0, width), zeros
        aa_ref[...], ba_ref[...], bb_ref[...] = own, zeros, zeros

    @pl.when(lax.rem(place_now(length), group) == 0)
    def _():
        halve(came_four, (aa_ref[...], ba_ref[...], bb_ref[...]), low_ref, high_ref)


def halve_kernel(came_four, aa_ref, ba_ref, bb_ref, low_ref, high_ref):
    halve(came_four, (aa_ref[...], ba_ref[...], bb_ref[...]), low_ref, high_ref)


def offset_of(length):
    return lax.rem(place_now(length), group)


def near_kernel(length, node, came_near, came_far, came_back, f_high, f_low, rest_ref):
    width = rest_ref.shape[0]
    turn = lax.rem(offset_of(length), group // 2)
    first, second = slice(0, width), slice(width, 2 * width)

    def put(rows, columns, mat):
        f_high[rows, columns], f_low[rows, columns] = parts_of(mat)

    def put_unit():
        r = lax.broadcasted_iota(jnp.int32, (width, 2 * width), 0)
        c = lax.broadcasted_iota(jnp.int32, (width, 2 * width), 1)
        f_high[second, :] = jnp.where(r == c, 1.0, 0.0).astype(bf16)
        f_low[second, :] = jnp.zeros((width, 2 * width), bf16)
        rest_ref[:, second] = jnp.zeros((width, width), f32)

    @pl.when(turn == 2)
    def _():
        d_own, g_own, h_own = get_node(node, width)
        put(first, first, -g_own)
        put(first, second, -h_own)
        rest_ref[:, first] = d_own
        put_unit()

    def odd(below, two):
        d_own, g_own, h_own = get_node(node, width)
        d_two, g_two, h_two = get_node(two, width)
        inward, outward = (h_own, g_own) if below else (g_own, h_own)
        inward = parts_of(inward)
        to_low, to_high = times(inward, parts_of(g_two)), times(inward, parts_of(h_two))
        put(first, first, to_low - outward if below else to_low)
        put(first, second, to_high if below else to_high - outward)
        link = -times(inward, parts_of(d_two))
        rest_ref[:, first] = d_own - times(inward, parts_of(link), True)
        if below:
            put_unit()
        else:
            put(second, first, -g_two)
            put(second, second, -h_two)
            rest_ref[:, second] = link

    @pl.when(turn == 1)
    def _():
        odd(True, came_near)

    offset = offset_of(length)
    for at, two in ((3, came_far), (7, came_back)):

        @pl.when(offset == at)
        def _(two=two):
            odd(False, two)


def choose_kernel(length, *refs):
    out_ref = refs[4]
    offset = offset_of(length)
    for at, ref in zip((1, 3, 5, 7), refs[:4]):

        @pl.when(offset == at)
        def _(ref=ref):
            out_ref[...] = ref[...]


def lower_kernel(length, parity, state, fh, fl, rest, _diag, _cross, diag_ref, cross_ref, out, sh, sl, sems):
    width = rest.shape[0]
    ps = sym_rows(width)
    offset = offset_of(length)
    first, second = slice(0, width), slice(width, 2 * width)

    def hand_over():
        fetch(sems, (out.at[:, first], diag_ref.at[0]), (out.at[:, second], cross_ref.at[0]))

    if parity == 0:

        @pl.when(offset == group // 2)
        def _():
            out[:, first] = get_sym(state, ps, width)
            out[:, second] = get_full(state, 2 * ps, width)
            hand_over()

    @pl.when(jnp.logical_and(lax.rem(offset, 2) == parity, lax.rem(offset, group // 2) > 0))
    def _():
        ba = get_full(state, 2 * ps, width)
        for rows, columns, mat in (
            (first, first, get_sym(state, 0, width)),
            (second, first, ba),
            (first, second, ba.T),
            (second, second, get_sym(state, ps, width)),
        ):
            sh[rows, columns], sl[rows, columns] = parts_of(mat)
        eh, el = fh[first, :], fl[first, :]
        triple = lambda h, l, axis_at: jnp.concatenate([h, l, h], axis=axis_at)
        left = jnp.concatenate([eh, eh, el], axis=1)
        passed = jnp.dot(left, triple(sh[...], sl[...], 0), preferred_element_type=f32)
        high, low = parts_of(passed)
        left = jnp.concatenate([high, high, low], axis=1)
        whole = lax.dot_general(
            left, triple(fh[...], fl[...], 1), (((1,), (1,)), ((), ())), preferred_element_type=f32
        )
        out[...] = rest[...] + whole
        hand_over()


def sent(array, length, *moves):
    device = lambda position: (position - row_offset) % length
    pairs = [(device(p), device(p + by)) for by, wanted in moves for p in range(length) if wanted(p)]
    return lax.ppermute(array, axis, pairs)


def upper_levels(inverse, lowers, uppers, length):
    width = inverse.shape[0]
    place = (lax.axis_index(axis) + row_offset) % length
    product = functools.partial(jnp.dot, precision=lax.Precision.HIGHEST, preferred_element_type=f32)
    node_g, node_h = product(inverse, lowers), product(inverse, uppers)
    everywhere = lambda p: True
    zeros = jnp.zeros((width, width), f32)
    sigma = jnp.where(place == 0, inverse, zeros)
    low_own, high_own, cross = zeros, zeros, zeros
    stride = length // 2
    while stride >= group:
        from_low, owned_high = (sent(x, length, (stride, everywhere)) for x in (sigma, high_own))
        from_high, owned_low = (sent(x, length, (-stride, everywhere)) for x in (sigma, low_own))
        has_upper = place + stride < length
        sigma_high = jnp.where(has_upper, from_high, zeros)
        sigma_ba = jnp.where(has_upper, owned_high.T + owned_low, zeros)
        active = place % (2 * stride) == stride
        low = -(product(node_g, from_low) + product(node_h, sigma_ba))
        high = -(product(node_g, sigma_ba.T) + product(node_h, sigma_high))
        own = inverse - product(node_g, low.T) - product(node_h, high.T)
        sigma = jnp.where(active, own, sigma)
        low_own = jnp.where(active, low, zeros)
        high_own = jnp.where(active, high, zeros)
        cross = jnp.where(active, low, cross)
        stride //= 2
    newest = lambda p: p % (2 * group) == group
    below_aa, below_ba, below_bb = (sent(x, length, (group, newest)) for x in (sigma, high_own.T, sigma_high))
    return sigma, cross, tuple(
        jnp.where(active, *pair) for pair in ((from_low, below_aa), (low_own, below_ba), (sigma, below_bb))
    )


def body(inv_diag, low_coupling, up_coupling):
    width = inv_diag.shape[1]
    length = lax.axis_size(axis)
    span = 4 * group
    is_open = length == span
    ps, pf = sym_rows(width), full_rows(width)
    node_rows, state_rows = ps + 2 * pf, 2 * ps + pf
    rows_of = lambda rows: jax.ShapeDtypeStruct((rows, lanes), f32)
    square = (width, width)
    whole = jax.ShapeDtypeStruct((1,) + square, f32)
    vmem, anywhere = pl.BlockSpec(memory_space=pltpu.VMEM), pl.BlockSpec(memory_space=pl.ANY)
    room = lambda *shape, kind=f32: pltpu.VMEM(shape, kind)
    sems = pltpu.SemaphoreType.DMA((4,))
    run = lambda kernel, mib, **more: pl.pallas_call(
        kernel, compiler_params=pltpu.CompilerParams(vmem_limit_bytes=mib * 2**20),
        cost_estimate=pl.CostEstimate(flops=1, bytes_accessed=1, transcendentals=0), **more
    )
    at = lambda turn: (lambda p: p % span == turn)
    inner = lambda offset: (lambda p: p % group == offset)
    mid, half = 2 * group, group // 2

    sym, part, node = run(
        own_kernel, 60, out_shape=(rows_of(ps), rows_of(ps + pf), rows_of(node_rows)),
        in_specs=[anywhere] * 3, out_specs=[vmem] * 3,
        scratch_shapes=[room(3, *square), sems], name="own",
    )(inv_diag, low_coupling, up_coupling)

    close = ((-1, inner(2)), (-1, inner(6)))
    if is_open:
        root_mid = sent(sym, length, (mid, at(0)))
        came_part = sent(part, length, (-group, at(mid)))
        root_low = sent(sym, length, (group, at(0)))
        came_near = sent(node, length, (group, at(group)), (group, at(3 * group)), *close)
    else:
        came_near = sent(node, length, *close)
    came_far = sent(node, length, (half, inner(half)), (1, inner(2)), (4, inner(6)))
    came_back = sent(came_far, length, (-3, inner(2)))

    if is_open:
        ahead, mid_sym = run(
            functools.partial(ahead_kernel, length), 16,
            out_shape=(jax.ShapeDtypeStruct((2,) + square, f32), rows_of(ps)),
            in_specs=[vmem] * 3, out_specs=[vmem] * 2, name="ahead",
        )(node, came_part, root_mid)
        mid_high = sent(mid_sym, length, (group, at(mid)))
        mid_zero = sent(mid_sym, length, (mid, at(mid)))
        diag, cross, low_half, high_half = run(
            functools.partial(upper_kernel, length), 16,
            out_shape=(whole, whole, rows_of(state_rows), rows_of(state_rows)),
            in_specs=[vmem] * 8, out_specs=[vmem] * 4,
            scratch_shapes=[room(*square)] * 3, name="upper",
        )(ahead, root_mid, root_low, mid_high, mid_zero, node, came_near, came_far)
    else:
        diag, cross, below = upper_levels(inv_diag[0], low_coupling[0], up_coupling[0], length)
        diag, cross = diag[None], cross[None]
        low_half, high_half = run(
            halve_kernel, 16, out_shape=(rows_of(state_rows),) * 2,
            in_specs=[vmem] * 4, out_specs=[vmem] * 2, name="halve",
        )(came_far, *below)

    to_five = sent(high_half, length, (-3, inner(0)))
    to_three = sent(low_half, length, (-5, inner(0)))
    to_one = sent(low_half, length, (-7, inner(0)))
    to_seven = sent(high_half, length, (-1, inner(0)))

    f_high, f_low, rest = run(
        functools.partial(near_kernel, length), 16,
        out_shape=(jax.ShapeDtypeStruct((2 * width, 2 * width), bf16),) * 2
        + (jax.ShapeDtypeStruct((width, 2 * width), f32),),
        in_specs=[vmem] * 4, out_specs=[vmem] * 3, name="near",
    )(node, came_near, came_far, came_back)

    state = run(
        functools.partial(choose_kernel, length), 16,
        out_shape=rows_of(state_rows), in_specs=[vmem] * 4, out_specs=vmem, name="choose",
    )(to_one, to_three, to_five, to_seven)
    state_next = sent(state, length, (1, inner(1)), (1, inner(3)), (1, inner(5)))

    for parity, came in ((1, state), (0, state_next)):
        diag, cross = run(
            functools.partial(lower_kernel, length, parity), 20,
            out_shape=(whole, whole), in_specs=[vmem] * 4 + [anywhere] * 2, out_specs=[anywhere] * 2,
            scratch_shapes=[room(width, 2 * width)]
            + [room(2 * width, 2 * width, kind=bf16)] * 2
            + [sems],
            input_output_aliases={4: 0, 5: 1},
            name="lower",
        )(came, f_high, f_low, rest, diag, cross)
    return diag, cross


def solution(mesh):
    placed = (P(axis, None, None),) * 3
    return jax.shard_map(
        body, mesh=mesh, in_specs=placed, out_specs=placed[:2], check_vma=False
    )
```

time: 292 us -> 85.9 us (0.29)
  the two profiles are of different devices: /device:TPU:4 before, /device:TPU:18 now
where the time goes in v2:
time: 85.9 us; the launch traced here: 85.6 us
  waiting for transfers between devices  58.8 us (68%)
  Pallas kernels  13.1 us (15%)
  starting transfers between devices  11.2 us (13%)
  local copies, waits for them, and re-layouts  1.38 us (2%)
  between operations  1.06 us (1%)
    ppermute x13, waiting for transfers between devices, sent(): return lax.ppermute(array, axis, pairs)  58.8 us
    ppermute x13, starting transfers between devices, sent(): return lax.ppermute(array, axis, pairs)  11.2 us
    pallas_call x2, Pallas kernels, body(): run(functools.partial(lower_kernel, length, parity), 20, out_shape=(whole...  4.98 us
    pallas_call x1, Pallas kernels, body(): run(own_kernel, 60, out_shape=(rows_of(ps), rows_of(ps + pf), rows_of(nod...  3.93 us
    pallas_call x1, Pallas kernels, body(): run(functools.partial(near_kernel, length), 16, out_shape=(jax.ShapeDtype...  3.09 us
  transfers between devices with their start and end apart: 13, of which 2 were waited for; matrix products, arithmetic and copies ran while one was open for 0% of the time, Pallas kernels for 9%

profile of v2, /device:TPU:18, one launch (start us, length us, event | category | flops | bytes accessed | tf_op | source)
XLA Modules:
  0.0 85.6 jit_solution(8252634837972596671)
XLA Ops:
  0.6 3.9 %own.1 = (f32[648,128]{1,0:T(8,128)}, f32[1800,128]{1,0:T(8,128)}, f32[2952,128]{1,0:T(8,128)}) custom-call(f32[1,384,384]{2,1,0:T(8,128)} %inv_ref.1, f32[1,384,384]{2,1,0:T(8,128)} %low_ref.1, f32[1,384,384]{2,1,0:T(8,128)} %up_ref.1), custom_call_target="tpu_custom_call" | custom-call | flops 1 | bytes 1 | tf_op jit(solution)/shard_map/own/pallas_call | solution.py:406
  4.6 0.8 collective-permute-start.6
  5.3 1.3 %collective-permute-start.5 = (f32[2952,128]{1,0:T(8,128)}, f32[2952,128]{1,0:T(8,128)S(1)}, u32[]{:S(2)}, u32[]{:S(2)}) collective-permute-start(f32[2952,128]{1,0:T(8,128)} %get-tuple-element.16.node), channel_id=1, source_target_pairs={{5,13},{21,29},{31,30},{7,6},{15,14},{23,22},{3,2},{11,10},{19,18}... | collective-permute-start | bytes 4534280 | tf_op jit(solution)/shard_map/ppermute | solution.py:350
  6.6 0.7 collective-permute-start
  7.4 0.7 collective-permute-start.1
  8.1 0.7 collective-permute-start.2
  8.7 0.0 collective-permute-done.1.came_root.root_mid
  8.8 0.0 collective-permute-done.came_part
  8.8 1.4 %copy-done = f32[2952,128]{1,0:T(8,128)S(1)} copy-done((f32[2952,128]{1,0:T(8,128)S(1)}, f32[2952,128]{1,0:T(8,128)}, u32[]{:S(2)}) %copy-start) | copy-done | bytes 1511448
  10.2 0.7 collective-permute-start.3
  10.8 0.7 collective-permute-start.4
  11.5 0.0 collective-permute-done.2.root_low
  11.5 0.0 collective-permute-done.3.mid_high
  11.5 0.0 collective-permute-done.4.mid_zero
  11.6 0.0 collective-permute-done.6.came_four.came_far
  11.6 0.4 collective-permute-done.5.came_node.came_near
  12.0 1.0 %upper.1 = (f32[1,384,384]{2,1,0:T(8,128)}, f32[1,384,384]{2,1,0:T(8,128)}, f32[2448,128]{1,0:T(8,128)S(1)}, f32[2448,128]{1,0:T(8,128)S(1)}) custom-call(f32[2,384,384]{2,1,0:T(8,128)S(1)} %get-tuple-element.19.ahead, f32[648,128]{1,0:T(8,128)S(1)} %collective-permute-done.1.came_root.root_mid, f32[648,128]{1,0:T(8,128)S(1)} %collective-permute-done.2.root_low, ...), custom_call_target="tpu_custom_call" | custom-call | flops 1 | bytes 1 | tf_op jit(solution)/shard_map/upper/pallas_call | solution.py:431
  13.0 0.7 collective-permute-start.10
  13.7 0.9 %collective-permute-start.7 = (f32[2448,128]{1,0:T(8,128)S(1)}, f32[2448,128]{1,0:T(8,128)S(1)}, u32[]{:S(2)}, u32[]{:S(2)}) collective-permute-start(f32[2448,128]{1,0:T(8,128)S(1)} %get-tuple-element.21), channel_id=1, source_target_pairs={{29,22},{5,30},{13,6},{21,14}} | collective-permute-start | bytes 3760136 | tf_op jit(solution)/shard_map/ppermute | solution.py:350
  14.6 0.7 collective-permute-start.8
  15.3 1.3 %collective-permute-start.9 = (f32[2448,128]{1,0:T(8,128)S(1)}, f32[2448,128]{1,0:T(8,128)S(1)}, u32[]{:S(2)}, u32[]{:S(2)}) collective-permute-start(f32[2448,128]{1,0:T(8,128)S(1)} %get-tuple-element.22), channel_id=1, source_target_pairs={{29,26},{5,2},{13,10},{21,18}} | collective-permute-start | bytes 3760136 | tf_op jit(solution)/shard_map/ppermute | solution.py:350
  16.6 0.8 collective-permute-start.12
  17.4 0.0 collective-permute-done.10.refs_3_
  17.4 0.0 collective-permute-done.7.refs_0_
  17.4 0.0 collective-permute-done.8.refs_1_
  17.4 58.4 %collective-permute-done.9.refs_2_ = f32[2448,128]{1,0:T(8,128)S(1)} collective-permute-done((f32[2448,128]{1,0:T(8,128)S(1)}, f32[2448,128]{1,0:T(8,128)S(1)}, u32[]{:S(2)}, u32[]{:S(2)}) %collective-permute-start.9) | collective-permute-done | bytes 1253408 | tf_op jit(solution)/shard_map/ppermute | solution.py:350
  75.8 0.1 choose.1.state
  75.9 1.4 %collective-permute-start.11 = (f32[2448,128]{1,0:T(8,128)S(1)}, f32[2448,128]{1,0:T(8,128)S(1)}, u32[]{:S(2)}, u32[]{:S(2)}) collective-permute-start(f32[2448,128]{1,0:T(8,128)S(1)} %choose.1.state), channel_id=1, source_target_pairs={{30,31},{6,7},{14,15},{22,23},{0,1},{8,9},{16,17},{24,25},{2,3},{1... | collective-permute-start | bytes 3760136 | tf_op jit(solution)/shard_map/ppermute | solution.py:350
  77.3 0.0 collective-permute-done.12.came_back
  77.3 3.1 %near.1 = (bf16[768,768]{1,0:T(8,128)(2,1)S(1)}, bf16[768,768]{1,0:T(8,128)(2,1)S(1)}, f32[384,768]{1,0:T(8,128)S(1)}) custom-call(f32[2952,128]{1,0:T(8,128)S(1)} %copy-done.1, f32[2952,128]{1,0:T(8,128)S(1)} %collective-permute-done.5.came_node.came_near, f32[2952,128]{1,0:T(8,128)S(1)} %collective-permute-done.6.came_four.came_far, ...), custom_call_target="tpu_custom_call" | custom-call | flops 1 | bytes 1 | tf_op jit(solution)/shard_map/near/pallas_call | solution.py:450
  80.4 4.9 %lower.2 = (f32[1,384,384]{2,1,0:T(8,128)}, f32[1,384,384]{2,1,0:T(8,128)}) custom-call(f32[2448,128]{1,0:T(8,128)S(1)} %choose.1.state, bf16[768,768]{1,0:T(8,128)(2,1)S(1)} %get-tuple-element.23.fh, bf16[768,768]{1,0:T(8,128)(2,1)S(1)} %get-tuple-element.24.fl, ...), custom_call_target="tpu_custom_call", output_to_operand_aliasing={{0}: (4, {}), {1}: (5, {})} | custom-call | flops 1 | bytes 1 | tf_op jit(solution)/shard_map/lower/pallas_call | solution.py:464
  85.3 0.1 lower.3
  (5 shorter events, 0.0 us)
Async XLA Ops:
  4.6 7.0 %collective-permute-start.6 = (f32[2952,128]{1,0:T(8,128)}, f32[2952,128]{1,0:T(8,128)S(1)}, u32[]{:S(2)}, u32[]{:S(2)}) collective-permute-start(f32[2952,128]{1,0:T(8,128)} %get-tuple-element.16.node), channel_id=1, source_target_pairs={{1,5},{9,13},{17,21},{25,29},{31,0},{7,8},{15,16},{23,24},{3,7},{1... | collective-permute-start | bytes 4534280 | tf_op jit(solution)/shard_map/ppermute | solution.py:350
  5.3 6.6 %collective-permute-start.5 = (f32[2952,128]{1,0:T(8,128)}, f32[2952,128]{1,0:T(8,128)S(1)}, u32[]{:S(2)}, u32[]{:S(2)}) collective-permute-start(f32[2952,128]{1,0:T(8,128)} %get-tuple-element.16.node), channel_id=1, source_target_pairs={{5,13},{21,29},{31,30},{7,6},{15,14},{23,22},{3,2},{11,10},{19,18}... | collective-permute-start | bytes 4534280 | tf_op jit(solution)/shard_map/ppermute | solution.py:350
  6.6 2.1 %collective-permute-start = (f32[1800,128]{1,0:T(8,128)}, f32[1800,128]{1,0:T(8,128)S(1)}, u32[]{:S(2)}, u32[]{:S(2)}) collective-permute-start(f32[1800,128]{1,0:T(8,128)} %get-tuple-element.17), channel_id=1, source_target_pairs={{13,5}} | collective-permute-start | bytes 2764808 | tf_op jit(solution)/shard_map/ppermute | solution.py:350
  7.4 1.4 %collective-permute-start.1 = (f32[648,128]{1,0:T(8,128)}, f32[648,128]{1,0:T(8,128)S(1)}, u32[]{:S(2)}, u32[]{:S(2)}) collective-permute-start(f32[648,128]{1,0:T(8,128)} %get-tuple-element.18), channel_id=1, source_target_pairs={{29,13}} | collective-permute-start | bytes 995336 | tf_op jit(solution)/shard_map/ppermute | solution.py:350
  8.1 3.5 %collective-permute-start.2 = (f32[648,128]{1,0:T(8,128)}, f32[648,128]{1,0:T(8,128)S(1)}, u32[]{:S(2)}, u32[]{:S(2)}) collective-permute-start(f32[648,128]{1,0:T(8,128)} %get-tuple-element.18), channel_id=1, source_target_pairs={{29,5}} | collective-permute-start | bytes 995336 | tf_op jit(solution)/shard_map/ppermute | solution.py:350
  8.8 1.4 %copy-start = (f32[2952,128]{1,0:T(8,128)S(1)}, f32[2952,128]{1,0:T(8,128)}, u32[]{:S(2)}) copy-start(f32[2952,128]{1,0:T(8,128)} %get-tuple-element.16.node) | copy-start | bytes 4534276
  10.2 1.4 %collective-permute-start.3 = (f32[648,128]{1,0:T(8,128)S(1)}, f32[648,128]{1,0:T(8,128)S(1)}, u32[]{:S(2)}, u32[]{:S(2)}) collective-permute-start(f32[648,128]{1,0:T(8,128)S(1)} %get-tuple-element.20), channel_id=1, source_target_pairs={{13,21}} | collective-permute-start | bytes 995336 | tf_op jit(solution)/shard_map/ppermute | solution.py:350
  10.8 0.7 collective-permute-start.4
  13.0 4.4 %collective-permute-start.10 = (f32[2448,128]{1,0:T(8,128)S(1)}, f32[2448,128]{1,0:T(8,128)S(1)}, u32[]{:S(2)}, u32[]{:S(2)}) collective-permute-start(f32[2448,128]{1,0:T(8,128)S(1)} %get-tuple-element.22), channel_id=1, source_target_pairs={{29,28},{5,4},{13,12},{21,20}} | collective-permute-start | bytes 3760136 | tf_op jit(solution)/shard_map/ppermute | solution.py:350
  13.7 63.6 %copy-start.1 = (f32[2952,128]{1,0:T(8,128)S(1)}, f32[2952,128]{1,0:T(8,128)}, u32[]{:S(2)}) copy-start(f32[2952,128]{1,0:T(8,128)} %get-tuple-element.16.node) | copy-start | bytes 4534276
  13.7 3.7 %collective-permute-start.7 = (f32[2448,128]{1,0:T(8,128)S(1)}, f32[2448,128]{1,0:T(8,128)S(1)}, u32[]{:S(2)}, u32[]{:S(2)}) collective-permute-start(f32[2448,128]{1,0:T(8,128)S(1)} %get-tuple-element.21), channel_id=1, source_target_pairs={{29,22},{5,30},{13,6},{21,14}} | collective-permute-start | bytes 3760136 | tf_op jit(solution)/shard_map/ppermute | solution.py:350
  14.6 2.8 %collective-permute-start.8 = (f32[2448,128]{1,0:T(8,128)S(1)}, f32[2448,128]{1,0:T(8,128)S(1)}, u32[]{:S(2)}, u32[]{:S(2)}) collective-permute-start(f32[2448,128]{1,0:T(8,128)S(1)} %get-tuple-element.21), channel_id=1, source_target_pairs={{29,24},{5,0},{13,8},{21,16}} | collective-permute-start | bytes 3760136 | tf_op jit(solution)/shard_map/ppermute | solution.py:350
  15.3 60.5 %collective-permute-start.9 = (f32[2448,128]{1,0:T(8,128)S(1)}, f32[2448,128]{1,0:T(8,128)S(1)}, u32[]{:S(2)}, u32[]{:S(2)}) collective-permute-start(f32[2448,128]{1,0:T(8,128)S(1)} %get-tuple-element.22), channel_id=1, source_target_pairs={{29,26},{5,2},{13,10},{21,18}} | collective-permute-start | bytes 3760136 | tf_op jit(solution)/shard_map/ppermute | solution.py:350
  16.6 60.7 %collective-permute-start.12 = (f32[2952,128]{1,0:T(8,128)S(1)}, f32[2952,128]{1,0:T(8,128)S(1)}, u32[]{:S(2)}, u32[]{:S(2)}) collective-permute-start(f32[2952,128]{1,0:T(8,128)S(1)} %collective-permute-done.6.came_four.came_far), channel_id=1, source_target_pairs={{31,28},{7,4},{15,12},{23,20}} | collective-permute-start | bytes 4534280 | tf_op jit(solution)/shard_map/ppermute | solution.py:350
  75.9 9.4 %collective-permute-start.11 = (f32[2448,128]{1,0:T(8,128)S(1)}, f32[2448,128]{1,0:T(8,128)S(1)}, u32[]{:S(2)}, u32[]{:S(2)}) collective-permute-start(f32[2448,128]{1,0:T(8,128)S(1)} %choose.1.state), channel_id=1, source_target_pairs={{30,31},{6,7},{14,15},{22,23},{0,1},{8,9},{16,17},{24,25},{2,3},{1... | collective-permute-start | bytes 3760136 | tf_op jit(solution)/shard_map/ppermute | solution.py:350

commit v3 on v2

--- a/solution.py
+++ b/solution.py
@@ -97,6 +97,45 @@
     return dot(left[0], right[0]) + (dot(left[0], right[1]) + dot(left[1], right[0]))
 
 
+def long_left(parts):
+    high, low = parts
+    return jnp.concatenate([high, high, low], axis=1)
+
+
+def long_right(parts, turned=False):
+    high, low = parts
+    return jnp.concatenate([high, low, high], axis=1 if turned else 0)
+
+
+def long_times(left, right, turned=False):
+    dims = (((1,), (1 if turned else 0,)), ((), ()))
+    return lax.dot_general(left, right, dims, preferred_element_type=f32)
+
+
+def symmetric_times(left, right):
+    width = left.shape[0]
+    most = width // (2 * lanes) * (2 * lanes)
+    wide = long_times(left, right[:most], True)
+    if most == width:
+        return wide
+    rest = long_times(left[most:], right[most:], True)
+    return jnp.concatenate([wide, jnp.concatenate([wide[most:].T, rest], axis=0)], axis=1)
+
+
+def set_state(sh, sl, aa, ba, bb):
+    width = aa.shape[0]
+    first, second = slice(0, width), slice(width, 2 * width)
+    for rows, columns, mat in ((first, first, aa), (second, first, ba), (first, second, ba.T), (second, second, bb)):
+        sh[rows, columns], sl[rows, columns] = parts_of(mat)
+
+
+def eliminate(node, sh, sl):
+    diag, g_mat, h_mat = node
+    left = long_left(parts_of(jnp.concatenate([g_mat, h_mat], axis=1)))
+    passed = -long_times(left, long_right((sh[...], sl[...])))
+    return passed, diag - symmetric_times(left, long_right(parts_of(passed), True))
+
+
 def place_now(length):
     return lax.rem(lax.axis_index(axis) + row_offset, length)
 
@@ -139,10 +178,29 @@
     return place == 0, place == group, place == 2 * group, place == 3 * group
 
 
-def ahead_kernel(length, node, came_part, came_root, out, sym_ref):
+def mid_kernel(length, part, came_root, out, sym_ref):
     width = out.shape[1]
     ps = sym_rows(width)
-    _, at_low, at_mid, _ = roles_of(length)
+    _, _, at_mid, _ = roles_of(length)
+
+    @pl.when(jnp.logical_not(at_mid))
+    def _():
+        sym_ref[...] = part[pl.ds(0, ps), :]
+
+    @pl.when(at_mid)
+    def _():
+        own_parts = parts_of(get_full(part, ps, width))
+        cross = -times(own_parts, parts_of(get_sym(came_root, 0, width)))
+        own = get_sym(part, 0, width) - times(own_parts, parts_of(cross), True)
+        put_sym(sym_ref, 0, own)
+        out[0] = cross
+        out[1] = own
+
+
+def low_kernel(length, node, came_part, _after, out):
+    width = out.shape[1]
+    ps = sym_rows(width)
+    _, at_low, _, _ = roles_of(length)
 
     @pl.when(at_low)
     def _():
@@ -152,62 +210,46 @@
         passed = times(h_parts, parts_of(get_sym(came_part, 0, width)))
         out[1] = own_d + times(parts_of(passed), h_parts, True)
 
-    @pl.when(at_mid)
-    def _():
-        own_d, own_g, _ = get_node(node, width)
-        own_parts = parts_of(own_g)
-        cross = -times(own_parts, parts_of(get_sym(came_root, 0, width)))
-        own = own_d - times(own_parts, parts_of(cross), True)
-        put_sym(sym_ref, 0, own)
-        out[0] = cross
-        out[1] = own
-
-
-def halve(four, state, low_ref, high_ref):
-    aa, ba, bb = state
-    width = aa.shape[0]
-    diag, g_mat, h_mat = get_node(four, width)
-    g_parts, h_parts = parts_of(g_mat), parts_of(h_mat)
-    ba_parts = parts_of(ba)
-    low = -(times(g_parts, parts_of(aa)) + times(h_parts, ba_parts))
-    put_full(low_ref, 2 * sym_rows(width), low)
-    high = -(times(g_parts, ba_parts, True) + times(h_parts, parts_of(bb)))
-    put_full(high_ref, 2 * sym_rows(width), high.T)
-    own = diag - times(g_parts, parts_of(low), True) - times(h_parts, parts_of(high), True)
+
+def halve(four, sh, sl, low_ref, low_cross_ref, high_ref):
+    width = sh.shape[0] // 2
     ps = sym_rows(width)
-    put_sym(low_ref, 0, aa)
+    passed, own = eliminate(get_node(four, width), sh, sl)
+    put_full(low_cross_ref, 0, passed[:, :width])
+    put_full(high_ref, 2 * ps, passed[:, width:].T)
     put_sym(low_ref, ps, own)
     high_ref[pl.ds(0, ps), :] = low_ref[pl.ds(ps, ps), :]
-    put_sym(high_ref, ps, bb)
 
 
 def upper_kernel(
-    length, ahead, root_mid, root_low, mid_high, mid_zero, node, came_node, came_four,
-    diag_ref, cross_ref, low_ref, high_ref, aa_ref, ba_ref, bb_ref,
+    length, at_m, at_l, root_mid, came_sym, mid_zero, node, came_node, came_four,
+    diag_ref, cross_ref, low_ref, low_cross_ref, high_ref, sh, sl,
 ):
-    width = aa_ref.shape[0]
+    width = diag_ref.shape[1]
+    ps = sym_rows(width)
     at_zero, at_low, at_mid, at_high = roles_of(length)
+    low_end, high_end = pl.ds(0, ps), pl.ds(ps, ps)
 
     @pl.when(at_low)
     def _():
-        root = get_sym(root_low, 0, width)
-        passed = parts_of(ahead[0])
+        root = get_sym(came_sym, 0, width)
+        passed = parts_of(at_l[0])
         cross = times(passed, parts_of(root))
-        own = ahead[1] + times(parts_of(cross), passed, True)
+        own = at_l[1] + symmetric_times(long_left(parts_of(cross)), long_right(passed, True))
         diag_ref[0], cross_ref[0] = own, cross
-        aa_ref[...], ba_ref[...], bb_ref[...] = root, cross, own
+        low_ref[low_end, :] = came_sym[...]
+        put_sym(high_ref, ps, own)
+        set_state(sh, sl, root, cross, own)
 
     @pl.when(at_mid)
     def _():
-        mid_cross, mid = ahead[0], ahead[1]
+        mid_cross, mid = at_m[0], at_m[1]
         diag_ref[0], cross_ref[0] = mid, mid_cross
-        low_d, low_g, low_h = get_node(came_node, width)
-        low_g, low_h = parts_of(low_g), parts_of(low_h)
-        cross_parts = parts_of(mid_cross)
-        part_low = -(times(low_g, parts_of(get_sym(root_mid, 0, width))) + times(low_h, cross_parts))
-        part_high = -(times(low_g, cross_parts, True) + times(low_h, parts_of(mid)))
-        own = low_d - times(low_g, parts_of(part_low), True) - times(low_h, parts_of(part_high), True)
-        aa_ref[...], ba_ref[...], bb_ref[...] = own, part_high.T, mid
+        set_state(sh, sl, get_sym(root_mid, 0, width), mid_cross, mid)
+        passed, own = eliminate(get_node(came_node, width), sh, sl)
+        put_sym(low_ref, 0, own)
+        put_sym(high_ref, ps, mid)
+        set_state(sh, sl, own, passed[:, width:].T, mid)
 
     def above(mid_ref, node_ref):
         own_d, own_g, _ = get_node(node_ref, width)
@@ -218,24 +260,32 @@
 
     @pl.when(at_high)
     def _():
-        mid, cross, own = above(mid_high, node)
+        mid, cross, own = above(came_sym, node)
         diag_ref[0], cross_ref[0] = own, cross
-        aa_ref[...], ba_ref[...], bb_ref[...] = mid, cross, own
+        low_ref[low_end, :] = came_sym[...]
+        put_sym(high_ref, ps, own)
+        set_state(sh, sl, mid, cross, own)
 
     @pl.when(at_zero)
     def _():
         _, _, own = above(mid_zero, came_node)
         zeros = jnp.zeros((width, width), f32)
         diag_ref[0], cross_ref[0] = get_sym(node, 0, width), zeros
-        aa_ref[...], ba_ref[...], bb_ref[...] = own, zeros, zeros
+        put_sym(low_ref, 0, own)
+        high_ref[high_end, :] = jnp.zeros((ps, lanes), f32)
+        set_state(sh, sl, own, zeros, zeros)
 
     @pl.when(lax.rem(place_now(length), group) == 0)
     def _():
-        halve(came_four, (aa_ref[...], ba_ref[...], bb_ref[...]), low_ref, high_ref)
-
-
-def halve_kernel(came_four, aa_ref, ba_ref, bb_ref, low_ref, high_ref):
-    halve(came_four, (aa_ref[...], ba_ref[...], bb_ref[...]), low_ref, high_ref)
+        halve(came_four, sh, sl, low_ref, low_cross_ref, high_ref)
+
+
+def halve_kernel(came_four, aa_ref, ba_ref, bb_ref, low_ref, low_cross_ref, high_ref, sh, sl):
+    aa, bb = aa_ref[...], bb_ref[...]
+    put_sym(low_ref, 0, aa)
+    put_sym(high_ref, sym_rows(aa.shape[0]), bb)
+    set_state(sh, sl, aa, ba_ref[...], bb)
+    halve(came_four, sh, sl, low_ref, low_cross_ref, high_ref)
 
 
 def offset_of(length):
@@ -250,20 +300,12 @@
     def put(rows, columns, mat):
         f_high[rows, columns], f_low[rows, columns] = parts_of(mat)
 
-    def put_unit():
-        r = lax.broadcasted_iota(jnp.int32, (width, 2 * width), 0)
-        c = lax.broadcasted_iota(jnp.int32, (width, 2 * width), 1)
-        f_high[second, :] = jnp.where(r == c, 1.0, 0.0).astype(bf16)
-        f_low[second, :] = jnp.zeros((width, 2 * width), bf16)
-        rest_ref[:, second] = jnp.zeros((width, width), f32)
-
     @pl.when(turn == 2)
     def _():
         d_own, g_own, h_own = get_node(node, width)
         put(first, first, -g_own)
         put(first, second, -h_own)
         rest_ref[:, first] = d_own
-        put_unit()
 
     def odd(below, two):
         d_own, g_own, h_own = get_node(node, width)
@@ -275,9 +317,7 @@
         put(first, second, to_high if below else to_high - outward)
         link = -times(inward, parts_of(d_two))
         rest_ref[:, first] = d_own - times(inward, parts_of(link), True)
-        if below:
-            put_unit()
-        else:
+        if not below:
             put(second, first, -g_two)
             put(second, second, -h_two)
             rest_ref[:, second] = link
@@ -294,54 +334,70 @@
             odd(False, two)
 
 
-def choose_kernel(length, *refs):
-    out_ref = refs[4]
+def choose_kernel(length, one, one_cross, three, three_cross, five, seven, _after, out_ref):
     offset = offset_of(length)
-    for at, ref in zip((1, 3, 5, 7), refs[:4]):
+    for at, ends, cross in ((1, one, one_cross), (3, three, three_cross)):
+
+        @pl.when(offset == at)
+        def _(ends=ends, cross=cross):
+            rows = ends.shape[0]
+            out_ref[pl.ds(0, rows), :] = ends[...]
+            out_ref[pl.ds(rows, cross.shape[0]), :] = cross[...]
+
+    for at, ref in ((5, five), (7, seven)):
 
         @pl.when(offset == at)
         def _(ref=ref):
             out_ref[...] = ref[...]
 
 
-def lower_kernel(length, parity, state, fh, fl, rest, _diag, _cross, diag_ref, cross_ref, out, sh, sl, sems):
+def lower_kernel(length, parity, state, fh, fl, rest, _diag, _cross, diag_ref, cross_ref, diag_out, cross_out, sh, sl, sems):
     width = rest.shape[0]
     ps = sym_rows(width)
     offset = offset_of(length)
+    turn = lax.rem(offset, group // 2)
     first, second = slice(0, width), slice(width, 2 * width)
-
-    def hand_over():
-        fetch(sems, (out.at[:, first], diag_ref.at[0]), (out.at[:, second], cross_ref.at[0]))
+    diag_copy = pltpu.make_async_copy(diag_out, diag_ref.at[0], sems.at[0])
+    cross_copy = pltpu.make_async_copy(cross_out, cross_ref.at[0], sems.at[1])
+
+    def passed_on():
+        set_state(sh, sl, get_sym(state, 0, width), get_full(state, 2 * ps, width), get_sym(state, ps, width))
+        left = long_left((fh[first, :], fl[first, :]))
+        return long_times(left, long_right((sh[...], sl[...])))
 
     if parity == 0:
 
         @pl.when(offset == group // 2)
         def _():
-            out[:, first] = get_sym(state, ps, width)
-            out[:, second] = get_full(state, 2 * ps, width)
-            hand_over()
-
-    @pl.when(jnp.logical_and(lax.rem(offset, 2) == parity, lax.rem(offset, group // 2) > 0))
-    def _():
-        ba = get_full(state, 2 * ps, width)
-        for rows, columns, mat in (
-            (first, first, get_sym(state, 0, width)),
-            (second, first, ba),
-            (first, second, ba.T),
-            (second, second, get_sym(state, ps, width)),
-        ):
-            sh[rows, columns], sl[rows, columns] = parts_of(mat)
-        eh, el = fh[first, :], fl[first, :]
-        triple = lambda h, l, axis_at: jnp.concatenate([h, l, h], axis=axis_at)
-        left = jnp.concatenate([eh, eh, el], axis=1)
-        passed = jnp.dot(left, triple(sh[...], sl[...], 0), preferred_element_type=f32)
-        high, low = parts_of(passed)
-        left = jnp.concatenate([high, high, low], axis=1)
-        whole = lax.dot_general(
-            left, triple(fh[...], fl[...], 1), (((1,), (1,)), ((), ())), preferred_element_type=f32
-        )
-        out[...] = rest[...] + whole
-        hand_over()
+            cross_out[...] = get_full(state, 2 * ps, width)
+            cross_copy.start()
+            diag_out[...] = get_sym(state, ps, width)
+            diag_copy.start()
+            diag_copy.wait()
+            cross_copy.wait()
+
+    @pl.when(turn == (1 if parity else 2))
+    def _():
+        passed = passed_on()
+        cross_out[...] = passed[:, first]
+        cross_copy.start()
+        right = long_right((fh[first, :], fl[first, :]), True)
+        diag_out[...] = rest[:, first] + symmetric_times(long_left(parts_of(passed)), right)
+        diag_copy.start()
+        diag_copy.wait()
+        cross_copy.wait()
+
+    if parity == 1:
+
+        @pl.when(turn == 3)
+        def _():
+            left = long_left(parts_of(passed_on()))
+            whole = long_times(left, long_right((fh[...], fl[...]), True), True) + rest[...]
+            diag_out[...], cross_out[...] = whole[:, first], whole[:, second]
+            diag_copy.start()
+            cross_copy.start()
+            diag_copy.wait()
+            cross_copy.wait()
 
 
 def sent(array, length, *moves):
@@ -410,42 +466,49 @@
     )(inv_diag, low_coupling, up_coupling)
 
     close = ((-1, inner(2)), (-1, inner(6)))
+    came_far = sent(node, length, (half, inner(half)), (1, inner(2)), (4, inner(6)))
     if is_open:
+        came_near = sent(node, length, (group, at(group)), (group, at(3 * group)), *close)
+        came_part = sent(part, length, (-group, at(mid)))
         root_mid = sent(sym, length, (mid, at(0)))
-        came_part = sent(part, length, (-group, at(mid)))
-        root_low = sent(sym, length, (group, at(0)))
-        came_near = sent(node, length, (group, at(group)), (group, at(3 * group)), *close)
     else:
         came_near = sent(node, length, *close)
-    came_far = sent(node, length, (half, inner(half)), (1, inner(2)), (4, inner(6)))
-    came_back = sent(came_far, length, (-3, inner(2)))
-
+
+    state_room = [room(2 * width, 2 * width, kind=bf16)] * 2
+    two = jax.ShapeDtypeStruct((2,) + square, f32)
     if is_open:
-        ahead, mid_sym = run(
-            functools.partial(ahead_kernel, length), 16,
-            out_shape=(jax.ShapeDtypeStruct((2,) + square, f32), rows_of(ps)),
-            in_specs=[vmem] * 3, out_specs=[vmem] * 2, name="ahead",
-        )(node, came_part, root_mid)
-        mid_high = sent(mid_sym, length, (group, at(mid)))
+        at_m, mid_sym = run(
+            functools.partial(mid_kernel, length), 16, out_shape=(two, rows_of(ps)),
+            in_specs=[vmem] * 2, out_specs=[vmem] * 2, name="middle",
+        )(part, root_mid)
+        came_sym = sent(mid_sym, length, (group, at(mid)), (group, at(0)))
         mid_zero = sent(mid_sym, length, (mid, at(mid)))
-        diag, cross, low_half, high_half = run(
+        at_l = run(
+            functools.partial(low_kernel, length), 16, out_shape=two,
+            in_specs=[vmem] * 2 + [anywhere], out_specs=vmem, name="low",
+        )(node, came_part, mid_sym)
+        later, *_ = lax.optimization_barrier((came_far, at_l, came_sym, mid_zero))
+        diag, cross, low_half, low_cross, high_half = run(
             functools.partial(upper_kernel, length), 16,
-            out_shape=(whole, whole, rows_of(state_rows), rows_of(state_rows)),
-            in_specs=[vmem] * 8, out_specs=[vmem] * 4,
-            scratch_shapes=[room(*square)] * 3, name="upper",
-        )(ahead, root_mid, root_low, mid_high, mid_zero, node, came_near, came_far)
+            out_shape=(whole, whole, rows_of(2 * ps), rows_of(pf), rows_of(state_rows)),
+            in_specs=[vmem] * 8, out_specs=[vmem] * 5, scratch_shapes=state_room, name="upper",
+        )(at_m, at_l, root_mid, came_sym, mid_zero, node, came_near, came_far)
     else:
         diag, cross, below = upper_levels(inv_diag[0], low_coupling[0], up_coupling[0], length)
         diag, cross = diag[None], cross[None]
-        low_half, high_half = run(
-            halve_kernel, 16, out_shape=(rows_of(state_rows),) * 2,
-            in_specs=[vmem] * 4, out_specs=[vmem] * 2, name="halve",
+        later = came_far
+        low_half, low_cross, high_half = run(
+            halve_kernel, 16, out_shape=(rows_of(2 * ps), rows_of(pf), rows_of(state_rows)),
+            in_specs=[vmem] * 4, out_specs=[vmem] * 3, scratch_shapes=state_room, name="halve",
         )(came_far, *below)
 
+    came_back = sent(later, length, (-3, inner(2)))
+    three_cross = sent(low_cross, length, (-5, inner(0)))
     to_five = sent(high_half, length, (-3, inner(0)))
+    to_one = sent(low_half, length, (-7, inner(0)))
     to_three = sent(low_half, length, (-5, inner(0)))
-    to_one = sent(low_half, length, (-7, inner(0)))
     to_seven = sent(high_half, length, (-1, inner(0)))
+    one_cross = sent(three_cross, length, (-2, inner(3)))
 
     f_high, f_low, rest = run(
         functools.partial(near_kernel, length), 16,
@@ -456,17 +519,15 @@
 
     state = run(
         functools.partial(choose_kernel, length), 16,
-        out_shape=rows_of(state_rows), in_specs=[vmem] * 4, out_specs=vmem, name="choose",
-    )(to_one, to_three, to_five, to_seven)
+        out_shape=rows_of(state_rows), in_specs=[vmem] * 6 + [anywhere], out_specs=vmem, name="choose",
+    )(to_one, one_cross, to_three, three_cross, to_five, to_seven, rest)
     state_next = sent(state, length, (1, inner(1)), (1, inner(3)), (1, inner(5)))
 
     for parity, came in ((1, state), (0, state_next)):
         diag, cross = run(
             functools.partial(lower_kernel, length, parity), 20,
             out_shape=(whole, whole), in_specs=[vmem] * 4 + [anywhere] * 2, out_specs=[anywhere] * 2,
-            scratch_shapes=[room(width, 2 * width)]
-            + [room(2 * width, 2 * width, kind=bf16)] * 2
-            + [sems],
+            scratch_shapes=[room(*square)] * 2 + state_room + [sems],
             input_output_aliases={4: 0, 5: 1},
             name="lower",
         )(came, f_high, f_low, rest, diag, cross)

time: 85.9 us -> 75.7 us (0.88)
  the two profiles are of different devices: /device:TPU:18 before, /device:TPU:27 now
where the time goes in v3:
time: 75.7 us; the launch traced here: 75.3 us
  waiting for transfers between devices  48.1 us (64%)
  starting transfers between devices  13.7 us (18%)
  Pallas kernels  9.86 us (13%)
  local copies, waits for them, and re-layouts  2.55 us (3%)
  between operations  1.06 us (1%)
    ppermute x14, waiting for transfers between devices, sent(): return lax.ppermute(array, axis, pairs)  48.1 us
    ppermute x14, starting transfers between devices, sent(): return lax.ppermute(array, axis, pairs)  13.7 us
    pallas_call x2, Pallas kernels, body(): run(functools.partial(lower_kernel, length, parity), 20, out_shape=(whole...  3.96 us
    pallas_call x1, Pallas kernels, body(): run(own_kernel, 60, out_shape=(rows_of(ps), rows_of(ps + pf), rows_of(nod...  3.94 us
    unnamed x4, local copies, waits for them, and re-layouts  2.55 us
  transfers between devices with their start and end apart: 14, of which 2 were waited for; matrix products, arithmetic and copies ran while one was open for 0% of the time, Pallas kernels for 2%

profile of v3, /device:TPU:27, one launch (start us, length us, event | category | flops | bytes accessed | tf_op | source)
XLA Modules:
  0.0 75.3 jit_solution(4969216494163799553)
XLA Ops:
  0.6 3.9 %own.1 = (f32[648,128]{1,0:T(8,128)}, f32[1800,128]{1,0:T(8,128)}, f32[2952,128]{1,0:T(8,128)}) custom-call(f32[1,384,384]{2,1,0:T(8,128)} %inv_ref.1, f32[1,384,384]{2,1,0:T(8,128)} %low_ref.1, f32[1,384,384]{2,1,0:T(8,128)} %up_ref.1), custom_call_target="tpu_custom_call" | custom-call | flops 1 | bytes 1 | tf_op jit(solution)/shard_map/own/pallas_call | solution.py:462
  4.6 3.2 %collective-permute-start.5 = (f32[2952,128]{1,0:T(8,128)}, f32[2952,128]{1,0:T(8,128)S(1)}, u32[]{:S(2)}, u32[]{:S(2)}) collective-permute-start(f32[2952,128]{1,0:T(8,128)} %get-tuple-element.21.node), channel_id=1, source_target_pairs={{1,5},{9,13},{17,21},{25,29},{31,0},{7,8},{15,16},{23,24},{3,7},{1... | collective-permute-start | bytes 4534280 | tf_op jit(solution)/shard_map/ppermute | solution.py:406
  7.8 0.7 collective-permute-start.1
  8.5 0.7 collective-permute-start
  9.2 1.4 %collective-permute-start.4 = (f32[2952,128]{1,0:T(8,128)}, f32[2952,128]{1,0:T(8,128)S(1)}, u32[]{:S(2)}, u32[]{:S(2)}) collective-permute-start(f32[2952,128]{1,0:T(8,128)} %get-tuple-element.21.node), channel_id=1, source_target_pairs={{5,13},{21,29},{31,30},{7,6},{15,14},{23,22},{3,2},{11,10},{19,18}... | collective-permute-start | bytes 4534280 | tf_op jit(solution)/shard_map/ppermute | solution.py:406
  10.6 0.0 collective-permute-done.came_root.root_mid
  10.7 1.2 %copy-done.1 = f32[1800,128]{1,0:T(8,128)S(1)} copy-done((f32[1800,128]{1,0:T(8,128)S(1)}, f32[1800,128]{1,0:T(8,128)}, u32[]{:S(2)}) %copy-start.1) | copy-done | bytes 921624
  11.9 0.7 collective-permute-start.3
  12.5 0.7 collective-permute-start.2
  13.2 0.0 collective-permute-done.1.came_part
  13.3 1.4 %copy-done = f32[2952,128]{1,0:T(8,128)S(1)} copy-done((f32[2952,128]{1,0:T(8,128)S(1)}, f32[2952,128]{1,0:T(8,128)}, u32[]{:S(2)}) %copy-start) | copy-done | bytes 1511448
  14.6 0.0 collective-permute-done.3.mid_zero
  14.6 0.0 collective-permute-done.2.came_sym
  14.6 10.1 %collective-permute-done.5.came_four.came_far = f32[2952,128]{1,0:T(8,128)S(1)} collective-permute-done((f32[2952,128]{1,0:T(8,128)}, f32[2952,128]{1,0:T(8,128)S(1)}, u32[]{:S(2)}, u32[]{:S(2)}) %collective-permute-start.5) | collective-permute-done | bytes 1511456 | tf_op jit(solution)/shard_map/ppermute | solution.py:406
  24.7 0.7 collective-permute-start.12
  25.5 0.0 collective-permute-done.4.came_node.came_near
  25.5 1.2 %upper.1 = (f32[1,384,384]{2,1,0:T(8,128)}, f32[1,384,384]{2,1,0:T(8,128)}, f32[1296,128]{1,0:T(8,128)S(1)}, f32[1152,128]{1,0:T(8,128)S(1)}, f32[2448,128]{1,0:T(8,128)S(1)}) custom-call(f32[2,384,384]{2,1,0:T(8,128)S(1)} %get-tuple-element.20.at_m, f32[2,384,384]{2,1,0:T(8,128)S(1)} %low.1.at_l, f32[648,128]{1,0:T(8,128)S(1)} %collective-permute-done.came_root.root_mid, ...), custom_call_target="tpu_custom_call" | custom-call | flops 1 | bytes 1 | tf_op jit(solution)/shard_map/upper/pallas_call | solution.py:491
  26.7 0.7 collective-permute-start.7
  27.4 0.7 collective-permute-start.11
  28.2 0.7 collective-permute-start.10
  28.9 0.7 collective-permute-start.9
  29.6 0.7 collective-permute-start.6
  30.4 0.7 collective-permute-start.8
  31.1 0.5 near.1
  31.5 0.0 collective-permute-done.6.one
  31.5 0.0 collective-permute-done.8.one_cross
  31.6 0.0 collective-permute-done.10.five
  31.6 0.3 choose.1.state
  31.8 1.3 %collective-permute-start.13 = (f32[2448,128]{1,0:T(8,128)S(1)}, f32[2448,128]{1,0:T(8,128)S(1)}, u32[]{:S(2)}, u32[]{:S(2)}) collective-permute-start(f32[2448,128]{1,0:T(8,128)S(1)} %choose.1.state), channel_id=1, source_target_pairs={{30,31},{6,7},{14,15},{22,23},{0,1},{8,9},{16,17},{24,25},{2,3},{1... | collective-permute-start | bytes 3760136 | tf_op jit(solution)/shard_map/ppermute | solution.py:406
  33.1 0.1 lower.2
  33.2 38.0 %collective-permute-done.13.state = f32[2448,128]{1,0:T(8,128)S(1)} collective-permute-done((f32[2448,128]{1,0:T(8,128)S(1)}, f32[2448,128]{1,0:T(8,128)S(1)}, u32[]{:S(2)}, u32[]{:S(2)}) %collective-permute-start.13) | collective-permute-done | bytes 1253408 | tf_op jit(solution)/shard_map/ppermute | solution.py:406
  71.2 3.9 %lower.3 = (f32[1,384,384]{2,1,0:T(8,128)}, f32[1,384,384]{2,1,0:T(8,128)}) custom-call(f32[2448,128]{1,0:T(8,128)S(1)} %collective-permute-done.13.state, bf16[768,768]{1,0:T(8,128)(2,1)S(1)} %get-tuple-element.28.fh, bf16[768,768]{1,0:T(8,128)(2,1)S(1)} %get-tuple-element.29.fl, ...), custom_call_target="tpu_custom_call", output_to_operand_aliasing={{0}: (4, {}), {1}: (5, {})} | custom-call | flops 1 | bytes 1 | tf_op jit(solution)/shard_map/lower/pallas_call | solution.py:527
  (8 shorter events, 0.0 us)
Async XLA Ops:
  4.6 20.2 %collective-permute-start.5 = (f32[2952,128]{1,0:T(8,128)}, f32[2952,128]{1,0:T(8,128)S(1)}, u32[]{:S(2)}, u32[]{:S(2)}) collective-permute-start(f32[2952,128]{1,0:T(8,128)} %get-tuple-element.21.node), channel_id=1, source_target_pairs={{1,5},{9,13},{17,21},{25,29},{31,0},{7,8},{15,16},{23,24},{3,7},{1... | collective-permute-start | bytes 4534280 | tf_op jit(solution)/shard_map/ppermute | solution.py:406
  7.8 5.4 %collective-permute-start.1 = (f32[1800,128]{1,0:T(8,128)}, f32[1800,128]{1,0:T(8,128)S(1)}, u32[]{:S(2)}, u32[]{:S(2)}) collective-permute-start(f32[1800,128]{1,0:T(8,128)} %get-tuple-element.18.part), channel_id=1, source_target_pairs={{13,5}} | collective-permute-start | bytes 2764808 | tf_op jit(solution)/shard_map/ppermute | solution.py:406
  8.5 2.1 %collective-permute-start = (f32[648,128]{1,0:T(8,128)}, f32[648,128]{1,0:T(8,128)S(1)}, u32[]{:S(2)}, u32[]{:S(2)}) collective-permute-start(f32[648,128]{1,0:T(8,128)} %get-tuple-element.19), channel_id=1, source_target_pairs={{29,13}} | collective-permute-start | bytes 995336 | tf_op jit(solution)/shard_map/ppermute | solution.py:406
  9.2 16.2 %collective-permute-start.4 = (f32[2952,128]{1,0:T(8,128)}, f32[2952,128]{1,0:T(8,128)S(1)}, u32[]{:S(2)}, u32[]{:S(2)}) collective-permute-start(f32[2952,128]{1,0:T(8,128)} %get-tuple-element.21.node), channel_id=1, source_target_pairs={{5,13},{21,29},{31,30},{7,6},{15,14},{23,22},{3,2},{11,10},{19,18}... | collective-permute-start | bytes 4534280 | tf_op jit(solution)/shard_map/ppermute | solution.py:406
  10.6 1.2 %copy-start.1 = (f32[1800,128]{1,0:T(8,128)S(1)}, f32[1800,128]{1,0:T(8,128)}, u32[]{:S(2)}) copy-start(f32[1800,128]{1,0:T(8,128)} %get-tuple-element.18.part) | copy-start | bytes 2764804
  11.9 2.8 %collective-permute-start.3 = (f32[648,128]{1,0:T(8,128)S(1)}, f32[648,128]{1,0:T(8,128)S(1)}, u32[]{:S(2)}, u32[]{:S(2)}) collective-permute-start(f32[648,128]{1,0:T(8,128)S(1)} %get-tuple-element.22._after), channel_id=1, source_target_pairs={{13,29}} | collective-permute-start | bytes 995336 | tf_op jit(solution)/shard_map/ppermute | solution.py:406
  12.5 2.1 %collective-permute-start.2 = (f32[648,128]{1,0:T(8,128)S(1)}, f32[648,128]{1,0:T(8,128)S(1)}, u32[]{:S(2)}, u32[]{:S(2)}) collective-permute-start(f32[648,128]{1,0:T(8,128)S(1)} %get-tuple-element.22._after), channel_id=1, source_target_pairs={{13,21},{29,5}} | collective-permute-start | bytes 995336 | tf_op jit(solution)/shard_map/ppermute | solution.py:406
  13.2 1.4 %copy-start = (f32[2952,128]{1,0:T(8,128)S(1)}, f32[2952,128]{1,0:T(8,128)}, u32[]{:S(2)}) copy-start(f32[2952,128]{1,0:T(8,128)} %get-tuple-element.21.node) | copy-start | bytes 4534276
  24.7 5.6 %collective-permute-start.12 = (f32[2952,128]{1,0:T(8,128)S(1)}, f32[2952,128]{1,0:T(8,128)S(1)}, u32[]{:S(2)}, u32[]{:S(2)}) collective-permute-start(f32[2952,128]{1,0:T(8,128)S(1)} %collective-permute-done.5.came_four.came_far), channel_id=1, source_target_pairs={{31,28},{7,4},{15,12},{23,20}} | collective-permute-start | bytes 4534280 | tf_op jit(solution)/shard_map/ppermute | solution.py:406
  26.7 2.9 %collective-permute-start.7 = (f32[1152,128]{1,0:T(8,128)S(1)}, f32[1152,128]{1,0:T(8,128)S(1)}, u32[]{:S(2)}, u32[]{:S(2)}) collective-permute-start(f32[1152,128]{1,0:T(8,128)S(1)} %get-tuple-element.24), channel_id=1, source_target_pairs={{29,24},{5,0},{13,8},{21,16}} | collective-permute-start | bytes 1769480 | tf_op jit(solution)/shard_map/ppermute | solution.py:406
  27.4 4.1 %collective-permute-start.11 = (f32[2448,128]{1,0:T(8,128)S(1)}, f32[2448,128]{1,0:T(8,128)S(1)}, u32[]{:S(2)}, u32[]{:S(2)}) collective-permute-start(f32[2448,128]{1,0:T(8,128)S(1)} %get-tuple-element.25), channel_id=1, source_target_pairs={{29,28},{5,4},{13,12},{21,20}} | collective-permute-start | bytes 3760136 | tf_op jit(solution)/shard_map/ppermute | solution.py:406
  28.2 3.4 %collective-permute-start.10 = (f32[2448,128]{1,0:T(8,128)S(1)}, f32[2448,128]{1,0:T(8,128)S(1)}, u32[]{:S(2)}, u32[]{:S(2)}) collective-permute-start(f32[2448,128]{1,0:T(8,128)S(1)} %get-tuple-element.25), channel_id=1, source_target_pairs={{29,26},{5,2},{13,10},{21,18}} | collective-permute-start | bytes 3760136 | tf_op jit(solution)/shard_map/ppermute | solution.py:406
  28.9 2.6 %collective-permute-start.9 = (f32[1296,128]{1,0:T(8,128)S(1)}, f32[1296,128]{1,0:T(8,128)S(1)}, u32[]{:S(2)}, u32[]{:S(2)}) collective-permute-start(f32[1296,128]{1,0:T(8,128)S(1)} %get-tuple-element.23), channel_id=1, source_target_pairs={{29,24},{5,0},{13,8},{21,16}} | collective-permute-start | bytes 1990664 | tf_op jit(solution)/shard_map/ppermute | solution.py:406
  29.6 1.9 %collective-permute-start.6 = (f32[1296,128]{1,0:T(8,128)S(1)}, f32[1296,128]{1,0:T(8,128)S(1)}, u32[]{:S(2)}, u32[]{:S(2)}) collective-permute-start(f32[1296,128]{1,0:T(8,128)S(1)} %get-tuple-element.23), channel_id=1, source_target_pairs={{29,22},{5,30},{13,6},{21,14}} | collective-permute-start | bytes 1990664 | tf_op jit(solution)/shard_map/ppermute | solution.py:406
  30.4 1.2 %collective-permute-start.8 = (f32[1152,128]{1,0:T(8,128)S(1)}, f32[1152,128]{1,0:T(8,128)S(1)}, u32[]{:S(2)}, u32[]{:S(2)}) collective-permute-start(f32[1152,128]{1,0:T(8,128)S(1)} %collective-permute-done.7.three_cross), channel_id=1, source_target_pairs={{0,30},{8,6},{16,14},{24,22}} | collective-permute-start | bytes 1769480 | tf_op jit(solution)/shard_map/ppermute | solution.py:406
  31.8 39.4 %collective-permute-start.13 = (f32[2448,128]{1,0:T(8,128)S(1)}, f32[2448,128]{1,0:T(8,128)S(1)}, u32[]{:S(2)}, u32[]{:S(2)}) collective-permute-start(f32[2448,128]{1,0:T(8,128)S(1)} %choose.1.state), channel_id=1, source_target_pairs={{30,31},{6,7},{14,15},{22,23},{0,1},{8,9},{16,17},{24,25},{2,3},{1... | collective-permute-start | bytes 3760136 | tf_op jit(solution)/shard_map/ppermute | solution.py:406

commit v4 on v3

--- a/solution.py
+++ b/solution.py
@@ -148,17 +148,35 @@
         copy.wait()
 
 
-def own_kernel(inv_ref, low_ref, up_ref, sym_ref, part_ref, node_ref, rooms, sems):
+def own_kernel(inv_ref, low_ref, up_ref, sym_ref, part_ref, node_ref, rooms, lines, sems, out_sems):
     width = inv_ref.shape[1]
-    fetch(sems, *((ref.at[0], rooms.at[i]) for i, ref in enumerate((inv_ref, low_ref, up_ref))))
+    ps, pf = sym_rows(width), full_rows(width)
+    loads = [
+        pltpu.make_async_copy(ref.at[0], rooms.at[i], sems.at[i]) for i, ref in enumerate((inv_ref, low_ref, up_ref))
+    ]
+    for load in loads:
+        load.start()
+    stores = []
+
+    def store(at, rows, *refs):
+        for ref in refs:
+            where = pl.ds(at, rows)
+            stores.append(pltpu.make_async_copy(lines.at[where, :], ref.at[where, :], out_sems.at[len(stores)]))
+            stores[-1].start()
+
+    loads[0].wait()
     inverse = rooms[0]
+    put_sym(lines, 0, inverse)
+    store(0, ps, sym_ref, part_ref, node_ref)
     inv_parts = parts_of(inverse)
-    ps, pf = sym_rows(width), full_rows(width)
-    put_sym(sym_ref, 0, inverse)
-    part_ref[pl.ds(0, ps), :] = sym_ref[...]
-    put_full(part_ref, ps, times(inv_parts, parts_of(rooms[1])))
-    node_ref[pl.ds(0, ps + pf), :] = part_ref[...]
-    put_full(node_ref, ps + pf, times(inv_parts, parts_of(rooms[2])))
+    loads[1].wait()
+    put_full(lines, ps, times(inv_parts, parts_of(rooms[1])))
+    store(ps, pf, part_ref, node_ref)
+    loads[2].wait()
+    put_full(lines, ps + pf, times(inv_parts, parts_of(rooms[2])))
+    store(ps + pf, pf, node_ref)
+    for copy in stores:
+        copy.wait()
 
 
 def get_node(ref, width):
@@ -211,24 +229,33 @@
         out[1] = own_d + times(parts_of(passed), h_parts, True)
 
 
-def halve(four, sh, sl, low_ref, low_cross_ref, high_ref):
-    width = sh.shape[0] // 2
+def hand_over(rooms, sems, diag_ref, cross_ref, diag, cross):
+    rooms[0], rooms[1] = diag, cross
+    fetch(sems, (rooms.at[0], diag_ref.at[0]), (rooms.at[1], cross_ref.at[0]))
+
+
+def first_kernel(length, at_m, root_mid, came_node, diag_ref, cross_ref, sh, sl, aa_ref, bb_ref, rooms, sems):
+    width = rooms.shape[1]
+    _, _, at_mid, _ = roles_of(length)
+
+    @pl.when(at_mid)
+    def _():
+        mid_cross, mid = at_m[0], at_m[1]
+        set_state(sh, sl, get_sym(root_mid, 0, width), mid_cross, mid)
+        passed, own = eliminate(get_node(came_node, width), sh, sl)
+        put_sym(aa_ref, 0, own)
+        put_sym(bb_ref, 0, mid)
+        set_state(sh, sl, own, passed[:, width:].T, mid)
+        hand_over(rooms, sems, diag_ref, cross_ref, mid, mid_cross)
+
+
+def second_kernel(
+    length, at_l, came_sym, mid_zero, part, came_part, _diag, _cross, _sh, _sl, _aa, _bb,
+    diag_ref, cross_ref, sh, sl, aa_ref, bb_ref, rooms, sems,
+):
+    width = rooms.shape[1]
     ps = sym_rows(width)
-    passed, own = eliminate(get_node(four, width), sh, sl)
-    put_full(low_cross_ref, 0, passed[:, :width])
-    put_full(high_ref, 2 * ps, passed[:, width:].T)
-    put_sym(low_ref, ps, own)
-    high_ref[pl.ds(0, ps), :] = low_ref[pl.ds(ps, ps), :]
-
-
-def upper_kernel(
-    length, at_m, at_l, root_mid, came_sym, mid_zero, node, came_node, came_four,
-    diag_ref, cross_ref, low_ref, low_cross_ref, high_ref, sh, sl,
-):
-    width = diag_ref.shape[1]
-    ps = sym_rows(width)
-    at_zero, at_low, at_mid, at_high = roles_of(length)
-    low_end, high_end = pl.ds(0, ps), pl.ds(ps, ps)
+    at_zero, at_low, _, at_high = roles_of(length)
 
     @pl.when(at_low)
     def _():
@@ -236,76 +263,79 @@
         passed = parts_of(at_l[0])
         cross = times(passed, parts_of(root))
         own = at_l[1] + symmetric_times(long_left(parts_of(cross)), long_right(passed, True))
-        diag_ref[0], cross_ref[0] = own, cross
-        low_ref[low_end, :] = came_sym[...]
-        put_sym(high_ref, ps, own)
+        aa_ref[...] = came_sym[...]
+        put_sym(bb_ref, 0, own)
         set_state(sh, sl, root, cross, own)
-
-    @pl.when(at_mid)
-    def _():
-        mid_cross, mid = at_m[0], at_m[1]
-        diag_ref[0], cross_ref[0] = mid, mid_cross
-        set_state(sh, sl, get_sym(root_mid, 0, width), mid_cross, mid)
-        passed, own = eliminate(get_node(came_node, width), sh, sl)
-        put_sym(low_ref, 0, own)
-        put_sym(high_ref, ps, mid)
-        set_state(sh, sl, own, passed[:, width:].T, mid)
+        hand_over(rooms, sems, diag_ref, cross_ref, own, cross)
 
     def above(mid_ref, node_ref):
-        own_d, own_g, _ = get_node(node_ref, width)
+        own_d, own_g = get_sym(node_ref, 0, width), parts_of(get_full(node_ref, ps, width))
         mid = get_sym(mid_ref, 0, width)
-        own_g = parts_of(own_g)
         cross = -times(own_g, parts_of(mid))
         return mid, cross, own_d - times(own_g, parts_of(cross), True)
 
     @pl.when(at_high)
     def _():
-        mid, cross, own = above(came_sym, node)
-        diag_ref[0], cross_ref[0] = own, cross
-        low_ref[low_end, :] = came_sym[...]
-        put_sym(high_ref, ps, own)
+        mid, cross, own = above(came_sym, part)
+        aa_ref[...] = came_sym[...]
+        put_sym(bb_ref, 0, own)
         set_state(sh, sl, mid, cross, own)
+        hand_over(rooms, sems, diag_ref, cross_ref, own, cross)
 
     @pl.when(at_zero)
     def _():
-        _, _, own = above(mid_zero, came_node)
+        _, _, own = above(mid_zero, came_part)
         zeros = jnp.zeros((width, width), f32)
-        diag_ref[0], cross_ref[0] = get_sym(node, 0, width), zeros
-        put_sym(low_ref, 0, own)
-        high_ref[high_end, :] = jnp.zeros((ps, lanes), f32)
+        put_sym(aa_ref, 0, own)
+        bb_ref[...] = jnp.zeros((ps, lanes), f32)
         set_state(sh, sl, own, zeros, zeros)
-
-    @pl.when(lax.rem(place_now(length), group) == 0)
-    def _():
-        halve(came_four, sh, sl, low_ref, low_cross_ref, high_ref)
-
-
-def halve_kernel(came_four, aa_ref, ba_ref, bb_ref, low_ref, low_cross_ref, high_ref, sh, sl):
+        hand_over(rooms, sems, diag_ref, cross_ref, get_sym(part, 0, width), zeros)
+
+
+def state_kernel(aa_ref, ba_ref, bb_ref, sh, sl, aa_out, bb_out):
     aa, bb = aa_ref[...], bb_ref[...]
-    put_sym(low_ref, 0, aa)
-    put_sym(high_ref, sym_rows(aa.shape[0]), bb)
+    put_sym(aa_out, 0, aa)
+    put_sym(bb_out, 0, bb)
     set_state(sh, sl, aa, ba_ref[...], bb)
-    halve(came_four, sh, sl, low_ref, low_cross_ref, high_ref)
+
+
+def halve_kernel(length, sh, sl, aa_ref, bb_ref, *refs):
+    fours, (low_ref, low_cross_ref, high_ref) = refs[:-3], refs[-3:]
+    width = sh.shape[0] // 2
+    ps = sym_rows(width)
+    place = place_now(length)
+
+    def work(four):
+        passed, own = eliminate(get_node(four, width), sh, sl)
+        put_full(low_cross_ref, 0, passed[:, :width])
+        put_full(high_ref, 2 * ps, passed[:, width:].T)
+        low_ref[pl.ds(0, ps), :] = aa_ref[...]
+        put_sym(low_ref, ps, own)
+        high_ref[pl.ds(0, ps), :] = low_ref[pl.ds(ps, ps), :]
+        high_ref[pl.ds(ps, ps), :] = bb_ref[...]
+
+    served = lax.rem(place, group) == 0
+    if len(fours) == 1:
+        pl.when(served)(lambda: work(fours[0]))
+    else:
+        at_mid = place == 2 * group
+        pl.when(at_mid)(lambda: work(fours[1]))
+        pl.when(jnp.logical_and(served, jnp.logical_not(at_mid)))(lambda: work(fours[0]))
 
 
 def offset_of(length):
     return lax.rem(place_now(length), group)
 
 
-def near_kernel(length, node, came_near, came_far, came_back, f_high, f_low, rest_ref):
+def near_kernel(length, late, node, *refs):
+    f_high, f_low, rest_ref = refs[-3:]
     width = rest_ref.shape[0]
-    turn = lax.rem(offset_of(length), group // 2)
+    offset = offset_of(length)
+    turn = lax.rem(offset, group // 2)
     first, second = slice(0, width), slice(width, 2 * width)
 
     def put(rows, columns, mat):
         f_high[rows, columns], f_low[rows, columns] = parts_of(mat)
-
-    @pl.when(turn == 2)
-    def _():
-        d_own, g_own, h_own = get_node(node, width)
-        put(first, first, -g_own)
-        put(first, second, -h_own)
-        rest_ref[:, first] = d_own
 
     def odd(below, two):
         d_own, g_own, h_own = get_node(node, width)
@@ -322,16 +352,19 @@
             put(second, second, -h_two)
             rest_ref[:, second] = link
 
-    @pl.when(turn == 1)
-    def _():
-        odd(True, came_near)
-
-    offset = offset_of(length)
-    for at, two in ((3, came_far), (7, came_back)):
-
-        @pl.when(offset == at)
-        def _(two=two):
-            odd(False, two)
+    if late:
+        pl.when(offset == group - 1)(lambda: odd(False, refs[0]))
+        return
+    came_near, came_far = refs[:2]
+    pl.when(turn == 1)(lambda: odd(True, came_near))
+    pl.when(offset == 3)(lambda: odd(False, came_far))
+
+    @pl.when(turn == 2)
+    def _():
+        d_own, g_own, h_own = get_node(node, width)
+        put(first, first, -g_own)
+        put(first, second, -h_own)
+        rest_ref[:, first] = d_own
 
 
 def choose_kernel(length, one, one_cross, three, three_cross, five, seven, _after, out_ref):
@@ -461,22 +494,23 @@
 
     sym, part, node = run(
         own_kernel, 60, out_shape=(rows_of(ps), rows_of(ps + pf), rows_of(node_rows)),
-        in_specs=[anywhere] * 3, out_specs=[vmem] * 3,
-        scratch_shapes=[room(3, *square), sems], name="own",
+        in_specs=[anywhere] * 3, out_specs=[anywhere] * 3,
+        scratch_shapes=[room(3, *square), room(node_rows, lanes), sems, pltpu.SemaphoreType.DMA((6,))], name="own",
     )(inv_diag, low_coupling, up_coupling)
 
     close = ((-1, inner(2)), (-1, inner(6)))
-    came_far = sent(node, length, (half, inner(half)), (1, inner(2)), (4, inner(6)))
+    away = ((1, inner(2)), (group // 2, inner(6)))
+    half_state = (jax.ShapeDtypeStruct((2 * width, 2 * width), bf16),) * 2 + (rows_of(ps),) * 2
+    rooms = [room(2, *square), sems]
     if is_open:
-        came_near = sent(node, length, (group, at(group)), (group, at(3 * group)), *close)
-        came_part = sent(part, length, (-group, at(mid)))
+        to_mid = lambda p: p == mid - half
+        came_far = sent(
+            node, length, (half, lambda p: inner(half)(p) and not to_mid(p)), (group, at(group)), *away
+        )
+        came_near = sent(node, length, (half, to_mid), *close)
+        came_part = sent(part, length, (-group, at(mid)), (group, at(3 * group)))
         root_mid = sent(sym, length, (mid, at(0)))
-    else:
-        came_near = sent(node, length, *close)
-
-    state_room = [room(2 * width, 2 * width, kind=bf16)] * 2
-    two = jax.ShapeDtypeStruct((2,) + square, f32)
-    if is_open:
+        two = jax.ShapeDtypeStruct((2,) + square, f32)
         at_m, mid_sym = run(
             functools.partial(mid_kernel, length), 16, out_shape=(two, rows_of(ps)),
             in_specs=[vmem] * 2, out_specs=[vmem] * 2, name="middle",
@@ -487,47 +521,61 @@
             functools.partial(low_kernel, length), 16, out_shape=two,
             in_specs=[vmem] * 2 + [anywhere], out_specs=vmem, name="low",
         )(node, came_part, mid_sym)
-        later, *_ = lax.optimization_barrier((came_far, at_l, came_sym, mid_zero))
-        diag, cross, low_half, low_cross, high_half = run(
-            functools.partial(upper_kernel, length), 16,
-            out_shape=(whole, whole, rows_of(2 * ps), rows_of(pf), rows_of(state_rows)),
-            in_specs=[vmem] * 8, out_specs=[vmem] * 5, scratch_shapes=state_room, name="upper",
-        )(at_m, at_l, root_mid, came_sym, mid_zero, node, came_near, came_far)
+        made = run(
+            functools.partial(first_kernel, length), 16, out_shape=(whole,) * 2 + half_state,
+            in_specs=[vmem] * 3, out_specs=[anywhere] * 2 + [vmem] * 4, scratch_shapes=rooms, name="first",
+        )(at_m, root_mid, came_far)
+        diag, cross, *ends = run(
+            functools.partial(second_kernel, length), 16, out_shape=(whole,) * 2 + half_state,
+            in_specs=[vmem] * 5 + [anywhere] * 2 + [vmem] * 4, out_specs=[anywhere] * 2 + [vmem] * 4,
+            scratch_shapes=rooms, input_output_aliases={5 + i: i for i in range(6)}, name="second",
+        )(at_l, came_sym, mid_zero, part, came_part, *made)
+        fours = (came_far, came_near)
     else:
+        came_far = sent(node, length, (half, inner(half)), *away)
+        came_near = sent(node, length, *close)
         diag, cross, below = upper_levels(inv_diag[0], low_coupling[0], up_coupling[0], length)
         diag, cross = diag[None], cross[None]
-        later = came_far
-        low_half, low_cross, high_half = run(
-            halve_kernel, 16, out_shape=(rows_of(2 * ps), rows_of(pf), rows_of(state_rows)),
-            in_specs=[vmem] * 4, out_specs=[vmem] * 3, scratch_shapes=state_room, name="halve",
-        )(came_far, *below)
-
-    came_back = sent(later, length, (-3, inner(2)))
+        ends = run(
+            state_kernel, 16, out_shape=half_state, in_specs=[vmem] * 3, out_specs=[vmem] * 4, name="state",
+        )(*below)
+        fours = (came_far,)
+    low_half, low_cross, high_half = run(
+        functools.partial(halve_kernel, length), 16,
+        out_shape=(rows_of(2 * ps), rows_of(pf), rows_of(state_rows)),
+        in_specs=[vmem] * (4 + len(fours)), out_specs=[vmem] * 3, name="halve",
+    )(*ends, *fours)
     three_cross = sent(low_cross, length, (-5, inner(0)))
     to_five = sent(high_half, length, (-3, inner(0)))
     to_one = sent(low_half, length, (-7, inner(0)))
     to_three = sent(low_half, length, (-5, inner(0)))
     to_seven = sent(high_half, length, (-1, inner(0)))
     one_cross = sent(three_cross, length, (-2, inner(3)))
-
+    later, _ = lax.optimization_barrier((came_far, three_cross))
+    came_back = sent(later, length, (-3, inner(2)))
+
+    shapes = (jax.ShapeDtypeStruct((2 * width, 2 * width), bf16),) * 2 + (jax.ShapeDtypeStruct((width, 2 * width), f32),)
+    composed = run(
+        functools.partial(near_kernel, length, False), 16, out_shape=shapes,
+        in_specs=[vmem] * 3, out_specs=[vmem] * 3, name="near",
+    )(node, came_near, came_far)
     f_high, f_low, rest = run(
-        functools.partial(near_kernel, length), 16,
-        out_shape=(jax.ShapeDtypeStruct((2 * width, 2 * width), bf16),) * 2
-        + (jax.ShapeDtypeStruct((width, 2 * width), f32),),
-        in_specs=[vmem] * 4, out_specs=[vmem] * 3, name="near",
-    )(node, came_near, came_far, came_back)
+        functools.partial(near_kernel, length, True), 16, out_shape=shapes,
+        in_specs=[vmem] * 2 + [vmem] * 3, out_specs=[vmem] * 3, name="back",
+        input_output_aliases={2: 0, 3: 1, 4: 2},
+    )(node, came_back, *composed)
 
     state = run(
         functools.partial(choose_kernel, length), 16,
         out_shape=rows_of(state_rows), in_specs=[vmem] * 6 + [anywhere], out_specs=vmem, name="choose",
-    )(to_one, one_cross, to_three, three_cross, to_five, to_seven, rest)
+    )(to_one, one_cross, to_three, three_cross, to_five, to_seven, composed[2])
     state_next = sent(state, length, (1, inner(1)), (1, inner(3)), (1, inner(5)))
 
     for parity, came in ((1, state), (0, state_next)):
         diag, cross = run(
             functools.partial(lower_kernel, length, parity), 20,
             out_shape=(whole, whole), in_specs=[vmem] * 4 + [anywhere] * 2, out_specs=[anywhere] * 2,
-            scratch_shapes=[room(*square)] * 2 + state_room + [sems],
+            scratch_shapes=[room(*square)] * 2 + [room(2 * width, 2 * width, kind=bf16)] * 2 + [sems],
             input_output_aliases={4: 0, 5: 1},
             name="lower",
         )(came, f_high, f_low, rest, diag, cross)

time: 75.7 us -> 69.9 us (0.923)
  the two profiles are of different devices: /device:TPU:27 before, /device:TPU:23 now
where the time goes in v4:
time: 69.9 us; the launch traced here: 69.4 us
  waiting for transfers between devices  41.1 us (59%)
  starting transfers between devices  15.1 us (22%)
  Pallas kernels  8.37 us (12%)
  local copies, waits for them, and re-layouts  3.67 us (5%)
  between operations  1.11 us (2%)
    ppermute x14, waiting for transfers between devices, sent(): return lax.ppermute(array, axis, pairs)  41.1 us
    ppermute x14, starting transfers between devices, sent(): return lax.ppermute(array, axis, pairs)  15.1 us
    pallas_call x2, Pallas kernels, body(): run(functools.partial(lower_kernel, length, parity), 20, out_shape=(whole...  3.93 us
    pallas_call x1, Pallas kernels, body(): run(own_kernel, 60, out_shape=(rows_of(ps), rows_of(ps + pf), rows_of(nod...  3.83 us
    unnamed x8, local copies, waits for them, and re-layouts  3.67 us
  transfers between devices with their start and end apart: 14, of which 3 were waited for; matrix products, arithmetic and copies ran while one was open for 0% of the time, Pallas kernels for 1%

profile of v4, /device:TPU:23, one launch (start us, length us, event | category | flops | bytes accessed | tf_op | source)
XLA Modules:
  0.0 69.4 jit_solution(10030238963347052667)
XLA Ops:
  0.6 3.8 %own.1 = (f32[648,128]{1,0:T(8,128)}, f32[1800,128]{1,0:T(8,128)}, f32[2952,128]{1,0:T(8,128)}) custom-call(f32[1,384,384]{2,1,0:T(8,128)} %inv_ref.1, f32[1,384,384]{2,1,0:T(8,128)} %low_ref.1, f32[1,384,384]{2,1,0:T(8,128)} %up_ref.1), custom_call_target="tpu_custom_call" | custom-call | flops 1 | bytes 1 | tf_op jit(solution)/shard_map/own/pallas_call | solution.py:495
  4.5 3.7 %collective-permute-start.4 = (f32[2952,128]{1,0:T(8,128)}, f32[2952,128]{1,0:T(8,128)S(1)}, u32[]{:S(2)}, u32[]{:S(2)}) collective-permute-start(f32[2952,128]{1,0:T(8,128)} %get-tuple-element.31.node), channel_id=1, source_target_pairs={{1,5},{17,21},{25,29},{5,13},{31,0},{7,8},{15,16},{23,24},{3,7},{1... | collective-permute-start | bytes 4534280 | tf_op jit(solution)/shard_map/ppermute | solution.py:439
  8.2 1.4 %collective-permute-start.5 = (f32[2952,128]{1,0:T(8,128)}, f32[2952,128]{1,0:T(8,128)S(1)}, u32[]{:S(2)}, u32[]{:S(2)}) collective-permute-start(f32[2952,128]{1,0:T(8,128)} %get-tuple-element.31.node), channel_id=1, source_target_pairs={{9,13},{31,30},{7,6},{15,14},{23,22},{3,2},{11,10},{19,18},{27,26}} | collective-permute-start | bytes 4534280 | tf_op jit(solution)/shard_map/ppermute | solution.py:439
  9.5 0.7 %collective-permute-start = (f32[1800,128]{1,0:T(8,128)}, f32[1800,128]{1,0:T(8,128)S(1)}, u32[]{:S(2)}, u32[]{:S(2)}) collective-permute-start(f32[1800,128]{1,0:T(8,128)} %get-tuple-element.32.part), channel_id=1, source_target_pairs={{13,5},{21,29}} | collective-permute-start | bytes 2764808 | tf_op jit(solution)/shard_map/ppermute | solution.py:439
  10.3 0.7 collective-permute-start.1
  11.0 0.0 collective-permute-done.1.came_root.root_mid
  11.0 1.2 %copy-done.2 = f32[1800,128]{1,0:T(8,128)S(1)} copy-done((f32[1800,128]{1,0:T(8,128)S(1)}, f32[1800,128]{1,0:T(8,128)}, u32[]{:S(2)}) %copy-start.2) | copy-done | bytes 921624
  12.2 0.7 collective-permute-start.2
  12.9 0.7 collective-permute-start.3
  13.6 0.0 collective-permute-done.came_part
  13.6 1.4 %copy-done = f32[2952,128]{1,0:T(8,128)S(1)} copy-done((f32[2952,128]{1,0:T(8,128)S(1)}, f32[2952,128]{1,0:T(8,128)}, u32[]{:S(2)}) %copy-start) | copy-done | bytes 1511448
  15.0 10.2 %collective-permute-done.4.came_node.refs_0_.refs_1_ = f32[2952,128]{1,0:T(8,128)S(1)} collective-permute-done((f32[2952,128]{1,0:T(8,128)}, f32[2952,128]{1,0:T(8,128)S(1)}, u32[]{:S(2)}, u32[]{:S(2)}) %collective-permute-start.4) | collective-permute-done | bytes 1511456 | tf_op jit(solution)/shard_map/ppermute | solution.py:439
  25.2 0.0 collective-permute-done.2.came_sym
  25.2 0.0 collective-permute-done.3.mid_zero
  25.2 1.1 %copy-done.3 = f32[1800,128]{1,0:T(8,128)S(1)} copy-done((f32[1800,128]{1,0:T(8,128)S(1)}, f32[1800,128]{1,0:T(8,128)}, u32[]{:S(2)}) %copy-start.3) | copy-done | bytes 921624
  26.4 0.0 collective-permute-done.5.refs_1_.refs_0_
  26.5 0.9 %collective-permute-start.10 = (f32[2448,128]{1,0:T(8,128)S(1)}, f32[2448,128]{1,0:T(8,128)S(1)}, u32[]{:S(2)}, u32[]{:S(2)}) collective-permute-start(f32[2448,128]{1,0:T(8,128)S(1)} %get-tuple-element.48), channel_id=1, source_target_pairs={{29,26},{5,2},{13,10},{21,18}} | collective-permute-start | bytes 3760136 | tf_op jit(solution)/shard_map/ppermute | solution.py:439
  27.3 0.7 %collective-permute-start.11 = (f32[2448,128]{1,0:T(8,128)S(1)}, f32[2448,128]{1,0:T(8,128)S(1)}, u32[]{:S(2)}, u32[]{:S(2)}) collective-permute-start(f32[2448,128]{1,0:T(8,128)S(1)} %get-tuple-element.48), channel_id=1, source_target_pairs={{29,28},{5,4},{13,12},{21,20}} | collective-permute-start | bytes 3760136 | tf_op jit(solution)/shard_map/ppermute | solution.py:439
  28.1 0.7 %collective-permute-start.7 = (f32[1152,128]{1,0:T(8,128)S(1)}, f32[1152,128]{1,0:T(8,128)S(1)}, u32[]{:S(2)}, u32[]{:S(2)}) collective-permute-start(f32[1152,128]{1,0:T(8,128)S(1)} %get-tuple-element.47), channel_id=1, source_target_pairs={{29,24},{5,0},{13,8},{21,16}} | collective-permute-start | bytes 1769480 | tf_op jit(solution)/shard_map/ppermute | solution.py:439
  28.8 0.7 %collective-permute-start.6 = (f32[1296,128]{1,0:T(8,128)S(1)}, f32[1296,128]{1,0:T(8,128)S(1)}, u32[]{:S(2)}, u32[]{:S(2)}) collective-permute-start(f32[1296,128]{1,0:T(8,128)S(1)} %get-tuple-element.46), channel_id=1, source_target_pairs={{29,22},{5,30},{13,6},{21,14}} | collective-permute-start | bytes 1990664 | tf_op jit(solution)/shard_map/ppermute | solution.py:439
  29.5 0.7 %collective-permute-start.9 = (f32[1296,128]{1,0:T(8,128)S(1)}, f32[1296,128]{1,0:T(8,128)S(1)}, u32[]{:S(2)}, u32[]{:S(2)}) collective-permute-start(f32[1296,128]{1,0:T(8,128)S(1)} %get-tuple-element.46), channel_id=1, source_target_pairs={{29,24},{5,0},{13,8},{21,16}} | collective-permute-start | bytes 1990664 | tf_op jit(solution)/shard_map/ppermute | solution.py:439
  30.2 0.0 collective-permute-done.7.three_cross
  30.2 0.7 %collective-permute-start.8 = (f32[1152,128]{1,0:T(8,128)S(1)}, f32[1152,128]{1,0:T(8,128)S(1)}, u32[]{:S(2)}, u32[]{:S(2)}) collective-permute-start(f32[1152,128]{1,0:T(8,128)S(1)} %collective-permute-done.7.three_cross), channel_id=1, source_target_pairs={{0,30},{8,6},{16,14},{24,22}} | collective-permute-start | bytes 1769480 | tf_op jit(solution)/shard_map/ppermute | solution.py:439
  30.9 0.0 collective-permute-done.6.one
  30.9 1.4 %collective-permute-start.13 = (f32[2952,128]{1,0:T(8,128)S(1)}, f32[2952,128]{1,0:T(8,128)S(1)}, u32[]{:S(2)}, u32[]{:S(2)}) collective-permute-start(f32[2952,128]{1,0:T(8,128)S(1)} %collective-permute-done.4.came_node.refs_0_.refs_1_), channel_id=1, source_target_pairs={{31,28},{7,4},{15,12},{23,20}} | collective-permute-start | bytes 4534280 | tf_op jit(solution)/shard_map/ppermute | solution.py:439
  32.3 0.5 near.1
  32.8 0.0 collective-permute-done.9.three
  32.8 0.0 collective-permute-done.11.seven
  32.9 1.5 %collective-permute-start.12 = (f32[2448,128]{1,0:T(8,128)S(1)}, f32[2448,128]{1,0:T(8,128)S(1)}, u32[]{:S(2)}, u32[]{:S(2)}) collective-permute-start(f32[2448,128]{1,0:T(8,128)S(1)} %choose.1.state), channel_id=1, source_target_pairs={{30,31},{6,7},{14,15},{22,23},{0,1},{8,9},{16,17},{24,25},{2,3},{1... | collective-permute-start | bytes 3760136 | tf_op jit(solution)/shard_map/ppermute | solution.py:439
  34.4 14.5 %collective-permute-done.13.refs_0_ = f32[2952,128]{1,0:T(8,128)S(1)} collective-permute-done((f32[2952,128]{1,0:T(8,128)S(1)}, f32[2952,128]{1,0:T(8,128)S(1)}, u32[]{:S(2)}, u32[]{:S(2)}) %collective-permute-start.13) | collective-permute-done | bytes 1511456 | tf_op jit(solution)/shard_map/ppermute | solution.py:439
  49.0 16.4 %collective-permute-done.12.state = f32[2448,128]{1,0:T(8,128)S(1)} collective-permute-done((f32[2448,128]{1,0:T(8,128)S(1)}, f32[2448,128]{1,0:T(8,128)S(1)}, u32[]{:S(2)}, u32[]{:S(2)}) %collective-permute-start.12) | collective-permute-done | bytes 1253408 | tf_op jit(solution)/shard_map/ppermute | solution.py:439
  65.3 3.9 %lower.3 = (f32[1,384,384]{2,1,0:T(8,128)}, f32[1,384,384]{2,1,0:T(8,128)}) custom-call(f32[2448,128]{1,0:T(8,128)S(1)} %collective-permute-done.12.state, bf16[768,768]{1,0:T(8,128)(2,1)S(1)} %get-tuple-element.53.fh, bf16[768,768]{1,0:T(8,128)(2,1)S(1)} %get-tuple-element.54.fl, ...), custom_call_target="tpu_custom_call", output_to_operand_aliasing={{0}: (4, {}), {1}: (5, {})} | custom-call | flops 1 | bytes 1 | tf_op jit(solution)/shard_map/lower/pallas_call | solution.py:575
  (15 shorter events, 0.2 us)
Async XLA Ops:
  4.5 20.7 %collective-permute-start.4 = (f32[2952,128]{1,0:T(8,128)}, f32[2952,128]{1,0:T(8,128)S(1)}, u32[]{:S(2)}, u32[]{:S(2)}) collective-permute-start(f32[2952,128]{1,0:T(8,128)} %get-tuple-element.31.node), channel_id=1, source_target_pairs={{1,5},{17,21},{25,29},{5,13},{31,0},{7,8},{15,16},{23,24},{3,7},{1... | collective-permute-start | bytes 4534280 | tf_op jit(solution)/shard_map/ppermute | solution.py:439
  8.2 18.3 %collective-permute-start.5 = (f32[2952,128]{1,0:T(8,128)}, f32[2952,128]{1,0:T(8,128)S(1)}, u32[]{:S(2)}, u32[]{:S(2)}) collective-permute-start(f32[2952,128]{1,0:T(8,128)} %get-tuple-element.31.node), channel_id=1, source_target_pairs={{9,13},{31,30},{7,6},{15,14},{23,22},{3,2},{11,10},{19,18},{27,26}} | collective-permute-start | bytes 4534280 | tf_op jit(solution)/shard_map/ppermute | solution.py:439
  9.5 4.0 %collective-permute-start = (f32[1800,128]{1,0:T(8,128)}, f32[1800,128]{1,0:T(8,128)S(1)}, u32[]{:S(2)}, u32[]{:S(2)}) collective-permute-start(f32[1800,128]{1,0:T(8,128)} %get-tuple-element.32.part), channel_id=1, source_target_pairs={{13,5},{21,29}} | collective-permute-start | bytes 2764808 | tf_op jit(solution)/shard_map/ppermute | solution.py:439
  10.3 0.7 collective-permute-start.1
  11.0 1.2 %copy-start.2 = (f32[1800,128]{1,0:T(8,128)S(1)}, f32[1800,128]{1,0:T(8,128)}, u32[]{:S(2)}) copy-start(f32[1800,128]{1,0:T(8,128)} %get-tuple-element.32.part) | copy-start | bytes 2764804
  12.2 13.0 %collective-permute-start.2 = (f32[648,128]{1,0:T(8,128)S(1)}, f32[648,128]{1,0:T(8,128)S(1)}, u32[]{:S(2)}, u32[]{:S(2)}) collective-permute-start(f32[648,128]{1,0:T(8,128)S(1)} %get-tuple-element.34._after), channel_id=1, source_target_pairs={{13,21},{29,5}} | collective-permute-start | bytes 995336 | tf_op jit(solution)/shard_map/ppermute | solution.py:439
  12.9 12.4 %collective-permute-start.3 = (f32[648,128]{1,0:T(8,128)S(1)}, f32[648,128]{1,0:T(8,128)S(1)}, u32[]{:S(2)}, u32[]{:S(2)}) collective-permute-start(f32[648,128]{1,0:T(8,128)S(1)} %get-tuple-element.34._after), channel_id=1, source_target_pairs={{13,29}} | collective-permute-start | bytes 995336 | tf_op jit(solution)/shard_map/ppermute | solution.py:439
  13.6 1.4 %copy-start = (f32[2952,128]{1,0:T(8,128)S(1)}, f32[2952,128]{1,0:T(8,128)}, u32[]{:S(2)}) copy-start(f32[2952,128]{1,0:T(8,128)} %get-tuple-element.31.node) | copy-start | bytes 4534276
  25.2 1.2 %copy-start.3 = (f32[1800,128]{1,0:T(8,128)S(1)}, f32[1800,128]{1,0:T(8,128)}, u32[]{:S(2)}) copy-start(f32[1800,128]{1,0:T(8,128)} %get-tuple-element.32.part) | copy-start | bytes 2764804
  26.4 5.9 %copy-start.1 = (f32[2952,128]{1,0:T(8,128)S(1)}, f32[2952,128]{1,0:T(8,128)}, u32[]{:S(2)}) copy-start(f32[2952,128]{1,0:T(8,128)} %get-tuple-element.31.node) | copy-start | bytes 4534276
  26.5 6.4 %collective-permute-start.10 = (f32[2448,128]{1,0:T(8,128)S(1)}, f32[2448,128]{1,0:T(8,128)S(1)}, u32[]{:S(2)}, u32[]{:S(2)}) collective-permute-start(f32[2448,128]{1,0:T(8,128)S(1)} %get-tuple-element.48), channel_id=1, source_target_pairs={{29,26},{5,2},{13,10},{21,18}} | collective-permute-start | bytes 3760136 | tf_op jit(solution)/shard_map/ppermute | solution.py:439
  27.3 5.5 %collective-permute-start.11 = (f32[2448,128]{1,0:T(8,128)S(1)}, f32[2448,128]{1,0:T(8,128)S(1)}, u32[]{:S(2)}, u32[]{:S(2)}) collective-permute-start(f32[2448,128]{1,0:T(8,128)S(1)} %get-tuple-element.48), channel_id=1, source_target_pairs={{29,28},{5,4},{13,12},{21,20}} | collective-permute-start | bytes 3760136 | tf_op jit(solution)/shard_map/ppermute | solution.py:439
  28.1 2.1 %collective-permute-start.7 = (f32[1152,128]{1,0:T(8,128)S(1)}, f32[1152,128]{1,0:T(8,128)S(1)}, u32[]{:S(2)}, u32[]{:S(2)}) collective-permute-start(f32[1152,128]{1,0:T(8,128)S(1)} %get-tuple-element.47), channel_id=1, source_target_pairs={{29,24},{5,0},{13,8},{21,16}} | collective-permute-start | bytes 1769480 | tf_op jit(solution)/shard_map/ppermute | solution.py:439
  28.8 2.1 %collective-permute-start.6 = (f32[1296,128]{1,0:T(8,128)S(1)}, f32[1296,128]{1,0:T(8,128)S(1)}, u32[]{:S(2)}, u32[]{:S(2)}) collective-permute-start(f32[1296,128]{1,0:T(8,128)S(1)} %get-tuple-element.46), channel_id=1, source_target_pairs={{29,22},{5,30},{13,6},{21,14}} | collective-permute-start | bytes 1990664 | tf_op jit(solution)/shard_map/ppermute | solution.py:439
  29.5 3.3 %collective-permute-start.9 = (f32[1296,128]{1,0:T(8,128)S(1)}, f32[1296,128]{1,0:T(8,128)S(1)}, u32[]{:S(2)}, u32[]{:S(2)}) collective-permute-start(f32[1296,128]{1,0:T(8,128)S(1)} %get-tuple-element.46), channel_id=1, source_target_pairs={{29,24},{5,0},{13,8},{21,16}} | collective-permute-start | bytes 1990664 | tf_op jit(solution)/shard_map/ppermute | solution.py:439
  30.2 2.6 %collective-permute-start.8 = (f32[1152,128]{1,0:T(8,128)S(1)}, f32[1152,128]{1,0:T(8,128)S(1)}, u32[]{:S(2)}, u32[]{:S(2)}) collective-permute-start(f32[1152,128]{1,0:T(8,128)S(1)} %collective-permute-done.7.three_cross), channel_id=1, source_target_pairs={{0,30},{8,6},{16,14},{24,22}} | collective-permute-start | bytes 1769480 | tf_op jit(solution)/shard_map/ppermute | solution.py:439
  30.9 18.0 %collective-permute-start.13 = (f32[2952,128]{1,0:T(8,128)S(1)}, f32[2952,128]{1,0:T(8,128)S(1)}, u32[]{:S(2)}, u32[]{:S(2)}) collective-permute-start(f32[2952,128]{1,0:T(8,128)S(1)} %collective-permute-done.4.came_node.refs_0_.refs_1_), channel_id=1, source_target_pairs={{31,28},{7,4},{15,12},{23,20}} | collective-permute-start | bytes 4534280 | tf_op jit(solution)/shard_map/ppermute | solution.py:439
  32.9 32.5 %collective-permute-start.12 = (f32[2448,128]{1,0:T(8,128)S(1)}, f32[2448,128]{1,0:T(8,128)S(1)}, u32[]{:S(2)}, u32[]{:S(2)}) collective-permute-start(f32[2448,128]{1,0:T(8,128)S(1)} %choose.1.state), channel_id=1, source_target_pairs={{30,31},{6,7},{14,15},{22,23},{0,1},{8,9},{16,17},{24,25},{2,3},{1... | collective-permute-start | bytes 3760136 | tf_op jit(solution)/shard_map/ppermute | solution.py:439

commit v5 on v4

--- a/solution.py
+++ b/solution.py
@@ -113,13 +113,24 @@
 
 
 def symmetric_times(left, right):
-    width = left.shape[0]
+    high, low = left
+    width = high.shape[0]
     most = width // (2 * lanes) * (2 * lanes)
-    wide = long_times(left, right[:most], True)
+
+    def part(rows, columns):
+        both = long_times(jnp.concatenate([high[rows], low[rows]], axis=0), right[0][columns], True)
+        count = both.shape[0] // 2
+        return (both[:count] + both[count:]) + long_times(high[rows], right[1][columns], True)
+
+    wide = part(slice(0, width), slice(0, most))
     if most == width:
         return wide
-    rest = long_times(left[most:], right[most:], True)
+    rest = part(slice(most, width), slice(most, width))
     return jnp.concatenate([wide, jnp.concatenate([wide[most:].T, rest], axis=0)], axis=1)
+
+
+def beside(left, right):
+    return tuple(jnp.concatenate(pair, axis=1) for pair in zip(left, right))
 
 
 def set_state(sh, sl, aa, ba, bb):
@@ -131,9 +142,9 @@
 
 def eliminate(node, sh, sl):
     diag, g_mat, h_mat = node
-    left = long_left(parts_of(jnp.concatenate([g_mat, h_mat], axis=1)))
-    passed = -long_times(left, long_right((sh[...], sl[...])))
-    return passed, diag - symmetric_times(left, long_right(parts_of(passed), True))
+    left = parts_of(jnp.concatenate([g_mat, h_mat], axis=1))
+    passed = -times(left, (sh[...], sl[...]))
+    return passed, diag - symmetric_times(left, parts_of(passed))
 
 
 def place_now(length):
@@ -196,100 +207,105 @@
     return place == 0, place == group, place == 2 * group, place == 3 * group
 
 
-def mid_kernel(length, part, came_root, out, sym_ref):
+def ready_kernel(length, node, diag_ref, g_ref, high_ref, low_ref):
+    width = diag_ref.shape[0]
+    ps, pf = sym_rows(width), full_rows(width)
+    at_zero, at_low, at_mid, at_high = roles_of(length)
+
+    @pl.when(jnp.logical_or(jnp.logical_or(at_zero, at_low), jnp.logical_or(at_mid, at_high)))
+    def _():
+        diag_ref[...] = get_sym(node, 0, width)
+        g_mat = get_full(node, ps, width)
+        g_ref[...] = g_mat
+
+        @pl.when(at_low)
+        def _():
+            high_ref[...], low_ref[...] = parts_of(get_full(node, ps + pf, width))
+
+        @pl.when(jnp.logical_not(at_low))
+        def _():
+            high_ref[...], low_ref[...] = parts_of(g_mat)
+
+
+def mid_kernel(length, node, diag, g_high, g_low, came_root, out, sym_ref):
     width = out.shape[1]
     ps = sym_rows(width)
     _, _, at_mid, _ = roles_of(length)
 
     @pl.when(jnp.logical_not(at_mid))
     def _():
-        sym_ref[...] = part[pl.ds(0, ps), :]
+        sym_ref[...] = node[pl.ds(0, ps), :]
 
     @pl.when(at_mid)
     def _():
-        own_parts = parts_of(get_full(part, ps, width))
-        cross = -times(own_parts, parts_of(get_sym(came_root, 0, width)))
-        own = get_sym(part, 0, width) - times(own_parts, parts_of(cross), True)
+        left = g_high[...], g_low[...]
+        cross = -times(left, parts_of(get_sym(came_root, 0, width)))
+        own = diag[...] - symmetric_times(left, parts_of(cross))
         put_sym(sym_ref, 0, own)
         out[0] = cross
         out[1] = own
 
 
-def low_kernel(length, node, came_part, _after, out):
-    width = out.shape[1]
-    ps = sym_rows(width)
-    _, at_low, _, _ = roles_of(length)
-
-    @pl.when(at_low)
-    def _():
-        own_d, own_g, own_h = get_node(node, width)
-        h_parts = parts_of(own_h)
-        out[0] = times(h_parts, parts_of(get_full(came_part, ps, width))) - own_g
-        passed = times(h_parts, parts_of(get_sym(came_part, 0, width)))
-        out[1] = own_d + times(parts_of(passed), h_parts, True)
-
-
-def hand_over(rooms, sems, diag_ref, cross_ref, diag, cross):
-    rooms[0], rooms[1] = diag, cross
-    fetch(sems, (rooms.at[0], diag_ref.at[0]), (rooms.at[1], cross_ref.at[0]))
-
-
-def first_kernel(length, at_m, root_mid, came_node, diag_ref, cross_ref, sh, sl, aa_ref, bb_ref, rooms, sems):
-    width = rooms.shape[1]
+def first_kernel(length, at_m, root_mid, came_node, kept, sh, sl, aa_ref, bb_ref):
+    width = kept.shape[1]
     _, _, at_mid, _ = roles_of(length)
 
     @pl.when(at_mid)
     def _():
         mid_cross, mid = at_m[0], at_m[1]
+        kept[0], kept[1] = mid, mid_cross
         set_state(sh, sl, get_sym(root_mid, 0, width), mid_cross, mid)
         passed, own = eliminate(get_node(came_node, width), sh, sl)
         put_sym(aa_ref, 0, own)
         put_sym(bb_ref, 0, mid)
         set_state(sh, sl, own, passed[:, width:].T, mid)
-        hand_over(rooms, sems, diag_ref, cross_ref, mid, mid_cross)
 
 
 def second_kernel(
-    length, at_l, came_sym, mid_zero, part, came_part, _diag, _cross, _sh, _sl, _aa, _bb,
-    diag_ref, cross_ref, sh, sl, aa_ref, bb_ref, rooms, sems,
+    length, diag, g_ref, high, low, came_part, came_sym, mid_high, _kept, _sh, _sl, _aa, _bb, kept, sh, sl, aa_ref, bb_ref
 ):
-    width = rooms.shape[1]
+    width = kept.shape[1]
     ps = sym_rows(width)
     at_zero, at_low, _, at_high = roles_of(length)
 
     @pl.when(at_low)
     def _():
+        h_parts = high[...], low[...]
+        mid_both = jnp.concatenate([get_full(came_part, ps, width), get_sym(came_part, 0, width)], axis=1)
+        both = times(h_parts, parts_of(mid_both))
+        e_parts = parts_of(both[:, :width] - g_ref[...])
         root = get_sym(came_sym, 0, width)
-        passed = parts_of(at_l[0])
-        cross = times(passed, parts_of(root))
-        own = at_l[1] + symmetric_times(long_left(parts_of(cross)), long_right(passed, True))
+        cross = times(e_parts, parts_of(root))
+        own = diag[...] + symmetric_times(
+            beside(parts_of(both[:, width:]), parts_of(cross)), beside(h_parts, e_parts)
+        )
         aa_ref[...] = came_sym[...]
         put_sym(bb_ref, 0, own)
         set_state(sh, sl, root, cross, own)
-        hand_over(rooms, sems, diag_ref, cross_ref, own, cross)
-
-    def above(mid_ref, node_ref):
-        own_d, own_g = get_sym(node_ref, 0, width), parts_of(get_full(node_ref, ps, width))
-        mid = get_sym(mid_ref, 0, width)
+        kept[0], kept[1] = own, cross
+
+    def above(mid, own_diag, own_g):
         cross = -times(own_g, parts_of(mid))
-        return mid, cross, own_d - times(own_g, parts_of(cross), True)
+        return cross, own_diag - symmetric_times(own_g, parts_of(cross))
 
     @pl.when(at_high)
     def _():
-        mid, cross, own = above(came_sym, part)
-        aa_ref[...] = came_sym[...]
+        mid = get_sym(mid_high, 0, width)
+        cross, own = above(mid, diag[...], (high[...], low[...]))
+        aa_ref[...] = mid_high[...]
         put_sym(bb_ref, 0, own)
         set_state(sh, sl, mid, cross, own)
-        hand_over(rooms, sems, diag_ref, cross_ref, own, cross)
+        kept[0], kept[1] = own, cross
 
     @pl.when(at_zero)
     def _():
-        _, _, own = above(mid_zero, came_part)
+        high_g = parts_of(get_full(came_part, ps, width))
+        _, own = above(get_sym(came_sym, 0, width), get_sym(came_part, 0, width), high_g)
         zeros = jnp.zeros((width, width), f32)
         put_sym(aa_ref, 0, own)
         bb_ref[...] = jnp.zeros((ps, lanes), f32)
         set_state(sh, sl, own, zeros, zeros)
-        hand_over(rooms, sems, diag_ref, cross_ref, get_sym(part, 0, width), zeros)
+        kept[0], kept[1] = diag[...], zeros
 
 
 def state_kernel(aa_ref, ba_ref, bb_ref, sh, sl, aa_out, bb_out):
@@ -367,7 +383,7 @@
         rest_ref[:, first] = d_own
 
 
-def choose_kernel(length, one, one_cross, three, three_cross, five, seven, _after, out_ref):
+def choose_kernel(length, one, one_cross, three, three_cross, five, _after, out_ref):
     offset = offset_of(length)
     for at, ends, cross in ((1, one, one_cross), (3, three, three_cross)):
 
@@ -377,14 +393,13 @@
             out_ref[pl.ds(0, rows), :] = ends[...]
             out_ref[pl.ds(rows, cross.shape[0]), :] = cross[...]
 
-    for at, ref in ((5, five), (7, seven)):
-
-        @pl.when(offset == at)
-        def _(ref=ref):
-            out_ref[...] = ref[...]
-
-
-def lower_kernel(length, parity, state, fh, fl, rest, _diag, _cross, diag_ref, cross_ref, diag_out, cross_out, sh, sl, sems):
+    @pl.when(offset == 5)
+    def _():
+        out_ref[...] = five[...]
+
+
+def lower_kernel(length, parity, state, seven, fh, fl, rest, kept, *refs):
+    diag_ref, cross_ref, diag_out, cross_out, sh, sl, sems = refs[-7:]
     width = rest.shape[0]
     ps = sym_rows(width)
     offset = offset_of(length)
@@ -393,10 +408,22 @@
     diag_copy = pltpu.make_async_copy(diag_out, diag_ref.at[0], sems.at[0])
     cross_copy = pltpu.make_async_copy(cross_out, cross_ref.at[0], sems.at[1])
 
-    def passed_on():
+    def finish():
+        diag_copy.start()
+        diag_copy.wait()
+        cross_copy.wait()
+
+    def passed_on(state):
         set_state(sh, sl, get_sym(state, 0, width), get_full(state, 2 * ps, width), get_sym(state, ps, width))
-        left = long_left((fh[first, :], fl[first, :]))
-        return long_times(left, long_right((sh[...], sl[...])))
+        return times((fh[first, :], fl[first, :]), (sh[...], sl[...]))
+
+    @pl.when(turn == (1 if parity else 2))
+    def _():
+        passed = passed_on(state)
+        cross_out[...] = passed[:, first]
+        cross_copy.start()
+        diag_out[...] = rest[:, first] + symmetric_times(parts_of(passed), (fh[first, :], fl[first, :]))
+        finish()
 
     if parity == 0:
 
@@ -405,32 +432,25 @@
             cross_out[...] = get_full(state, 2 * ps, width)
             cross_copy.start()
             diag_out[...] = get_sym(state, ps, width)
-            diag_copy.start()
-            diag_copy.wait()
-            cross_copy.wait()
-
-    @pl.when(turn == (1 if parity else 2))
-    def _():
-        passed = passed_on()
-        cross_out[...] = passed[:, first]
-        cross_copy.start()
-        right = long_right((fh[first, :], fl[first, :]), True)
-        diag_out[...] = rest[:, first] + symmetric_times(long_left(parts_of(passed)), right)
-        diag_copy.start()
-        diag_copy.wait()
-        cross_copy.wait()
-
-    if parity == 1:
-
-        @pl.when(turn == 3)
+            finish()
+
+    else:
+
+        for at, ref in ((3, state), (group - 1, seven)):
+
+            @pl.when(offset == at)
+            def _(ref=ref):
+                left = long_left(parts_of(passed_on(ref)))
+                whole = long_times(left, long_right((fh[...], fl[...]), True), True) + rest[...]
+                diag_out[...], cross_out[...] = whole[:, first], whole[:, second]
+                cross_copy.start()
+                finish()
+
+        @pl.when(offset == 0)
         def _():
-            left = long_left(parts_of(passed_on()))
-            whole = long_times(left, long_right((fh[...], fl[...]), True), True) + rest[...]
-            diag_out[...], cross_out[...] = whole[:, first], whole[:, second]
-            diag_copy.start()
+            diag_out[...], cross_out[...] = kept[0], kept[1]
             cross_copy.start()
-            diag_copy.wait()
-            cross_copy.wait()
+            finish()
 
 
 def sent(array, length, *moves):
@@ -484,9 +504,9 @@
     vmem, anywhere = pl.BlockSpec(memory_space=pltpu.VMEM), pl.BlockSpec(memory_space=pl.ANY)
     room = lambda *shape, kind=f32: pltpu.VMEM(shape, kind)
     sems = pltpu.SemaphoreType.DMA((4,))
-    run = lambda kernel, mib, **more: pl.pallas_call(
+    run = lambda kernel, mib, flops=1, **more: pl.pallas_call(
         kernel, compiler_params=pltpu.CompilerParams(vmem_limit_bytes=mib * 2**20),
-        cost_estimate=pl.CostEstimate(flops=1, bytes_accessed=1, transcendentals=0), **more
+        cost_estimate=pl.CostEstimate(flops=flops, bytes_accessed=1, transcendentals=0), **more
     )
     at = lambda turn: (lambda p: p % span == turn)
     inner = lambda offset: (lambda p: p % group == offset)
@@ -501,7 +521,6 @@
     close = ((-1, inner(2)), (-1, inner(6)))
     away = ((1, inner(2)), (group // 2, inner(6)))
     half_state = (jax.ShapeDtypeStruct((2 * width, 2 * width), bf16),) * 2 + (rows_of(ps),) * 2
-    rooms = [room(2, *square), sems]
     if is_open:
         to_mid = lambda p: p == mid - half
         came_far = sent(
@@ -511,31 +530,33 @@
         came_part = sent(part, length, (-group, at(mid)), (group, at(3 * group)))
         root_mid = sent(sym, length, (mid, at(0)))
         two = jax.ShapeDtypeStruct((2,) + square, f32)
+        one = jax.ShapeDtypeStruct(square, f32)
+        ready = run(
+            functools.partial(ready_kernel, length), 16,
+            out_shape=(one, one) + (jax.ShapeDtypeStruct(square, bf16),) * 2,
+            in_specs=[vmem], out_specs=[vmem] * 4, name="ready",
+        )(node)
         at_m, mid_sym = run(
-            functools.partial(mid_kernel, length), 16, out_shape=(two, rows_of(ps)),
-            in_specs=[vmem] * 2, out_specs=[vmem] * 2, name="middle",
-        )(part, root_mid)
-        came_sym = sent(mid_sym, length, (group, at(mid)), (group, at(0)))
-        mid_zero = sent(mid_sym, length, (mid, at(mid)))
-        at_l = run(
-            functools.partial(low_kernel, length), 16, out_shape=two,
-            in_specs=[vmem] * 2 + [anywhere], out_specs=vmem, name="low",
-        )(node, came_part, mid_sym)
+            functools.partial(mid_kernel, length), 16, 4 * 10**9, out_shape=(two, rows_of(ps)),
+            in_specs=[vmem] * 5, out_specs=[vmem] * 2, name="middle",
+        )(node, ready[0], *ready[2:], root_mid)
+        came_sym = sent(mid_sym, length, (mid, at(mid)), (group, at(0)))
+        mid_high = sent(mid_sym, length, (group, at(mid)))
         made = run(
-            functools.partial(first_kernel, length), 16, out_shape=(whole,) * 2 + half_state,
-            in_specs=[vmem] * 3, out_specs=[anywhere] * 2 + [vmem] * 4, scratch_shapes=rooms, name="first",
+            functools.partial(first_kernel, length), 16, out_shape=(two,) + half_state,
+            in_specs=[vmem] * 3, out_specs=[vmem] * 5, name="first",
         )(at_m, root_mid, came_far)
-        diag, cross, *ends = run(
-            functools.partial(second_kernel, length), 16, out_shape=(whole,) * 2 + half_state,
-            in_specs=[vmem] * 5 + [anywhere] * 2 + [vmem] * 4, out_specs=[anywhere] * 2 + [vmem] * 4,
-            scratch_shapes=rooms, input_output_aliases={5 + i: i for i in range(6)}, name="second",
-        )(at_l, came_sym, mid_zero, part, came_part, *made)
+        kept, *ends = run(
+            functools.partial(second_kernel, length), 16, out_shape=(two,) + half_state,
+            in_specs=[vmem] * 12, out_specs=[vmem] * 5,
+            input_output_aliases={7 + i: i for i in range(5)}, name="second",
+        )(*ready, came_part, came_sym, mid_high, *made)
         fours = (came_far, came_near)
     else:
         came_far = sent(node, length, (half, inner(half)), *away)
         came_near = sent(node, length, *close)
         diag, cross, below = upper_levels(inv_diag[0], low_coupling[0], up_coupling[0], length)
-        diag, cross = diag[None], cross[None]
+        kept = jnp.stack([diag, cross])
         ends = run(
             state_kernel, 16, out_shape=half_state, in_specs=[vmem] * 3, out_specs=[vmem] * 4, name="state",
         )(*below)
@@ -549,8 +570,8 @@
     to_five = sent(high_half, length, (-3, inner(0)))
     to_one = sent(low_half, length, (-7, inner(0)))
     to_three = sent(low_half, length, (-5, inner(0)))
+    one_cross = sent(three_cross, length, (-2, inner(3)))
     to_seven = sent(high_half, length, (-1, inner(0)))
-    one_cross = sent(three_cross, length, (-2, inner(3)))
     later, _ = lax.optimization_barrier((came_far, three_cross))
     came_back = sent(later, length, (-3, inner(2)))
 
@@ -566,20 +587,20 @@
     )(node, came_back, *composed)
 
     state = run(
-        functools.partial(choose_kernel, length), 16,
-        out_shape=rows_of(state_rows), in_specs=[vmem] * 6 + [anywhere], out_specs=vmem, name="choose",
-    )(to_one, one_cross, to_three, three_cross, to_five, to_seven, composed[2])
+        functools.partial(choose_kernel, length), 16, 4 * 10**9,
+        out_shape=rows_of(state_rows), in_specs=[vmem] * 5 + [anywhere], out_specs=vmem, name="choose",
+    )(to_one, one_cross, to_three, three_cross, to_five, composed[2])
     state_next = sent(state, length, (1, inner(1)), (1, inner(3)), (1, inner(5)))
 
+    outputs = ()
     for parity, came in ((1, state), (0, state_next)):
-        diag, cross = run(
+        outputs = run(
             functools.partial(lower_kernel, length, parity), 20,
-            out_shape=(whole, whole), in_specs=[vmem] * 4 + [anywhere] * 2, out_specs=[anywhere] * 2,
+            out_shape=(whole, whole), in_specs=[vmem] * 6 + [anywhere] * len(outputs), out_specs=[anywhere] * 2,
             scratch_shapes=[room(*square)] * 2 + [room(2 * width, 2 * width, kind=bf16)] * 2 + [sems],
-            input_output_aliases={4: 0, 5: 1},
-            name="lower",
-        )(came, f_high, f_low, rest, diag, cross)
-    return diag, cross
+            input_output_aliases={6 + i: i for i in range(len(outputs))}, name="lower",
+        )(came, to_seven, f_high, f_low, rest, kept, *outputs)
+    return outputs
 
 
 def solution(mesh):

time: 69.9 us -> 65.6 us (0.938)
  the two profiles are of different devices: /device:TPU:23 before, /device:TPU:3 now
where the time goes in v5:
time: 65.6 us; the launch traced here: 65.2 us
  waiting for transfers between devices  40.3 us (61%)
  starting transfers between devices  13.9 us (21%)
  Pallas kernels  8.66 us (13%)
  local copies, waits for them, and re-layouts  1.38 us (2%)
  between operations  1.08 us (2%)
    ppermute x14, waiting for transfers between devices, sent(): return lax.ppermute(array, axis, pairs)  40.3 us
    ppermute x14, starting transfers between devices, sent(): return lax.ppermute(array, axis, pairs)  13.9 us
    pallas_call x2, Pallas kernels, body(): run(functools.partial(lower_kernel, length, parity), 20, out_shape=(whole...  3.85 us
    pallas_call x1, Pallas kernels, body(): run(own_kernel, 60, out_shape=(rows_of(ps), rows_of(ps + pf), rows_of(nod...  3.83 us
    unnamed x4, local copies, waits for them, and re-layouts  1.38 us
  transfers between devices with their start and end apart: 14, of which 2 were waited for; matrix products, arithmetic and copies ran while one was open for 0% of the time, Pallas kernels for 1%

profile of v5, /device:TPU:3, one launch (start us, length us, event | category | flops | bytes accessed | tf_op | source)
XLA Modules:
  0.0 65.2 jit_solution(849452108895731676)
XLA Ops:
  0.6 3.8 %own.1 = (f32[648,128]{1,0:T(8,128)}, f32[1800,128]{1,0:T(8,128)}, f32[2952,128]{1,0:T(8,128)}) custom-call(f32[1,384,384]{2,1,0:T(8,128)} %inv_ref.1, f32[1,384,384]{2,1,0:T(8,128)} %low_ref.1, f32[1,384,384]{2,1,0:T(8,128)} %up_ref.1), custom_call_target="tpu_custom_call" | custom-call | flops 1 | bytes 1 | tf_op jit(solution)/shard_map/own/pallas_call | solution.py:515
  4.5 3.2 %collective-permute-start.4 = (f32[2952,128]{1,0:T(8,128)}, f32[2952,128]{1,0:T(8,128)S(1)}, u32[]{:S(2)}, u32[]{:S(2)}) collective-permute-start(f32[2952,128]{1,0:T(8,128)} %get-tuple-element.33.node), channel_id=1, source_target_pairs={{1,5},{17,21},{25,29},{5,13},{31,0},{7,8},{15,16},{23,24},{3,7},{1... | collective-permute-start | bytes 4534280 | tf_op jit(solution)/shard_map/ppermute | solution.py:459
  7.7 1.4 %collective-permute-start.5 = (f32[2952,128]{1,0:T(8,128)}, f32[2952,128]{1,0:T(8,128)S(1)}, u32[]{:S(2)}, u32[]{:S(2)}) collective-permute-start(f32[2952,128]{1,0:T(8,128)} %get-tuple-element.33.node), channel_id=1, source_target_pairs={{9,13},{31,30},{7,6},{15,14},{23,22},{3,2},{11,10},{19,18},{27,26}} | collective-permute-start | bytes 4534280 | tf_op jit(solution)/shard_map/ppermute | solution.py:459
  9.1 0.7 %collective-permute-start.1 = (f32[648,128]{1,0:T(8,128)}, f32[648,128]{1,0:T(8,128)S(1)}, u32[]{:S(2)}, u32[]{:S(2)}) collective-permute-start(f32[648,128]{1,0:T(8,128)} %get-tuple-element.39), channel_id=1, source_target_pairs={{29,13}} | collective-permute-start | bytes 995336 | tf_op jit(solution)/shard_map/ppermute | solution.py:459
  9.8 0.7 %collective-permute-start = (f32[1800,128]{1,0:T(8,128)}, f32[1800,128]{1,0:T(8,128)S(1)}, u32[]{:S(2)}, u32[]{:S(2)}) collective-permute-start(f32[1800,128]{1,0:T(8,128)} %get-tuple-element.38), channel_id=1, source_target_pairs={{13,5},{21,29}} | collective-permute-start | bytes 2764808 | tf_op jit(solution)/shard_map/ppermute | solution.py:459
  10.5 1.4 %copy-done = f32[2952,128]{1,0:T(8,128)S(1)} copy-done((f32[2952,128]{1,0:T(8,128)S(1)}, f32[2952,128]{1,0:T(8,128)}, u32[]{:S(2)}) %copy-start) | copy-done | bytes 1511448
  11.9 0.0 collective-permute-done.1.came_root.root_mid
  11.9 0.7 %collective-permute-start.2 = (f32[648,128]{1,0:T(8,128)S(1)}, f32[648,128]{1,0:T(8,128)S(1)}, u32[]{:S(2)}, u32[]{:S(2)}) collective-permute-start(f32[648,128]{1,0:T(8,128)S(1)} %get-tuple-element.40), channel_id=1, source_target_pairs={{13,29},{29,5}} | collective-permute-start | bytes 995336 | tf_op jit(solution)/shard_map/ppermute | solution.py:459
  12.6 0.7 %collective-permute-start.3 = (f32[648,128]{1,0:T(8,128)S(1)}, f32[648,128]{1,0:T(8,128)S(1)}, u32[]{:S(2)}, u32[]{:S(2)}) collective-permute-start(f32[648,128]{1,0:T(8,128)S(1)} %get-tuple-element.40), channel_id=1, source_target_pairs={{13,21}} | collective-permute-start | bytes 995336 | tf_op jit(solution)/shard_map/ppermute | solution.py:459
  13.3 11.3 %collective-permute-done.4.came_node.refs_0_.refs_1_ = f32[2952,128]{1,0:T(8,128)S(1)} collective-permute-done((f32[2952,128]{1,0:T(8,128)}, f32[2952,128]{1,0:T(8,128)S(1)}, u32[]{:S(2)}, u32[]{:S(2)}) %collective-permute-start.4) | collective-permute-done | bytes 1511456 | tf_op jit(solution)/shard_map/ppermute | solution.py:459
  24.6 0.0 collective-permute-done.2.came_sym
  24.6 0.0 collective-permute-done.3.mid_high
  24.6 0.0 collective-permute-done.came_part
  24.7 0.0 collective-permute-done.5.refs_1_.refs_0_
  24.7 0.2 halve.1
  24.9 0.9 %collective-permute-start.10 = (f32[2448,128]{1,0:T(8,128)S(1)}, f32[2448,128]{1,0:T(8,128)S(1)}, u32[]{:S(2)}, u32[]{:S(2)}) collective-permute-start(f32[2448,128]{1,0:T(8,128)S(1)} %get-tuple-element.53), channel_id=1, source_target_pairs={{29,26},{5,2},{13,10},{21,18}} | collective-permute-start | bytes 3760136 | tf_op jit(solution)/shard_map/ppermute | solution.py:459
  25.8 0.7 %collective-permute-start.7 = (f32[1152,128]{1,0:T(8,128)S(1)}, f32[1152,128]{1,0:T(8,128)S(1)}, u32[]{:S(2)}, u32[]{:S(2)}) collective-permute-start(f32[1152,128]{1,0:T(8,128)S(1)} %get-tuple-element.52), channel_id=1, source_target_pairs={{29,24},{5,0},{13,8},{21,16}} | collective-permute-start | bytes 1769480 | tf_op jit(solution)/shard_map/ppermute | solution.py:459
  26.5 0.7 %collective-permute-start.6 = (f32[1296,128]{1,0:T(8,128)S(1)}, f32[1296,128]{1,0:T(8,128)S(1)}, u32[]{:S(2)}, u32[]{:S(2)}) collective-permute-start(f32[1296,128]{1,0:T(8,128)S(1)} %get-tuple-element.51), channel_id=1, source_target_pairs={{29,22},{5,30},{13,6},{21,14}} | collective-permute-start | bytes 1990664 | tf_op jit(solution)/shard_map/ppermute | solution.py:459
  27.2 0.7 %collective-permute-start.9 = (f32[1296,128]{1,0:T(8,128)S(1)}, f32[1296,128]{1,0:T(8,128)S(1)}, u32[]{:S(2)}, u32[]{:S(2)}) collective-permute-start(f32[1296,128]{1,0:T(8,128)S(1)} %get-tuple-element.51), channel_id=1, source_target_pairs={{29,24},{5,0},{13,8},{21,16}} | collective-permute-start | bytes 1990664 | tf_op jit(solution)/shard_map/ppermute | solution.py:459
  27.9 0.0 collective-permute-done.7.three_cross
  27.9 0.7 %collective-permute-start.8 = (f32[1152,128]{1,0:T(8,128)S(1)}, f32[1152,128]{1,0:T(8,128)S(1)}, u32[]{:S(2)}, u32[]{:S(2)}) collective-permute-start(f32[1152,128]{1,0:T(8,128)S(1)} %collective-permute-done.7.three_cross), channel_id=1, source_target_pairs={{0,30},{8,6},{16,14},{24,22}} | collective-permute-start | bytes 1769480 | tf_op jit(solution)/shard_map/ppermute | solution.py:459
  28.6 0.7 %collective-permute-start.12 = (f32[2448,128]{1,0:T(8,128)S(1)}, f32[2448,128]{1,0:T(8,128)S(1)}, u32[]{:S(2)}, u32[]{:S(2)}) collective-permute-start(f32[2448,128]{1,0:T(8,128)S(1)} %get-tuple-element.53), channel_id=1, source_target_pairs={{29,28},{5,4},{13,12},{21,20}} | collective-permute-start | bytes 3760136 | tf_op jit(solution)/shard_map/ppermute | solution.py:459
  29.4 0.5 near.1
  29.8 0.0 collective-permute-done.6.one
  29.9 0.8 %collective-permute-start.13 = (f32[2952,128]{1,0:T(8,128)S(1)}, f32[2952,128]{1,0:T(8,128)S(1)}, u32[]{:S(2)}, u32[]{:S(2)}) collective-permute-start(f32[2952,128]{1,0:T(8,128)S(1)} %collective-permute-done.4.came_node.refs_0_.refs_1_), channel_id=1, source_target_pairs={{31,28},{7,4},{15,12},{23,20}} | collective-permute-start | bytes 4534280 | tf_op jit(solution)/shard_map/ppermute | solution.py:459
  30.6 0.0 collective-permute-done.8.one_cross
  30.7 1.3 %collective-permute-start.11 = (f32[2448,128]{1,0:T(8,128)S(1)}, f32[2448,128]{1,0:T(8,128)S(1)}, u32[]{:S(2)}, u32[]{:S(2)}) collective-permute-start(f32[2448,128]{1,0:T(8,128)S(1)} %choose.1.state), channel_id=1, source_target_pairs={{30,31},{6,7},{14,15},{22,23},{0,1},{8,9},{16,17},{24,25},{2,3},{1... | collective-permute-start | bytes 3760136 | tf_op jit(solution)/shard_map/ppermute | solution.py:459
  32.0 0.2 back.1
  32.2 0.0 collective-permute-done.12.seven
  32.3 0.1 lower.2
  32.3 28.9 %collective-permute-done.11.state = f32[2448,128]{1,0:T(8,128)S(1)} collective-permute-done((f32[2448,128]{1,0:T(8,128)S(1)}, f32[2448,128]{1,0:T(8,128)S(1)}, u32[]{:S(2)}, u32[]{:S(2)}) %collective-permute-start.11) | collective-permute-done | bytes 1253408 | tf_op jit(solution)/shard_map/ppermute | solution.py:459
  61.3 3.8 %lower.3 = (f32[1,384,384]{2,1,0:T(8,128)}, f32[1,384,384]{2,1,0:T(8,128)}) custom-call(f32[2448,128]{1,0:T(8,128)S(1)} %collective-permute-done.11.state, f32[2448,128]{1,0:T(8,128)S(1)} %collective-permute-done.12.seven, bf16[768,768]{1,0:T(8,128)(2,1)S(1)} %get-tuple-element.58.fh, ...), custom_call_target="tpu_custom_call", output_to_operand_aliasing={{0}: (6, {}), {1}: (7, {})} | custom-call | flops 1 | bytes 1 | tf_op jit(solution)/shard_map/lower/pallas_call | solution.py:597
  (11 shorter events, 0.1 us)
Async XLA Ops:
  4.5 20.2 %collective-permute-start.4 = (f32[2952,128]{1,0:T(8,128)}, f32[2952,128]{1,0:T(8,128)S(1)}, u32[]{:S(2)}, u32[]{:S(2)}) collective-permute-start(f32[2952,128]{1,0:T(8,128)} %get-tuple-element.33.node), channel_id=1, source_target_pairs={{1,5},{17,21},{25,29},{5,13},{31,0},{7,8},{15,16},{23,24},{3,7},{1... | collective-permute-start | bytes 4534280 | tf_op jit(solution)/shard_map/ppermute | solution.py:459
  7.7 17.0 %collective-permute-start.5 = (f32[2952,128]{1,0:T(8,128)}, f32[2952,128]{1,0:T(8,128)S(1)}, u32[]{:S(2)}, u32[]{:S(2)}) collective-permute-start(f32[2952,128]{1,0:T(8,128)} %get-tuple-element.33.node), channel_id=1, source_target_pairs={{9,13},{31,30},{7,6},{15,14},{23,22},{3,2},{11,10},{19,18},{27,26}} | collective-permute-start | bytes 4534280 | tf_op jit(solution)/shard_map/ppermute | solution.py:459
  9.1 2.8 %collective-permute-start.1 = (f32[648,128]{1,0:T(8,128)}, f32[648,128]{1,0:T(8,128)S(1)}, u32[]{:S(2)}, u32[]{:S(2)}) collective-permute-start(f32[648,128]{1,0:T(8,128)} %get-tuple-element.39), channel_id=1, source_target_pairs={{29,13}} | collective-permute-start | bytes 995336 | tf_op jit(solution)/shard_map/ppermute | solution.py:459
  9.8 14.8 %collective-permute-start = (f32[1800,128]{1,0:T(8,128)}, f32[1800,128]{1,0:T(8,128)S(1)}, u32[]{:S(2)}, u32[]{:S(2)}) collective-permute-start(f32[1800,128]{1,0:T(8,128)} %get-tuple-element.38), channel_id=1, source_target_pairs={{13,5},{21,29}} | collective-permute-start | bytes 2764808 | tf_op jit(solution)/shard_map/ppermute | solution.py:459
  10.5 1.4 %copy-start = (f32[2952,128]{1,0:T(8,128)S(1)}, f32[2952,128]{1,0:T(8,128)}, u32[]{:S(2)}) copy-start(f32[2952,128]{1,0:T(8,128)} %get-tuple-element.33.node) | copy-start | bytes 4534276
  11.9 12.7 %collective-permute-start.2 = (f32[648,128]{1,0:T(8,128)S(1)}, f32[648,128]{1,0:T(8,128)S(1)}, u32[]{:S(2)}, u32[]{:S(2)}) collective-permute-start(f32[648,128]{1,0:T(8,128)S(1)} %get-tuple-element.40), channel_id=1, source_target_pairs={{13,29},{29,5}} | collective-permute-start | bytes 995336 | tf_op jit(solution)/shard_map/ppermute | solution.py:459
  12.6 12.0 %collective-permute-start.3 = (f32[648,128]{1,0:T(8,128)S(1)}, f32[648,128]{1,0:T(8,128)S(1)}, u32[]{:S(2)}, u32[]{:S(2)}) collective-permute-start(f32[648,128]{1,0:T(8,128)S(1)} %get-tuple-element.40), channel_id=1, source_target_pairs={{13,21}} | collective-permute-start | bytes 995336 | tf_op jit(solution)/shard_map/ppermute | solution.py:459
  24.7 4.7 %copy-start.1 = (f32[2952,128]{1,0:T(8,128)S(1)}, f32[2952,128]{1,0:T(8,128)}, u32[]{:S(2)}) copy-start(f32[2952,128]{1,0:T(8,128)} %get-tuple-element.33.node) | copy-start | bytes 4534276
  24.9 5.7 %collective-permute-start.10 = (f32[2448,128]{1,0:T(8,128)S(1)}, f32[2448,128]{1,0:T(8,128)S(1)}, u32[]{:S(2)}, u32[]{:S(2)}) collective-permute-start(f32[2448,128]{1,0:T(8,128)S(1)} %get-tuple-element.53), channel_id=1, source_target_pairs={{29,26},{5,2},{13,10},{21,18}} | collective-permute-start | bytes 3760136 | tf_op jit(solution)/shard_map/ppermute | solution.py:459
  25.8 2.1 %collective-permute-start.7 = (f32[1152,128]{1,0:T(8,128)S(1)}, f32[1152,128]{1,0:T(8,128)S(1)}, u32[]{:S(2)}, u32[]{:S(2)}) collective-permute-start(f32[1152,128]{1,0:T(8,128)S(1)} %get-tuple-element.52), channel_id=1, source_target_pairs={{29,24},{5,0},{13,8},{21,16}} | collective-permute-start | bytes 1769480 | tf_op jit(solution)/shard_map/ppermute | solution.py:459
  26.5 3.4 %collective-permute-start.6 = (f32[1296,128]{1,0:T(8,128)S(1)}, f32[1296,128]{1,0:T(8,128)S(1)}, u32[]{:S(2)}, u32[]{:S(2)}) collective-permute-start(f32[1296,128]{1,0:T(8,128)S(1)} %get-tuple-element.51), channel_id=1, source_target_pairs={{29,22},{5,30},{13,6},{21,14}} | collective-permute-start | bytes 1990664 | tf_op jit(solution)/shard_map/ppermute | solution.py:459
  27.2 3.4 %collective-permute-start.9 = (f32[1296,128]{1,0:T(8,128)S(1)}, f32[1296,128]{1,0:T(8,128)S(1)}, u32[]{:S(2)}, u32[]{:S(2)}) collective-permute-start(f32[1296,128]{1,0:T(8,128)S(1)} %get-tuple-element.51), channel_id=1, source_target_pairs={{29,24},{5,0},{13,8},{21,16}} | collective-permute-start | bytes 1990664 | tf_op jit(solution)/shard_map/ppermute | solution.py:459
  27.9 2.7 %collective-permute-start.8 = (f32[1152,128]{1,0:T(8,128)S(1)}, f32[1152,128]{1,0:T(8,128)S(1)}, u32[]{:S(2)}, u32[]{:S(2)}) collective-permute-start(f32[1152,128]{1,0:T(8,128)S(1)} %collective-permute-done.7.three_cross), channel_id=1, source_target_pairs={{0,30},{8,6},{16,14},{24,22}} | collective-permute-start | bytes 1769480 | tf_op jit(solution)/shard_map/ppermute | solution.py:459
  28.6 3.6 %collective-permute-start.12 = (f32[2448,128]{1,0:T(8,128)S(1)}, f32[2448,128]{1,0:T(8,128)S(1)}, u32[]{:S(2)}, u32[]{:S(2)}) collective-permute-start(f32[2448,128]{1,0:T(8,128)S(1)} %get-tuple-element.53), channel_id=1, source_target_pairs={{29,28},{5,4},{13,12},{21,20}} | collective-permute-start | bytes 3760136 | tf_op jit(solution)/shard_map/ppermute | solution.py:459
  29.9 2.1 %collective-permute-start.13 = (f32[2952,128]{1,0:T(8,128)S(1)}, f32[2952,128]{1,0:T(8,128)S(1)}, u32[]{:S(2)}, u32[]{:S(2)}) collective-permute-start(f32[2952,128]{1,0:T(8,128)S(1)} %collective-permute-done.4.came_node.refs_0_.refs_1_), channel_id=1, source_target_pairs={{31,28},{7,4},{15,12},{23,20}} | collective-permute-start | bytes 4534280 | tf_op jit(solution)/shard_map/ppermute | solution.py:459
  30.7 30.6 %collective-permute-start.11 = (f32[2448,128]{1,0:T(8,128)S(1)}, f32[2448,128]{1,0:T(8,128)S(1)}, u32[]{:S(2)}, u32[]{:S(2)}) collective-permute-start(f32[2448,128]{1,0:T(8,128)S(1)} %choose.1.state), channel_id=1, source_target_pairs={{30,31},{6,7},{14,15},{22,23},{0,1},{8,9},{16,17},{24,25},{2,3},{1... | collective-permute-start | bytes 3760136 | tf_op jit(solution)/shard_map/ppermute | solution.py:459
